TPU v7x, 32 devices: a whole 2x2x4 slice. The times are simulated.
32 devices in a mesh: cin: 4 (over x, core), cout: 8 (over z, y).
Axes of the slice: x: 2, y: 2, z: 4, core: 2. Of those that a mesh axis runs over, the one named last changes fastest.
Arguments:
- inputs: bfloat16 [4096, 4, 128], P(('cin', 'cout')), may hold values from -6 to 6
- cotangent: bfloat16 [4096, 4, 128], P(('cout', 'cin')), may hold values from -6 to 6
- matrices: bfloat16 [24, 4096, 4096], P(None, 'cout', 'cin'), may hold values from -0.09375 to 0.09375
- filters: float32 [24, 128], replicated, may hold values from -0.109375 to 0.109375
Outputs:
- matrix_grads: bfloat16 [24, 4096, 4096], P(None, 'cout', 'cin')
- input_grads: bfloat16 [4096, 4, 128], P(('cin', 'cout'))
All inputs are finite; a program needn't handle non-finite values.
Results may differ from a plain program's by a relative error of at most 0.002.
Values may be sent and summed in bfloat16 or wider, within the bound.
No kernel may reach another device: no remote copies, remote signals or barrier semaphores. Data moves between devices by JAX's collectives and lax.ppermute only.
A program may use at most 128 MiB of HBM per device.

v0:
```python
import jax
import jax.numpy as jnp
from jax import lax
from jax.sharding import PartitionSpec as P


def toeplitz_upper(filter_row):
    length = filter_row.shape[0]
    padded = jnp.concatenate([filter_row, jnp.zeros((length,), filter_row.dtype)])
    tiled_rows = jnp.tile(padded, length)[: length * (2 * length - 1)]
    return tiled_rows.reshape(length, 2 * length - 1)[:, :length]


def shards(inputs, cotangent, matrices, filters):
    highest = lax.Precision.HIGHEST
    inputs_all = lax.all_gather(inputs, "cout", axis=0, tiled=True)
    grads_all = lax.all_gather(cotangent, "cin", axis=0, tiled=True)
    in_width = inputs_all.shape[0]
    out_width = grads_all.shape[0]
    seq_count = inputs_all.shape[1]
    length = inputs_all.shape[2]
    inputs_flat = inputs_all.reshape(in_width, seq_count * length)
    grads_flat = grads_all.reshape(out_width, seq_count * length)
    inputs_wide = inputs_flat.astype(jnp.float32)
    grads_wide = grads_flat.astype(jnp.float32)

    def per_filter(carried, pair):
        filter_row, matrix_tile = pair
        upper_table = toeplitz_upper(filter_row)
        filtered = jnp.dot(inputs_wide.reshape(-1, length), upper_table, precision=highest).reshape(
            in_width, -1
        )
        matrix_grad = jnp.dot(grads_wide, filtered.T, precision=highest).astype(jnp.bfloat16)
        backward = jnp.dot(matrix_tile.T, grads_flat, preferred_element_type=jnp.float32)
        pulled = jnp.dot(backward.reshape(-1, length), upper_table.T, precision=highest)
        return (carried + pulled.reshape(in_width, -1), matrix_grad)

    start_sum = jnp.zeros((in_width, seq_count * length), jnp.float32)
    partial_sum, matrix_grads = lax.scan(per_filter, start_sum, (filters, matrices))
    summed = lax.psum_scatter(partial_sum, "cout", scatter_dimension=0, tiled=True)
    input_grads = summed.reshape(summed.shape[0], seq_count, length).astype(jnp.bfloat16)
    return (matrix_grads, input_grads)


def solution(mesh):
    placed = (
        P(("cin", "cout"), None, None),
        P(("cout", "cin"), None, None),
        P(None, "cout", "cin"),
        P(),
    )
    return jax.shard_map(
        shards,
        mesh=mesh,
        in_specs=placed,
        out_specs=(P(None, "cout", "cin"), P(("cin", "cout"), None, None)),
        check_vma=False,
    )
```

profile of v0, /device:TPU:0, one launch (start us, length us, event | category | flops | bytes accessed | tf_op | source)
XLA Modules:
  0.0 832.4 jit_solution(12586481924988134386)
XLA Ops:
  8.0 8.8 %all_gather.6 = bf16[512,4,128]{2,1,0:T(4,128)(2,1)S(1)} all-gather(bf16[128,4,128]{2,1,0:T(4,128)(2,1)} %param.7), channel_id=1, replica_groups=mesh['cin'=4,'cout'=8] {'cin'}, dimensions={0}, use_global_device_ids=true | all-gather | bytes 655360 | tf_op jit(solution)/shard_map/all_gather | solution.py:17
  18.2 34.8 %all-gather.2.cloned.1.call-done = bf16[1024,4,128]{2,1,0:T(4,128)(2,1)} async-done(((bf16[128,4,128]{2,1,0:T(4,128)(2,1)}), bf16[1024,4,128]{2,1,0:T(4,128)(2,1)}) %all-gather.2.cloned.1.call-update) | async-done | bytes 1048592 | tf_op jit(solution)/shard_map/all_gather | solution.py:16
  57.5 699.8 %while.14 = (s32[]{:T(128)}, f32[1024,512]{1,0:T(8,128)}, bf16[24,512,1024]{2,1,0:T(8,128)(2,1)}, bf16[24,512,1024]{2,1,0:T(8,128)(2,1)}, bf16[512,512]{1,0:T(8,...) while((s32[]{:T(128)}, f32[1024,512]{1,0:T(8,128)}, ...), condition=%wide.wide.region_1.2_spmd.clone, body=%wide.wide.region_0.1_spmd.clone.sunk | while | flops 5370281984 | bytes 63179496 | solution.py:39
  122.4 5.4 fusion.50
  151.6 5.4 fusion.50
  180.9 5.4 fusion.50
  210.1 5.4 fusion.50
  239.3 5.4 fusion.50
  268.5 5.4 fusion.50
  297.8 5.4 fusion.50
  327.0 5.4 fusion.50
  356.2 5.4 fusion.50
  385.4 5.4 fusion.50
  414.7 5.4 fusion.50
  443.9 5.4 fusion.50
  473.1 5.4 fusion.50
  502.3 5.4 fusion.50
  531.6 5.4 fusion.50
  560.8 5.4 fusion.50
  619.2 5.4 fusion.50
  677.7 5.4 fusion.50
  706.9 5.4 fusion.50
  736.1 5.4 fusion.50
  757.3 66.5 %reduce-scatter.2.cloned.1.call-done = f32[128,512]{1,0:T(8,128)} async-done(((f32[1024,512]{1,0:T(8,128)}), f32[128,512]{1,0:T(8,128)}) %reduce-scatter.2.cloned.1.call-update) | async-done | bytes 262160 | tf_op jit(solution)/shard_map/reduce_scatter | solution.py:40
  (519 shorter events, 599.1 us)
Async XLA Ops:
  7.2 45.8 %all-gather.2.cloned.1.call-start = ((), (), s32[]{:S(2)}) async-start(), calls=%async_computation.1 | async-start | bytes 1179648 | tf_op jit(solution)/shard_map/all_gather | solution.py:16
  7.9 816.0 %reduce-scatter.2.cloned.1.call-start = ((), (), s32[]{:S(2)}) async-start(), calls=%async_computation.2 | async-start | bytes 2359296 | tf_op jit(solution)/shard_map/reduce_scatter | solution.py:40
  122.4 5.9 copy-start.2
  151.6 5.9 copy-start.2
  180.9 5.9 copy-start.2
  210.1 5.9 copy-start.2
  239.3 5.9 copy-start.2
  268.5 5.9 copy-start.2
  297.8 5.9 copy-start.2
  327.0 5.9 copy-start.2
  356.2 5.9 copy-start.2
  385.4 5.9 copy-start.2
  414.7 5.9 copy-start.2
  443.9 5.9 copy-start.2
  473.1 5.9 copy-start.2
  502.3 5.9 copy-start.2
  531.6 5.9 copy-start.2
  560.8 5.9 copy-start.2
  590.0 5.9 copy-start.2
  619.2 5.9 copy-start.2
  648.5 5.9 copy-start.2
  677.7 5.9 copy-start.2
  706.9 5.9 copy-start.2
  736.1 5.9 copy-start.2
  (50 other events, 90.4 us)
Sparse Core Ops, SparseCore 0:
  10.1 42.8 all-gather.1
  757.5 66.3 reduce-scatter.1
where the time goes:
time: 838 us; the launch traced here: 832 us
  matrix products  364 us (43%)
  local copies, waits for them, and re-layouts  259 us (31%)
  waiting for transfers between devices  102 us (12%)
  other arithmetic  82.7 us (10%)
  between operations  14.1 us (2%)
  blocking collectives  8.83 us (1%)
    dot_general x24, matrix products, per_filter(): jnp.dot(grads_wide, filtered.T, precision=highest).astype(jnp.bfloat16)  129 us
    add x24, other arithmetic, per_filter(): return (carried + pulled.reshape(in_width, -1), matrix_grad)  80.4 us
    dot_general x24, matrix products, per_filter(): jnp.dot(matrix_tile.T, grads_flat, preferred_element_type=jnp.float32)  80 us
    dot_general x24, matrix products, per_filter(): jnp.dot(inputs_wide.reshape(-1, length), upper_table, precision=highest)  79 us
    dot_general x24, matrix products, per_filter(): jnp.dot(backward.reshape(-1, length), upper_table.T, precision=highest)  75.8 us
    reduce_scatter x1, waiting for transfers between devices, shards(): lax.psum_scatter(partial_sum, 'cout', scatter_dimension=0, tiled=True)  66.5 us
    dot_general x24, local copies, waits for them, and re-layouts, per_filter(): jnp.dot(inputs_wide.reshape(-1, length), upper_table, precision=highest)  45.8 us
    reshape x24, local copies, waits for them, and re-layouts, per_filter(): return (carried + pulled.reshape(in_width, -1), matrix_grad)  41.6 us
  transfers between devices with their start and end apart: 2, of which 2 were waited for; matrix products, arithmetic and copies ran while one was open for 0% of the time, Pallas kernels for 0%

commit v1 on v0

v1 whole, which is shorter than its diff:
```python
import functools

import jax
import jax.numpy as jnp
from jax import lax
from jax.experimental import pallas as pl
from jax.experimental.pallas import tpu as pltpu
from jax.sharding import PartitionSpec as P

BF16 = jnp.bfloat16
F32 = jnp.float32
VMEM_LIMIT = 56 * 1024 * 1024


def split(wide):
    high = wide.astype(BF16)
    return high, (wide - high.astype(F32)).astype(BF16)


def dot(left, right):
    return jnp.dot(left, right, preferred_element_type=F32)


def call(body, cost, **kwargs):
    flops, moved = cost
    return pl.pallas_call(
        body,
        compiler_params=pltpu.CompilerParams(vmem_limit_bytes=VMEM_LIMIT),
        cost_estimate=pl.CostEstimate(flops=flops, bytes_accessed=moved, transcendentals=0),
        **kwargs,
    )


def table_kernel(filters_ref, rows_ref, columns_ref):
    count, length = filters_ref.shape
    source = lax.broadcasted_iota(jnp.int32, (length, length), 0)
    token = lax.broadcasted_iota(jnp.int32, (length, length), 1)
    for k in range(count):
        spread = jnp.broadcast_to(filters_ref[k : k + 1, :], (length, length))
        shifted = pltpu.roll(spread, 0, 1, stride=1, stride_axis=0)
        upper = jnp.where(token >= source, shifted, 0.0)
        high, low = split(upper)
        rows_ref[k, :, :length] = high
        rows_ref[k, :, length:] = low
        high, low = split(upper.T)
        columns_ref[:length, k * length : (k + 1) * length] = high
        columns_ref[length:, k * length : (k + 1) * length] = low


def make_tables(filters):
    count, length = filters.shape
    return call(
        table_kernel,
        (count * length * length * 4, count * length * length * 8),
        out_shape=(
            jax.ShapeDtypeStruct((count, length, 2 * length), BF16),
            jax.ShapeDtypeStruct((2 * length, count * length), BF16),
        ),
    )(filters)


def back_kernel(half, per_step, cin_count, pair, *refs):
    pieces = refs[:cin_count]
    place_ref, rows_ref, matrix_ref = refs[cin_count : cin_count + 3]
    outs = refs[cin_count + 3 : -4]
    grads, high, low, total = refs[-4:]
    step = pl.program_id(0)
    length = rows_ref.shape[1]
    seqs = grads.shape[0]
    out_width = grads.shape[2]

    @pl.when(step == 0)
    def _():
        total[...] = jnp.zeros_like(total)
        block = pieces[0].shape[0]
        for r, piece in enumerate(pieces):
            if cin_count == 1:
                columns = slice(None)
            else:
                columns = pl.ds(pl.multiple_of((place_ref[0] ^ r) * block, block), block)
            for b in range(seqs):
                first = (half * seqs + b) * length
                turned = piece[:, first : first + length].astype(F32).T.astype(BF16)
                grads[b, :length, columns] = turned
                grads[b, length:, columns] = turned

    table = rows_ref[...].reshape(per_step * length, 2 * length)
    for b in range(seqs):
        filtered = dot(table, grads[b])
        hi, lo = split(filtered)
        for k in range(per_step):
            rows, columns = slice(b * length, (b + 1) * length), slice(k * out_width, (k + 1) * out_width)
            high[rows, columns] = hi[k * length : (k + 1) * length]
            low[rows, columns] = lo[k * length : (k + 1) * length]
    matrix = matrix_ref[...].reshape(per_step * out_width, -1)
    total[...] += dot(high[...], matrix) + dot(low[...], matrix)

    @pl.when(step == pl.num_programs(0) - 1)
    def _():
        if not pair:
            outs[0][...] = total[...].T
            return
        keep, send = outs
        block = keep.shape[1]
        me = place_ref[1]
        for r in range(keep.shape[0]):
            for out, target in ((keep, me ^ (2 * r)), (send, me ^ (2 * r) ^ 1)):
                columns = pl.ds(pl.multiple_of(target * block, block), block)
                out[r] = total[:, columns].T


def back_half(half, place, pieces, rows, matrices, pair_blocks, per_step=4):
    count, out_width, in_width = matrices.shape
    length = rows.shape[1]
    tokens = pieces[0].shape[1]
    seqs = tokens // length // 2
    width = seqs * length
    if pair_blocks:
        block = in_width // (2 * pair_blocks)
        outs = [jax.ShapeDtypeStruct((pair_blocks, block, width), F32)] * 2
    else:
        outs = [jax.ShapeDtypeStruct((in_width, width), F32)]
    whole = lambda array: pl.BlockSpec(array.shape, lambda i: (0,) * len(array.shape))
    return call(
        functools.partial(back_kernel, half, per_step, len(pieces), bool(pair_blocks)),
        (4 * count * out_width * in_width * width, 2 * matrices.size),
        out_shape=outs,
        grid=(count // per_step,),
        in_specs=[whole(piece) for piece in pieces]
        + [
            pl.BlockSpec(memory_space=pltpu.SMEM),
            pl.BlockSpec((per_step, length, 2 * length), lambda i: (i, 0, 0)),
            pl.BlockSpec((per_step, out_width, in_width), lambda i: (i, 0, 0)),
        ],
        out_specs=[whole(out) for out in outs],
        scratch_shapes=[
            pltpu.VMEM((seqs, 2 * length, out_width), BF16),
            pltpu.VMEM((width, per_step * out_width), BF16),
            pltpu.VMEM((width, per_step * out_width), BF16),
            pltpu.VMEM((width, in_width), F32),
        ],
    )(*pieces, place, rows, matrices)


def matrix_kernel(per_step, cin_count, cout_count, has_base, *refs):
    grad_pieces = refs[:cin_count]
    input_pieces = refs[cin_count : cin_count + cout_count]
    refs = refs[cin_count + cout_count :]
    place_ref, columns_ref = refs[:2]
    out_ref, grads, inputs, parts = refs[2 + has_base :]
    step = pl.program_id(0)
    length = columns_ref.shape[0] // 2
    seqs = grads.shape[0]
    tokens = seqs * length

    @pl.when(step == 0)
    def _():
        block = grad_pieces[0].shape[0]
        for r, piece in enumerate(grad_pieces):
            rows = slice(None)
            if cin_count > 1:
                rows = pl.ds(pl.multiple_of((place_ref[0] ^ r) * block, block), block)
            for b in range(seqs):
                part = piece[:, b * length : (b + 1) * length]
                grads[b, rows, :length] = part
                grads[b, rows, length:] = part
        block = input_pieces[0].shape[0]
        for r, piece in enumerate(input_pieces):
            columns = slice(None)
            if cout_count > 1:
                columns = pl.ds(pl.multiple_of((place_ref[1] ^ r) * block, block), block)
            turned = piece[...].astype(F32).T.astype(BF16)
            inputs[:tokens, columns] = turned
            inputs[tokens:, columns] = turned

    table = columns_ref[...]
    for b in range(seqs):
        hi, lo = split(dot(grads[b], table))
        for k in range(per_step):
            parts[k, :, b * length : (b + 1) * length] = hi[:, k * length : (k + 1) * length]
            parts[k, :, tokens + b * length : tokens + (b + 1) * length] = lo[:, k * length : (k + 1) * length]
    for k in range(per_step):
        out_ref[k] = dot(parts[k], inputs[...]).astype(BF16)


def matrix_range(first, filters, place, grad_pieces, input_pieces, columns, base, shape, per_step=2):
    count, out_width, in_width = shape
    length = columns.shape[0] // 2
    tokens = grad_pieces[0].shape[1]
    seqs = tokens // length
    start = first // per_step
    whole = lambda array: pl.BlockSpec(array.shape, lambda i: (0,) * len(array.shape))
    operands = [*grad_pieces, *input_pieces, place, columns]
    in_specs = [whole(piece) for piece in (*grad_pieces, *input_pieces)] + [
        pl.BlockSpec(memory_space=pltpu.SMEM),
        pl.BlockSpec((2 * length, per_step * length), lambda i: (0, start + i)),
    ]
    aliases = {}
    if base is not None:
        aliases = {len(operands): 0}
        operands.append(base)
        in_specs.append(pl.BlockSpec(memory_space=pl.ANY))
    return call(
        functools.partial(matrix_kernel, per_step, len(grad_pieces), len(input_pieces), base is not None),
        (4 * filters * out_width * in_width * tokens, 2 * filters * out_width * in_width),
        out_shape=jax.ShapeDtypeStruct(shape, BF16),
        grid=(filters // per_step,),
        in_specs=in_specs,
        out_specs=pl.BlockSpec((per_step, out_width, in_width), lambda i: (start + i, 0, 0)),
        scratch_shapes=[
            pltpu.VMEM((seqs, out_width, 2 * length), BF16),
            pltpu.VMEM((2 * tokens, in_width), BF16),
            pltpu.VMEM((per_step, out_width, 2 * tokens), BF16),
        ],
        input_output_aliases=aliases,
    )(*operands)


def add_kernel(keep_ref, came_ref, *outs):
    for r, out in enumerate(outs):
        out[...] = keep_ref[r] + came_ref[r]


def add_pair(keep, came):
    return call(
        add_kernel,
        (keep.size, 12 * keep.size),
        out_shape=[jax.ShapeDtypeStruct(keep.shape[1:], F32)] * keep.shape[0],
    )(keep, came)


def exchange(array, axis, count, flip):
    return lax.ppermute(array, axis, [(i, i ^ flip) for i in range(count)])


def gather_pieces(array, axis, count):
    if count & (count - 1) or array.shape[0] % 128:
        return [lax.all_gather(array, axis, axis=0, tiled=True)]
    return [array] + [exchange(array, axis, count, flip) for flip in range(1, count)]


def shards(cin, cout, inputs, cotangent, matrices, filters):
    own, seq_count, length = inputs.shape
    tokens = seq_count * length
    place = jnp.stack([lax.axis_index("cin"), lax.axis_index("cout")]).astype(jnp.int32)
    grad_pieces = gather_pieces(cotangent.reshape(-1, tokens), "cin", cin)
    input_pieces = gather_pieces(inputs.reshape(-1, tokens), "cout", cout)
    rows, columns = make_tables(filters)
    staged = cout % 2 == 0 and len(input_pieces) == cout
    pair_blocks = cout // 2 if staged else 0
    count = matrices.shape[0]
    middle = count // 2

    first = back_half(0, place, grad_pieces, rows, matrices, pair_blocks)
    second = back_half(1, place, grad_pieces, rows, matrices, pair_blocks)
    if staged:
        came_first = exchange(first[1], "cout", cout, 1)
        came_second = exchange(second[1], "cout", cout, 1)
    build = functools.partial(matrix_range, place=place, grad_pieces=grad_pieces, input_pieces=input_pieces, columns=columns, shape=matrices.shape)
    matrix_grads = build(0, middle, base=None)
    matrix_grads = build(middle, count - middle, base=matrix_grads)
    if staged:
        sums = []
        for keep, came in ((first[0], came_first), (second[0], came_second)):
            mine, *others = add_pair(keep, came)
            for r, other in enumerate(others):
                mine = mine + exchange(other, "cout", cout, 2 * (r + 1))
            sums.append(mine)
    else:
        sums = [lax.psum_scatter(part[0], "cout", scatter_dimension=0, tiled=True) for part in (first, second)]
    summed = jnp.concatenate([part.astype(BF16) for part in sums], axis=1)
    return (matrix_grads, summed.reshape(own, seq_count, length))


def solution(mesh):
    placed = (
        P(("cin", "cout"), None, None),
        P(("cout", "cin"), None, None),
        P(None, "cout", "cin"),
        P(),
    )
    return jax.shard_map(
        functools.partial(shards, mesh.shape["cin"], mesh.shape["cout"]),
        mesh=mesh,
        in_specs=placed,
        out_specs=(P(None, "cout", "cin"), P(("cin", "cout"), None, None)),
        check_vma=False,
    )
```

time: 838 us -> 128 us (0.15)
  matrix products: 364 us -> 0 us
  local copies, waits for them, and re-layouts: 259 us -> 4.85 us
  waiting for transfers between devices: 102 us -> 7.27 us
  Pallas kernels: 0 us -> 87.3 us
  other arithmetic: 82.7 us -> 1.64 us
  starting transfers between devices: 0.08 us -> 25.5 us
  between operations: 14.1 us -> 0.81 us
  blocking collectives: 8.83 us -> 0 us
    dot_general x96 -> x0, matrix products: 364 us -> none  [the longest x24 129 us: per_filter(): jnp.dot(grads_wide, filtered.T, precision=highest).astype(jnp.bfloat16)]
    reshape x97 -> x1, local copies, waits for them, and re-layouts: 127 us -> 0.69 us  [shards(): return (matrix_grads, summed.reshape(own, seq_count, length))]
    pallas_call x0 -> x7, Pallas kernels: none -> 87.3 us  [the longest x2 40.5 us: matrix_range(): call(functools.partial(matrix_kernel, per_step, len(grad_pieces), len(inp...]
    add x24 -> x0, other arithmetic: 80.4 us -> none  [per_filter(): return (carried + pulled.reshape(in_width, -1), matrix_grad)]
    reduce_scatter x1 -> x0, waiting for transfers between devices: 66.5 us -> none  [shards(): lax.psum_scatter(partial_sum, 'cout', scatter_dimension=0, tiled=True)]
    dot_general x24 -> x0, local copies, waits for them, and re-layouts: 45.8 us -> none  [per_filter(): jnp.dot(inputs_wide.reshape(-1, length), upper_table, precision=highest)]
    dynamic_update_slice x48 -> x0, local copies, waits for them, and re-layouts: 37.7 us -> none  [shards(): lax.scan(per_filter, start_sum, (filters, matrices))]
    all_gather x1 -> x0, waiting for transfers between devices: 34.8 us -> none  [shards(): inputs_all = lax.all_gather(inputs, 'cout', axis=0, tiled=True)]
  transfers between devices with their start and end apart: 2 -> 18, of which waited for: 2 -> 2; matrix products, arithmetic and copies ran while one was open for 0% -> 1% of each run, Pallas kernels for 0% -> 69%
where the time goes in v1:
time: 128 us; the launch traced here: 127 us
  Pallas kernels  87.3 us (68%)
  starting transfers between devices  25.5 us (20%)
  waiting for transfers between devices  7.27 us (6%)
  local copies, waits for them, and re-layouts  4.85 us (4%)
  other arithmetic  1.64 us (1%)
    pallas_call x2, Pallas kernels, matrix_range(): call(functools.partial(matrix_kernel, per_step, len(grad_pieces), len(inp...  40.5 us
    pallas_call x2, Pallas kernels, back_half(): call(functools.partial(back_kernel, half, per_step, len(pieces), bool(pai...  39.6 us
    ppermute x18, starting transfers between devices, exchange(): return lax.ppermute(array, axis, [(i, i ^ flip) for i in range(count)])  25.5 us
    ppermute x18, waiting for transfers between devices, exchange(): return lax.ppermute(array, axis, [(i, i ^ flip) for i in range(count)])  7.27 us
    unnamed x34, local copies, waits for them, and re-layouts  4.16 us
    pallas_call x2, Pallas kernels, add_pair(): call(add_kernel, (keep.size, 12 * keep.size), out_shape=[jax.ShapeDtypeSt...  4.03 us
    pallas_call x1, Pallas kernels, make_tables(): call(table_kernel, (count * length * length * 4, count * length * length...  3.14 us
  transfers between devices with their start and end apart: 18, of which 2 were waited for; matrix products, arithmetic and copies ran while one was open for 1% of the time, Pallas kernels for 69%

profile of v1, /device:TPU:0, one launch (start us, length us, event | category | flops | bytes accessed | tf_op | source)
XLA Modules:
  0.0 127.3 jit_solution(10792431615935724910)
XLA Ops:
  0.6 0.9 copy.12
  1.6 2.4 %collective-permute-start.2 = (bf16[128,512]{1,0:T(8,128)(2,1)S(1)}, bf16[128,512]{1,0:T(8,128)(2,1)S(1)}, u32[]{:S(2)}, u32[]{:S(2)}) collective-permute-start(bf16[128,512]{1,0:T(8,128)(2,1)S(1)} %bitcast.10), channel_id=1, source_target_pairs={{0,24},{8,16},{16,8},{24,0},{1,25},{9,17},{17,9},{25,1},{2,26},{10... | collective-permute-start | bytes 393224 | tf_op jit(solution)/shard_map/ppermute | solution.py:233
  4.7 0.9 copy.11
  5.6 4.9 %collective-permute-start.9 = (bf16[128,512]{1,0:T(8,128)(2,1)S(1)}, bf16[128,512]{1,0:T(8,128)(2,1)S(1)}, u32[]{:S(2)}, u32[]{:S(2)}) collective-permute-start(bf16[128,512]{1,0:T(8,128)(2,1)S(1)} %bitcast.17), channel_id=1, source_target_pairs={{0,7},{1,6},{2,5},{3,4},{4,3},{5,2},{6,1},{7,0},{8,15},{9,14},{10,... | collective-permute-start | bytes 393224 | tf_op jit(solution)/shard_map/ppermute | solution.py:233
  10.7 3.1 %shard_map.59 = (bf16[24,128,256]{2,1,0:T(8,128)(2,1)}, bf16[256,3072]{1,0:T(8,128)(2,1)}) custom-call(f32[24,128]{1,0:T(8,128)} %filters_ref.1), custom_call_target="tpu_custom_call" | custom-call | flops 1572864 | bytes 3145728 | tf_op jit(solution)/shard_map/pallas_call | solution.py:52
  14.5 0.7 collective-permute-start.7
  15.3 2.0 %collective-permute-start.6 = (bf16[128,512]{1,0:T(8,128)(2,1)S(1)}, bf16[128,512]{1,0:T(8,128)(2,1)S(1)}, u32[]{:S(2)}, u32[]{:S(2)}) collective-permute-start(bf16[128,512]{1,0:T(8,128)(2,1)S(1)} %bitcast.20), channel_id=1, source_target_pairs={{0,4},{1,5},{2,6},{3,7},{4,0},{5,1},{6,2},{7,3},{8,12},{9,13},{10,... | collective-permute-start | bytes 393224 | tf_op jit(solution)/shard_map/ppermute | solution.py:233
  17.3 2.4 %collective-permute-start.5 = (bf16[128,512]{1,0:T(8,128)(2,1)S(1)}, bf16[128,512]{1,0:T(8,128)(2,1)S(1)}, u32[]{:S(2)}, u32[]{:S(2)}) collective-permute-start(bf16[128,512]{1,0:T(8,128)(2,1)S(1)} %bitcast.21), channel_id=1, source_target_pairs={{0,3},{1,2},{2,1},{3,0},{4,7},{5,6},{6,5},{7,4},{8,11},{9,10},{10,... | collective-permute-start | bytes 393224 | tf_op jit(solution)/shard_map/ppermute | solution.py:233
  19.7 19.8 %shard_map.64 = (f32[4,128,256]{2,1,0:T(8,128)}, f32[4,128,256]{2,1,0:T(8,128)}) custom-call(bf16[128,512]{1,0:T(8,128)(2,1)} %bitcast.13, bf16[128,512]{1,0:T(8,128)(2,1)} %copy-done.6, bf16[128,512]{1,0:T(8,128)(2,1)} %copy-done.5, bf16[128,512]{1,0:T(8,128)(2,1)} %copy-done.4, s32[2]{0:T(128)} %pad_add_fusion.refs_12_.refs_4_, ...), custom_call_target="tpu_custom_call" | custom-call | flops 12884901888 | bytes 25165824 | tf_op jit(solution)/shard_map/pallas_call | solution.py:124
  39.5 0.8 collective-permute-start.4
  40.8 19.8 %shard_map.62 = (f32[4,128,256]{2,1,0:T(8,128)}, f32[4,128,256]{2,1,0:T(8,128)}) custom-call(bf16[128,512]{1,0:T(8,128)(2,1)} %bitcast.14, bf16[128,512]{1,0:T(8,128)(2,1)} %copy-done.6, bf16[128,512]{1,0:T(8,128)(2,1)} %copy-done.5, bf16[128,512]{1,0:T(8,128)(2,1)} %copy-done.4, s32[2]{0:T(128)} %pad_add_fusion.refs_12_.refs_4_, ...), custom_call_target="tpu_custom_call" | custom-call | flops 12884901888 | bytes 25165824 | tf_op jit(solution)/shard_map/pallas_call | solution.py:124
  60.6 1.6 %collective-permute-start.14 = (f32[4,128,256]{2,1,0:T(8,128)S(1)}, f32[4,128,256]{2,1,0:T(8,128)S(1)}, u32[]{:S(2)}, u32[]{:S(2)}) collective-permute-start(f32[4,128,256]{2,1,0:T(8,128)S(1)} %copy-done.15), channel_id=1, source_target_pairs={{0,1},{1,0},{2,3},{3,2},{4,5},{5,4},{6,7},{7,6},{8,9},{9,8},{10,11... | collective-permute-start | bytes 1572872 | tf_op jit(solution)/shard_map/ppermute | solution.py:233
  63.5 20.2 %shard_map.60.refs_14_ = bf16[24,512,1024]{2,1,0:T(8,128)(2,1)} custom-call(bf16[128,512]{1,0:T(8,128)(2,1)} %bitcast.15, bf16[128,512]{1,0:T(8,128)(2,1)} %copy-done.6, bf16[128,512]{1,0:T(8,128)(2,1)} %copy-done.5, bf16[128,512]{1,0:T(8,128)(2,1)} %copy-done.4, bf16[128,512]{1,0:T(8,128)(2,1)} %bitcast.24, bf16[128,512]{1,0:T(8,128)(2,1)} %copy-done.13, ...), custom_call_target="tpu_custom_call" | custom-call | flops 12884901888 | bytes 12582912 | tf_op jit(solution)/shard_map/pallas_call | solution.py:203
  83.7 0.8 copy-done.3
  84.5 2.0 %shard_map.65 = (f32[128,256]{1,0:T(8,128)}, f32[128,256]{1,0:T(8,128)}, f32[128,256]{1,0:T(8,128)}, f32[128,256]{1,0:T(8,128)}) custom-call(f32[4,128,256]{2,1,0:T(8,128)} %get-tuple-element.24.keep_ref, f32[4,128,256]{2,1,0:T(8,128)} %copy-done.3), custom_call_target="tpu_custom_call" | custom-call | flops 131072 | bytes 1572864 | tf_op jit(solution)/shard_map/pallas_call | solution.py:225
  86.5 1.4 %collective-permute-start.15 = (f32[128,256]{1,0:T(8,128)}, f32[128,256]{1,0:T(8,128)S(1)}, u32[]{:S(2)}, u32[]{:S(2)}) collective-permute-start(f32[128,256]{1,0:T(8,128)} %get-tuple-element.27), channel_id=1, source_target_pairs={{0,2},{1,3},{2,0},{3,1},{4,6},{5,7},{6,4},{7,5},{8,10},{9,11},{10,... | collective-permute-start | bytes 393224 | tf_op jit(solution)/shard_map/ppermute | solution.py:233
  88.0 2.8 %collective-permute-start.16 = (f32[128,256]{1,0:T(8,128)}, f32[128,256]{1,0:T(8,128)S(1)}, u32[]{:S(2)}, u32[]{:S(2)}) collective-permute-start(f32[128,256]{1,0:T(8,128)} %get-tuple-element.28), channel_id=1, source_target_pairs={{0,4},{1,5},{2,6},{3,7},{4,0},{5,1},{6,2},{7,3},{8,12},{9,13},{10,... | collective-permute-start | bytes 393224 | tf_op jit(solution)/shard_map/ppermute | solution.py:233
  90.9 20.2 %shard_map.61 = bf16[24,512,1024]{2,1,0:T(8,128)(2,1)} custom-call(bf16[128,512]{1,0:T(8,128)(2,1)} %bitcast.16, bf16[128,512]{1,0:T(8,128)(2,1)} %copy-done.6, bf16[128,512]{1,0:T(8,128)(2,1)} %copy-done.5, bf16[128,512]{1,0:T(8,128)(2,1)} %copy-done.4, bf16[128,512]{1,0:T(8,128)(2,1)} %bitcast.25, ...), custom_call_target="tpu_custom_call", output_to_operand_aliasing={{}: (14, {})} | custom-call | flops 12884901888 | bytes 12582912 | tf_op jit(solution)/shard_map/pallas_call | solution.py:203
  111.2 0.8 copy-done.2
  112.0 2.0 %shard_map.63 = (f32[128,256]{1,0:T(8,128)}, f32[128,256]{1,0:T(8,128)}, f32[128,256]{1,0:T(8,128)}, f32[128,256]{1,0:T(8,128)}) custom-call(f32[4,128,256]{2,1,0:T(8,128)} %get-tuple-element.18.keep_ref, f32[4,128,256]{2,1,0:T(8,128)} %copy-done.2), custom_call_target="tpu_custom_call" | custom-call | flops 131072 | bytes 1572864 | tf_op jit(solution)/shard_map/pallas_call | solution.py:225
  114.5 3.6 %collective-permute-start.12 = (f32[128,256]{1,0:T(8,128)}, f32[128,256]{1,0:T(8,128)S(1)}, u32[]{:S(2)}, u32[]{:S(2)}) collective-permute-start(f32[128,256]{1,0:T(8,128)} %get-tuple-element.22), channel_id=1, source_target_pairs={{0,4},{1,5},{2,6},{3,7},{4,0},{5,1},{6,2},{7,3},{8,12},{9,13},{10,... | collective-permute-start | bytes 393224 | tf_op jit(solution)/shard_map/ppermute | solution.py:233
  118.4 1.4 %collective-permute-done.11 = f32[128,256]{1,0:T(8,128)S(1)} collective-permute-done((f32[128,256]{1,0:T(8,128)}, f32[128,256]{1,0:T(8,128)S(1)}, u32[]{:S(2)}, u32[]{:S(2)}) %collective-permute-start.11) | collective-permute-done | bytes 131104 | tf_op jit(solution)/shard_map/ppermute | solution.py:233
  119.9 5.8 %collective-permute-done.12 = f32[128,256]{1,0:T(8,128)S(1)} collective-permute-done((f32[128,256]{1,0:T(8,128)}, f32[128,256]{1,0:T(8,128)S(1)}, u32[]{:S(2)}, u32[]{:S(2)}) %collective-permute-start.12) | collective-permute-done | bytes 131104 | tf_op jit(solution)/shard_map/ppermute | solution.py:233
  125.7 0.9 add_convert_fusion.1
  (58 shorter events, 5.0 us)
Async XLA Ops:
  1.6 18.1 %copy-start = (bf16[16,8,4,128]{3,1,2,0:T(8,128)(2,1)}, bf16[16,8,4,128]{3,1,2,0:T(8,128)(2,1)S(1)}, u32[]{:S(2)}) copy-start(bf16[16,8,4,128]{3,1,2,0:T(8,128)(2,1)S(1)} %copy.12) | copy-start | bytes 393220
  1.6 12.9 %collective-permute-start.2 = (bf16[128,512]{1,0:T(8,128)(2,1)S(1)}, bf16[128,512]{1,0:T(8,128)(2,1)S(1)}, u32[]{:S(2)}, u32[]{:S(2)}) collective-permute-start(bf16[128,512]{1,0:T(8,128)(2,1)S(1)} %bitcast.10), channel_id=1, source_target_pairs={{0,24},{8,16},{16,8},{24,0},{1,25},{9,17},{17,9},{25,1},{2,26},{10... | collective-permute-start | bytes 393224 | tf_op jit(solution)/shard_map/ppermute | solution.py:233
  4.0 11.2 %collective-permute-start.1 = (bf16[128,512]{1,0:T(8,128)(2,1)S(1)}, bf16[128,512]{1,0:T(8,128)(2,1)S(1)}, u32[]{:S(2)}, u32[]{:S(2)}) collective-permute-start(bf16[128,512]{1,0:T(8,128)(2,1)S(1)} %bitcast.11), channel_id=1, source_target_pairs={{0,16},{8,24},{16,0},{24,8},{1,17},{9,25},{17,1},{25,9},{2,18},{10... | collective-permute-start | bytes 393224 | tf_op jit(solution)/shard_map/ppermute | solution.py:233
  4.7 12.7 %collective-permute-start = (bf16[128,512]{1,0:T(8,128)(2,1)S(1)}, bf16[128,512]{1,0:T(8,128)(2,1)S(1)}, u32[]{:S(2)}, u32[]{:S(2)}) collective-permute-start(bf16[128,512]{1,0:T(8,128)(2,1)S(1)} %bitcast.12), channel_id=1, source_target_pairs={{0,8},{8,0},{16,24},{24,16},{1,9},{9,1},{17,25},{25,17},{2,10},{10... | collective-permute-start | bytes 393224 | tf_op jit(solution)/shard_map/ppermute | solution.py:233
  5.6 55.0 %copy-start.1 = (bf16[16,8,4,128]{3,1,2,0:T(8,128)(2,1)}, bf16[16,8,4,128]{3,1,2,0:T(8,128)(2,1)S(1)}, u32[]{:S(2)}) copy-start(bf16[16,8,4,128]{3,1,2,0:T(8,128)(2,1)S(1)} %copy.11) | copy-start | bytes 393220
  5.6 33.9 %collective-permute-start.9 = (bf16[128,512]{1,0:T(8,128)(2,1)S(1)}, bf16[128,512]{1,0:T(8,128)(2,1)S(1)}, u32[]{:S(2)}, u32[]{:S(2)}) collective-permute-start(bf16[128,512]{1,0:T(8,128)(2,1)S(1)} %bitcast.17), channel_id=1, source_target_pairs={{0,7},{1,6},{2,5},{3,4},{4,3},{5,2},{6,1},{7,0},{8,15},{9,14},{10,... | collective-permute-start | bytes 393224 | tf_op jit(solution)/shard_map/ppermute | solution.py:233
  10.5 29.8 %collective-permute-start.8 = (bf16[128,512]{1,0:T(8,128)(2,1)S(1)}, bf16[128,512]{1,0:T(8,128)(2,1)S(1)}, u32[]{:S(2)}, u32[]{:S(2)}) collective-permute-start(bf16[128,512]{1,0:T(8,128)(2,1)S(1)} %bitcast.18), channel_id=1, source_target_pairs={{0,6},{1,7},{2,4},{3,5},{4,2},{5,3},{6,0},{7,1},{8,14},{9,15},{10,... | collective-permute-start | bytes 393224 | tf_op jit(solution)/shard_map/ppermute | solution.py:233
  14.5 46.1 %collective-permute-start.7 = (bf16[128,512]{1,0:T(8,128)(2,1)S(1)}, bf16[128,512]{1,0:T(8,128)(2,1)S(1)}, u32[]{:S(2)}, u32[]{:S(2)}) collective-permute-start(bf16[128,512]{1,0:T(8,128)(2,1)S(1)} %bitcast.19), channel_id=1, source_target_pairs={{0,5},{1,4},{2,7},{3,6},{4,1},{5,0},{6,3},{7,2},{8,13},{9,12},{10,... | collective-permute-start | bytes 393224 | tf_op jit(solution)/shard_map/ppermute | solution.py:233
  15.3 47.0 %collective-permute-start.6 = (bf16[128,512]{1,0:T(8,128)(2,1)S(1)}, bf16[128,512]{1,0:T(8,128)(2,1)S(1)}, u32[]{:S(2)}, u32[]{:S(2)}) collective-permute-start(bf16[128,512]{1,0:T(8,128)(2,1)S(1)} %bitcast.20), channel_id=1, source_target_pairs={{0,4},{1,5},{2,6},{3,7},{4,0},{5,1},{6,2},{7,3},{8,12},{9,13},{10,... | collective-permute-start | bytes 393224 | tf_op jit(solution)/shard_map/ppermute | solution.py:233
  17.3 45.4 %collective-permute-start.5 = (bf16[128,512]{1,0:T(8,128)(2,1)S(1)}, bf16[128,512]{1,0:T(8,128)(2,1)S(1)}, u32[]{:S(2)}, u32[]{:S(2)}) collective-permute-start(bf16[128,512]{1,0:T(8,128)(2,1)S(1)} %bitcast.21), channel_id=1, source_target_pairs={{0,3},{1,2},{2,1},{3,0},{4,7},{5,6},{6,5},{7,4},{8,11},{9,10},{10,... | collective-permute-start | bytes 393224 | tf_op jit(solution)/shard_map/ppermute | solution.py:233
  39.5 21.1 %copy-start.15 = (f32[4,128,256]{2,1,0:T(8,128)S(1)}, f32[4,128,256]{2,1,0:T(8,128)}, u32[]{:S(2)}) copy-start(f32[4,128,256]{2,1,0:T(8,128)} %get-tuple-element.25) | copy-start | bytes 1572868
  39.5 23.2 %copy-start.7 = (bf16[128,512]{1,0:T(8,128)(2,1)}, bf16[128,512]{1,0:T(8,128)(2,1)S(1)}, u32[]{:S(2)}) copy-start(bf16[128,512]{1,0:T(8,128)(2,1)S(1)} %collective-permute-done.9.refs_11_) | copy-start | bytes 393220
  39.5 23.2 %collective-permute-start.4 = (bf16[128,512]{1,0:T(8,128)(2,1)S(1)}, bf16[128,512]{1,0:T(8,128)(2,1)S(1)}, u32[]{:S(2)}, u32[]{:S(2)}) collective-permute-start(bf16[128,512]{1,0:T(8,128)(2,1)S(1)} %bitcast.22), channel_id=1, source_target_pairs={{0,2},{1,3},{2,0},{3,1},{4,6},{5,7},{6,4},{7,5},{8,10},{9,11},{10,... | collective-permute-start | bytes 393224 | tf_op jit(solution)/shard_map/ppermute | solution.py:233
  40.3 22.5 %copy-start.8 = (bf16[128,512]{1,0:T(8,128)(2,1)}, bf16[128,512]{1,0:T(8,128)(2,1)S(1)}, u32[]{:S(2)}) copy-start(bf16[128,512]{1,0:T(8,128)(2,1)S(1)} %collective-permute-done.8.refs_10_) | copy-start | bytes 393220
  40.3 22.4 %collective-permute-start.3 = (bf16[128,512]{1,0:T(8,128)(2,1)S(1)}, bf16[128,512]{1,0:T(8,128)(2,1)S(1)}, u32[]{:S(2)}, u32[]{:S(2)}) collective-permute-start(bf16[128,512]{1,0:T(8,128)(2,1)S(1)} %bitcast.23), channel_id=1, source_target_pairs={{0,1},{1,0},{2,3},{3,2},{4,5},{5,4},{6,7},{7,6},{8,9},{9,8},{10,11... | collective-permute-start | bytes 393224 | tf_op jit(solution)/shard_map/ppermute | solution.py:233
  60.6 23.1 %collective-permute-start.14 = (f32[4,128,256]{2,1,0:T(8,128)S(1)}, f32[4,128,256]{2,1,0:T(8,128)S(1)}, u32[]{:S(2)}, u32[]{:S(2)}) collective-permute-start(f32[4,128,256]{2,1,0:T(8,128)S(1)} %copy-done.15), channel_id=1, source_target_pairs={{0,1},{1,0},{2,3},{3,2},{4,5},{5,4},{6,7},{7,6},{8,9},{9,8},{10,11... | collective-permute-start | bytes 1572872 | tf_op jit(solution)/shard_map/ppermute | solution.py:233
  62.2 48.9 %collective-permute-start.10 = (f32[4,128,256]{2,1,0:T(8,128)}, f32[4,128,256]{2,1,0:T(8,128)S(1)}, u32[]{:S(2)}, u32[]{:S(2)}) collective-permute-start(f32[4,128,256]{2,1,0:T(8,128)} %get-tuple-element.19), channel_id=1, source_target_pairs={{0,1},{1,0},{2,3},{3,2},{4,5},{5,4},{6,7},{7,6},{8,9},{9,8},{10,11... | collective-permute-start | bytes 1572872 | tf_op jit(solution)/shard_map/ppermute | solution.py:233
  86.5 31.6 %collective-permute-start.15 = (f32[128,256]{1,0:T(8,128)}, f32[128,256]{1,0:T(8,128)S(1)}, u32[]{:S(2)}, u32[]{:S(2)}) collective-permute-start(f32[128,256]{1,0:T(8,128)} %get-tuple-element.27), channel_id=1, source_target_pairs={{0,2},{1,3},{2,0},{3,1},{4,6},{5,7},{6,4},{7,5},{8,10},{9,11},{10,... | collective-permute-start | bytes 393224 | tf_op jit(solution)/shard_map/ppermute | solution.py:233
  88.0 30.4 %collective-permute-start.16 = (f32[128,256]{1,0:T(8,128)}, f32[128,256]{1,0:T(8,128)S(1)}, u32[]{:S(2)}, u32[]{:S(2)}) collective-permute-start(f32[128,256]{1,0:T(8,128)} %get-tuple-element.28), channel_id=1, source_target_pairs={{0,4},{1,5},{2,6},{3,7},{4,0},{5,1},{6,2},{7,3},{8,12},{9,13},{10,... | collective-permute-start | bytes 393224 | tf_op jit(solution)/shard_map/ppermute | solution.py:233
  90.7 27.6 %copy-start.14 = (f32[128,256]{1,0:T(8,128)S(1)}, f32[128,256]{1,0:T(8,128)}, u32[]{:S(2)}) copy-start(f32[128,256]{1,0:T(8,128)} %get-tuple-element.26) | copy-start | bytes 393220
  90.7 27.6 %collective-permute-start.17 = (f32[128,256]{1,0:T(8,128)}, f32[128,256]{1,0:T(8,128)S(1)}, u32[]{:S(2)}, u32[]{:S(2)}) collective-permute-start(f32[128,256]{1,0:T(8,128)} %get-tuple-element.29), channel_id=1, source_target_pairs={{0,6},{1,7},{2,4},{3,5},{4,2},{5,3},{6,0},{7,1},{8,14},{9,15},{10,... | collective-permute-start | bytes 393224 | tf_op jit(solution)/shard_map/ppermute | solution.py:233
  114.0 5.9 %collective-permute-start.11 = (f32[128,256]{1,0:T(8,128)}, f32[128,256]{1,0:T(8,128)S(1)}, u32[]{:S(2)}, u32[]{:S(2)}) collective-permute-start(f32[128,256]{1,0:T(8,128)} %get-tuple-element.21), channel_id=1, source_target_pairs={{0,2},{1,3},{2,0},{3,1},{4,6},{5,7},{6,4},{7,5},{8,10},{9,11},{10,... | collective-permute-start | bytes 393224 | tf_op jit(solution)/shard_map/ppermute | solution.py:233
  114.5 11.1 %collective-permute-start.12 = (f32[128,256]{1,0:T(8,128)}, f32[128,256]{1,0:T(8,128)S(1)}, u32[]{:S(2)}, u32[]{:S(2)}) collective-permute-start(f32[128,256]{1,0:T(8,128)} %get-tuple-element.22), channel_id=1, source_target_pairs={{0,4},{1,5},{2,6},{3,7},{4,0},{5,1},{6,2},{7,3},{8,12},{9,13},{10,... | collective-permute-start | bytes 393224 | tf_op jit(solution)/shard_map/ppermute | solution.py:233
  118.2 7.5 %collective-permute-start.13 = (f32[128,256]{1,0:T(8,128)}, f32[128,256]{1,0:T(8,128)S(1)}, u32[]{:S(2)}, u32[]{:S(2)}) collective-permute-start(f32[128,256]{1,0:T(8,128)} %get-tuple-element.23), channel_id=1, source_target_pairs={{0,6},{1,7},{2,4},{3,5},{4,2},{5,3},{6,0},{7,1},{8,14},{9,15},{10,... | collective-permute-start | bytes 393224 | tf_op jit(solution)/shard_map/ppermute | solution.py:233
  (10 other events, 18.5 us)

commit v2 on v1

v2 whole, which is shorter than its diff:
```python
import functools

import jax
import jax.numpy as jnp
from jax import lax
from jax.experimental import pallas as pl
from jax.experimental.pallas import tpu as pltpu
from jax.sharding import PartitionSpec as P

BF16 = jnp.bfloat16
F32 = jnp.float32
VMEM_LIMIT = 56 * 1024 * 1024


def split(wide):
    high = wide.astype(BF16)
    return high, (wide - high.astype(F32)).astype(BF16)


def dot(left, right):
    return jnp.dot(left, right, preferred_element_type=F32)


def call(body, cost, **kwargs):
    flops, moved = cost
    return pl.pallas_call(
        body,
        compiler_params=pltpu.CompilerParams(vmem_limit_bytes=VMEM_LIMIT),
        cost_estimate=pl.CostEstimate(flops=flops, bytes_accessed=moved, transcendentals=0),
        **kwargs,
    )


def table_kernel(filters_ref, rows_ref):
    count, length = filters_ref.shape
    source = lax.broadcasted_iota(jnp.int32, (length, length), 0)
    token = lax.broadcasted_iota(jnp.int32, (length, length), 1)
    for k in range(count):
        spread = jnp.broadcast_to(filters_ref[k : k + 1, :], (length, length))
        shifted = pltpu.roll(spread, 0, 1, stride=1, stride_axis=0)
        high, low = split(jnp.where(token >= source, shifted, 0.0))
        rows_ref[k, :, :length] = high
        rows_ref[k, :, length:] = low


def make_tables(filters):
    count, length = filters.shape
    return call(
        table_kernel,
        (count * length * length * 4, count * length * length * 4),
        out_shape=jax.ShapeDtypeStruct((count, length, 2 * length), BF16),
    )(filters)


def whole(array):
    return pl.BlockSpec(array.shape, lambda i: (0,) * len(array.shape))


def spot(place, flip, block, count):
    if count == 1:
        return slice(None)
    return pl.ds(pl.multiple_of((place ^ flip) * block, block), block)


def back_kernel(half, cin_count, pair, *refs):
    pieces = refs[:cin_count]
    place_ref, rows_ref, matrix_ref = refs[cin_count : cin_count + 3]
    outs = refs[cin_count + 3 : -4]
    grads, early, late, total = refs[-4:]
    step = pl.program_id(0)
    count, length, _ = rows_ref.shape
    out_width = matrix_ref.shape[1]
    seqs = grads.shape[1] // out_width
    width = seqs * length

    def filter_pair(first, parts):
        table = rows_ref[pl.ds(first, 2)].reshape(2 * length, 2 * length)
        high, low = split(dot(table, grads[...]))
        for b in range(seqs):
            for k in range(2):
                source = slice(k * length, (k + 1) * length), slice(b * out_width, (b + 1) * out_width)
                columns = slice(k * out_width, (k + 1) * out_width)
                parts[b * length : (b + 1) * length, columns] = high[source]
                parts[width + b * length : width + (b + 1) * length, columns] = low[source]

    def add_pair_products(first, parts):
        matrix = matrix_ref[first : first + 2].reshape(2 * out_width, -1)
        total[...] += dot(parts[...], matrix)

    @pl.when(step == 0)
    def _():
        total[...] = jnp.zeros_like(total)
        block = pieces[0].shape[0]
        for b in range(seqs):
            first = (half * seqs + b) * length
            for r, piece in enumerate(pieces):
                turned = piece[:, first : first + length].astype(F32).T.astype(BF16)
                if cin_count == 1:
                    columns = slice(b * out_width, (b + 1) * out_width)
                else:
                    columns = pl.ds(pl.multiple_of(b * out_width + (place_ref[0] ^ r) * block, block), block)
                grads[:length, columns] = turned
                grads[length:, columns] = turned
        filter_pair(0, early)

    filter_pair(4 * step + 2, late)
    add_pair_products(0, early)
    filter_pair(lax.rem(4 * step + 4, count), early)
    add_pair_products(2, late)

    @pl.when(step == pl.num_programs(0) - 1)
    def _():
        if not pair:
            outs[0][...] = (total[:width] + total[width:]).T
            return
        keep, send = outs
        block = keep.shape[1]
        for r in range(keep.shape[0]):
            for out, flip in ((keep, 2 * r), (send, 2 * r + 1)):
                columns = spot(place_ref[1], flip, block, 2)
                out[r] = (total[:width, columns] + total[width:, columns]).T


def back_half(half, place, pieces, rows, matrices, pair_blocks):
    count, out_width, in_width = matrices.shape
    length = rows.shape[1]
    tokens = pieces[0].shape[1]
    seqs = tokens // length // 2
    width = seqs * length
    if pair_blocks:
        block = in_width // (2 * pair_blocks)
        outs = [jax.ShapeDtypeStruct((pair_blocks, block, width), F32)] * 2
    else:
        outs = [jax.ShapeDtypeStruct((in_width, width), F32)]
    return call(
        functools.partial(back_kernel, half, len(pieces), bool(pair_blocks)),
        (4 * count * out_width * in_width * width, 2 * matrices.size),
        out_shape=outs,
        grid=(count // 4,),
        in_specs=[whole(piece) for piece in pieces]
        + [
            pl.BlockSpec(memory_space=pltpu.SMEM),
            whole(rows),
            pl.BlockSpec((4, out_width, in_width), lambda i: (i, 0, 0)),
        ],
        out_specs=[whole(out) for out in outs],
        scratch_shapes=[
            pltpu.VMEM((2 * length, seqs * out_width), BF16),
            pltpu.VMEM((2 * width, 2 * out_width), BF16),
            pltpu.VMEM((2 * width, 2 * out_width), BF16),
            pltpu.VMEM((2 * width, in_width), F32),
        ],
    )(*pieces, place, rows, matrices)


def turn_kernel(cout_count, *refs):
    pieces = refs[:-2]
    place_ref, inputs = refs[-2:]
    tokens = inputs.shape[0] // 2
    block = pieces[0].shape[-2]
    for r, piece in enumerate(pieces):
        for half in range(piece.shape[0]):
            columns = spot(place_ref[1], 2 * half + r, block, cout_count)
            turned = piece[half].astype(F32).T.astype(BF16)
            inputs[:tokens, columns] = turned
            inputs[tokens:, columns] = turned


def turn_inputs(pieces, place, cout_count, in_width):
    tokens = pieces[0].shape[-1]
    in_vmem = pl.BlockSpec(memory_space=pltpu.VMEM)
    return call(
        functools.partial(turn_kernel, cout_count),
        (0, 6 * tokens * in_width),
        in_specs=[in_vmem] * len(pieces) + [pl.BlockSpec(memory_space=pltpu.SMEM)],
        out_specs=in_vmem,
        out_shape=jax.ShapeDtypeStruct((2 * tokens, in_width), BF16),
    )(*pieces, place)


def matrix_kernel(start, cin_count, has_base, *refs):
    pieces = refs[:cin_count]
    place_ref, rows_ref, inputs_ref = refs[cin_count : cin_count + 3]
    out_ref, grads, early, late = refs[cin_count + 3 + has_base :]
    step = pl.program_id(0)
    count, length, _ = rows_ref.shape
    tokens = inputs_ref.shape[0] // 2
    seqs = tokens // length
    out_width = out_ref.shape[1]

    def filter_pair(first, parts):
        table = rows_ref[pl.ds(first, 2)].reshape(2 * length, 2 * length)
        filtered = lax.dot_general(grads[...], table, (((1,), (1,)), ((), ())), preferred_element_type=F32)
        high, low = split(filtered)
        for b in range(seqs):
            for k in range(2):
                source = slice(b * out_width, (b + 1) * out_width), slice(k * length, (k + 1) * length)
                rows = slice(k * out_width, (k + 1) * out_width)
                parts[rows, b * length : (b + 1) * length] = high[source]
                parts[rows, tokens + b * length : tokens + (b + 1) * length] = low[source]

    def write_pair(first, parts):
        product = dot(parts[...], inputs_ref[...]).astype(BF16)
        out_ref[first : first + 2] = product.reshape(2, out_width, -1)

    @pl.when(step == 0)
    def _():
        block = pieces[0].shape[0]
        for b in range(seqs):
            for r, piece in enumerate(pieces):
                if cin_count == 1:
                    rows = slice(b * out_width, (b + 1) * out_width)
                else:
                    rows = pl.ds(pl.multiple_of(b * out_width + (place_ref[0] ^ r) * block, block), block)
                part = piece[:, b * length : (b + 1) * length]
                grads[rows, :length] = part
                grads[rows, length:] = part
        filter_pair(start, early)

    filter_pair(start + 4 * step + 2, late)
    write_pair(0, early)
    filter_pair(lax.rem(start + 4 * step + 4, count), early)
    write_pair(2, late)


def matrix_range(start, filters, base, place, pieces, inputs, rows, shape):
    _, out_width, in_width = shape
    length = rows.shape[1]
    tokens = inputs.shape[0] // 2
    seqs = tokens // length
    operands = [*pieces, place, rows, inputs]
    in_specs = [whole(piece) for piece in pieces] + [pl.BlockSpec(memory_space=pltpu.SMEM), whole(rows), whole(inputs)]
    aliases = {}
    if base is not None:
        aliases = {len(operands): 0}
        operands.append(base)
        in_specs.append(pl.BlockSpec(memory_space=pl.ANY))
    return call(
        functools.partial(matrix_kernel, start, len(pieces), base is not None),
        (4 * filters * out_width * in_width * tokens, 2 * filters * out_width * in_width),
        out_shape=jax.ShapeDtypeStruct(shape, BF16),
        grid=(filters // 4,),
        in_specs=in_specs,
        out_specs=pl.BlockSpec((4, out_width, in_width), lambda i: (start // 4 + i, 0, 0)),
        scratch_shapes=[
            pltpu.VMEM((seqs * out_width, 2 * length), BF16),
            pltpu.VMEM((2 * out_width, 2 * tokens), BF16),
            pltpu.VMEM((2 * out_width, 2 * tokens), BF16),
        ],
        input_output_aliases=aliases,
    )(*operands)


def add_kernel(keep_ref, came_ref, *outs):
    for r, out in enumerate(outs):
        out[...] = keep_ref[r] + came_ref[r]


def add_pair(keep, came):
    return call(
        add_kernel,
        (keep.size, 12 * keep.size),
        out_shape=[jax.ShapeDtypeStruct(keep.shape[1:], F32)] * keep.shape[0],
    )(keep, came)


def exchange(array, axis, count, flip):
    return lax.ppermute(array, axis, [(i, i ^ flip) for i in range(count)])


def after(array, *others):
    return lax.optimization_barrier((array, *others))[0]


def shards(cin, cout, inputs, cotangent, matrices, filters):
    own, seq_count, length = inputs.shape
    tokens = seq_count * length
    count, out_width, in_width = matrices.shape
    place = jnp.stack([lax.axis_index("cin"), lax.axis_index("cout")]).astype(jnp.int32)
    flat_grads = cotangent.reshape(-1, tokens)
    flat_inputs = inputs.reshape(-1, tokens)
    if cin & (cin - 1) or flat_grads.shape[0] % 128:
        pieces = [lax.all_gather(flat_grads, "cin", axis=0, tiled=True)]
    else:
        pieces = [flat_grads] + [exchange(flat_grads, "cin", cin, flip) for flip in range(1, cin)]
    rows = make_tables(filters)
    staged = cout & (cout - 1) == 0 and cout > 1 and own % 128 == 0
    pair_blocks = cout // 2 if staged else 0
    if staged:
        columns = [flat_inputs] + [exchange(flat_inputs, "cout", cout, 2 * r) for r in range(1, pair_blocks)]

    first = back_half(0, place, pieces, rows, matrices, pair_blocks)
    if staged:
        came_first = exchange(first[1], "cout", cout, 1)
        mine = jnp.stack(after(columns, first[0]))
        input_pieces = [mine, exchange(mine, "cout", cout, 1)]
    else:
        input_pieces = [lax.all_gather(flat_inputs, "cout", axis=0, tiled=True)[None]]
    second = back_half(1, after(place, first[0]), pieces, rows, matrices, pair_blocks)
    if staged:
        came_second = exchange(second[1], "cout", cout, 1)
    turned = turn_inputs(input_pieces, after(place, second[0]), cout if staged else 1, in_width)

    build = functools.partial(matrix_range, pieces=pieces, inputs=turned, rows=rows, shape=matrices.shape)
    sixth = count // 6
    grads = build(0, sixth, None, place)
    if staged:
        sums = []
        halves = ((sixth, 3 * sixth, first[0], came_first), (3 * sixth, count, second[0], came_second))
        for start, stop, keep, came in halves:
            keep = after(keep, grads)
            mine, *others = add_pair(keep, came)
            place = after(place, mine)
            sums.append([mine] + [exchange(other, "cout", cout, 2 * (r + 1)) for r, other in enumerate(others)])
            grads = build(start, stop - start, grads, place)
        sums = [functools.reduce(jnp.add, terms) for terms in sums]
    else:
        grads = build(sixth, count - sixth, grads, place)
        sums = [lax.psum_scatter(part[0], "cout", scatter_dimension=0, tiled=True) for part in (first, second)]
    summed = jnp.concatenate(sums, axis=1).astype(BF16)
    return (grads, summed.reshape(own, seq_count, length))


def solution(mesh):
    placed = (
        P(("cin", "cout"), None, None),
        P(("cout", "cin"), None, None),
        P(None, "cout", "cin"),
        P(),
    )
    return jax.shard_map(
        functools.partial(shards, mesh.shape["cin"], mesh.shape["cout"]),
        mesh=mesh,
        in_specs=placed,
        out_specs=(P(None, "cout", "cin"), P(("cin", "cout"), None, None)),
        check_vma=False,
    )
```

time: 128 us -> 130 us (1.016)
  Pallas kernels: 87.3 us -> 96.3 us
  starting transfers between devices: 25.5 us -> 20 us
  waiting for transfers between devices: 7.27 us -> 5.8 us
    pallas_call x4 -> x6, Pallas kernels: 80.1 us -> 89.9 us  [the longest x3 45.4 us: matrix_range(): call(functools.partial(matrix_kernel, start, len(pieces), base is not Non...]
    ppermute x18 -> x15, starting transfers between devices: 25.5 us -> 20 us  [exchange(): return lax.ppermute(array, axis, [(i, i ^ flip) for i in range(count)])]
    ppermute x18 -> x15, waiting for transfers between devices: 7.27 us -> 5.8 us  [exchange(): return lax.ppermute(array, axis, [(i, i ^ flip) for i in range(count)])]
    unnamed x34 -> x24, local copies, waits for them, and re-layouts: 4.16 us -> 5.58 us
  transfers between devices with their start and end apart: 18 -> 15, of which waited for: 2 -> 1; matrix products, arithmetic and copies ran while one was open for 1% -> 1% of each run, Pallas kernels for 69% -> 74%
where the time goes in v2:
time: 130 us
  Pallas kernels  96.3 us (74%)
  starting transfers between devices  20 us (15%)
  waiting for transfers between devices  5.8 us (4%)
  local copies, waits for them, and re-layouts  5.63 us (4%)
  other arithmetic  1.55 us (1%)
    pallas_call x3, Pallas kernels, matrix_range(): call(functools.partial(matrix_kernel, start, len(pieces), base is not Non...  45.4 us
    pallas_call x2, Pallas kernels, back_half(): call(functools.partial(back_kernel, half, len(pieces), bool(pair_blocks))...  41.3 us
    ppermute x15, starting transfers between devices, exchange(): return lax.ppermute(array, axis, [(i, i ^ flip) for i in range(count)])  20 us
    ppermute x15, waiting for transfers between devices, exchange(): return lax.ppermute(array, axis, [(i, i ^ flip) for i in range(count)])  5.8 us
    unnamed x24, local copies, waits for them, and re-layouts  5.58 us
    pallas_call x2, Pallas kernels, add_pair(): call(add_kernel, (keep.size, 12 * keep.size), out_shape=[jax.ShapeDtypeSt...  4.04 us
    pallas_call x1, Pallas kernels, turn_inputs(): call(functools.partial(turn_kernel, cout_count), (0, 6 * tokens * in_widt...  3.15 us
  transfers between devices with their start and end apart: 15, of which 1 were waited for; matrix products, arithmetic and copies ran while one was open for 1% of the time, Pallas kernels for 74%

profile of v2, /device:TPU:0, one launch (start us, length us, event | category | flops | bytes accessed | tf_op | source)
XLA Modules:
  0.0 130.1 jit_solution(13477897467058948530)
XLA Ops:
  0.6 0.9 copy.13
  2.1 2.6 %collective-permute-start.1 = (bf16[128,512]{1,0:T(8,128)(2,1)S(1)}, bf16[128,512]{1,0:T(8,128)(2,1)S(1)}, u32[]{:S(2)}, u32[]{:S(2)}) collective-permute-start(bf16[128,512]{1,0:T(8,128)(2,1)S(1)} %bitcast.15), channel_id=1, source_target_pairs={{0,16},{8,24},{16,0},{24,8},{1,17},{9,25},{17,1},{25,9},{2,18},{10... | collective-permute-start | bytes 393224 | tf_op jit(solution)/shard_map/ppermute | solution.py:268
  4.7 0.9 copy.12
  5.6 1.9 %collective-permute-start.3 = (bf16[128,512]{1,0:T(8,128)(2,1)S(1)}, bf16[128,512]{1,0:T(8,128)(2,1)S(1)}, u32[]{:S(2)}, u32[]{:S(2)}) collective-permute-start(bf16[128,512]{1,0:T(8,128)(2,1)S(1)} %bitcast.22), channel_id=1, source_target_pairs={{0,2},{1,3},{2,0},{3,1},{4,6},{5,7},{6,4},{7,5},{8,10},{9,11},{10,... | collective-permute-start | bytes 393224 | tf_op jit(solution)/shard_map/ppermute | solution.py:268
  7.5 2.6 %collective-permute-start.4 = (bf16[128,512]{1,0:T(8,128)(2,1)S(1)}, bf16[128,512]{1,0:T(8,128)(2,1)S(1)}, u32[]{:S(2)}, u32[]{:S(2)}) collective-permute-start(bf16[128,512]{1,0:T(8,128)(2,1)S(1)} %bitcast.23), channel_id=1, source_target_pairs={{0,4},{1,5},{2,6},{3,7},{4,0},{5,1},{6,2},{7,3},{8,12},{9,13},{10,... | collective-permute-start | bytes 393224 | tf_op jit(solution)/shard_map/ppermute | solution.py:268
  10.1 2.3 %shard_map.59.refs_5_ = bf16[24,128,256]{2,1,0:T(8,128)(2,1)} custom-call(f32[24,128]{1,0:T(8,128)} %filters_ref.1), custom_call_target="tpu_custom_call" | custom-call | flops 1572864 | bytes 1572864 | tf_op jit(solution)/shard_map/pallas_call | solution.py:48
  14.4 20.7 %shard_map.60 = (f32[4,128,256]{2,1,0:T(8,128)}, f32[4,128,256]{2,1,0:T(8,128)}) custom-call(bf16[128,512]{1,0:T(8,128)(2,1)} %bitcast.17, bf16[128,512]{1,0:T(8,128)(2,1)} %copy-done.2, bf16[128,512]{1,0:T(8,128)(2,1)} %copy-done.3, bf16[128,512]{1,0:T(8,128)(2,1)} %copy-done.4, s32[2]{0:T(128)} %pad_add_fusion.refs_4_.refs_2_, ...), custom_call_target="tpu_custom_call" | custom-call | flops 12884901888 | bytes 25165824 | tf_op jit(solution)/shard_map/pallas_call | solution.py:135
  35.2 1.8 %collective-permute-start.6 = (bf16[4,128,512]{2,1,0:T(8,128)(2,1)S(1)}, bf16[4,128,512]{2,1,0:T(8,128)(2,1)S(1)}, u32[]{:S(2)}, u32[]{:S(2)}) collective-permute-start(bf16[4,128,512]{2,1,0:T(8,128)(2,1)S(1)} %pad_maximum_fusion.refs_0_), channel_id=1, source_target_pairs={{0,1},{1,0},{2,3},{3,2},{4,5},{5,4},{6,7},{7,6},{8,9},{9,8},{10,11... | collective-permute-start | bytes 1572872 | tf_op jit(solution)/shard_map/ppermute | solution.py:268
  37.3 20.6 %shard_map.61 = (f32[4,128,256]{2,1,0:T(8,128)}, f32[4,128,256]{2,1,0:T(8,128)}) custom-call(bf16[128,512]{1,0:T(8,128)(2,1)} %bitcast.18, bf16[128,512]{1,0:T(8,128)(2,1)} %copy-done.2, bf16[128,512]{1,0:T(8,128)(2,1)} %copy-done.3, bf16[128,512]{1,0:T(8,128)(2,1)} %copy-done.4, s32[2]{0:T(128)} %pad_add_fusion.refs_4_.refs_2_, ...), custom_call_target="tpu_custom_call" | custom-call | flops 12884901888 | bytes 25165824 | tf_op jit(solution)/shard_map/pallas_call | solution.py:135
  57.9 1.7 %collective-permute-start.8 = (f32[4,128,256]{2,1,0:T(8,128)}, f32[4,128,256]{2,1,0:T(8,128)S(1)}, u32[]{:S(2)}, u32[]{:S(2)}) collective-permute-start(f32[4,128,256]{2,1,0:T(8,128)} %get-tuple-element.37), channel_id=1, source_target_pairs={{0,1},{1,0},{2,3},{3,2},{4,5},{5,4},{6,7},{7,6},{8,9},{9,8},{10,11... | collective-permute-start | bytes 1572872 | tf_op jit(solution)/shard_map/ppermute | solution.py:268
  59.7 0.8 copy-done.7
  60.5 3.2 %shard_map.62.refs_6_ = bf16[1024,1024]{1,0:T(8,128)(2,1)} custom-call(bf16[4,128,512]{2,1,0:T(8,128)(2,1)} %copy-done.1, bf16[4,128,512]{2,1,0:T(8,128)(2,1)} %copy-done.7, s32[2]{0:T(128)} %pad_add_fusion.refs_4_.refs_2_), custom_call_target="tpu_custom_call" | custom-call | bytes 3145728 | tf_op jit(solution)/shard_map/pallas_call | solution.py:172
  63.6 9.9 %shard_map.63.refs_7_ = bf16[24,512,1024]{2,1,0:T(8,128)(2,1)} custom-call(bf16[128,512]{1,0:T(8,128)(2,1)} %bitcast.19, bf16[128,512]{1,0:T(8,128)(2,1)} %copy-done.2, bf16[128,512]{1,0:T(8,128)(2,1)} %copy-done.3, bf16[128,512]{1,0:T(8,128)(2,1)} %copy-done.4, s32[2]{0:T(128)} %pad_add_fusion.refs_4_.refs_2_, bf16[24,128,256]{2,1,0:T(8,128)(2,1)} %shard_map.59.refs_5_, ...), custom_call_target="tpu_custom_call" | custom-call | flops 4294967296 | bytes 4194304 | tf_op jit(solution)/shard_map/pallas_call | solution.py:238
  74.3 2.0 %shard_map.64 = (f32[128,256]{1,0:T(8,128)}, f32[128,256]{1,0:T(8,128)}, f32[128,256]{1,0:T(8,128)}, f32[128,256]{1,0:T(8,128)}) custom-call(f32[4,128,256]{2,1,0:T(8,128)} %get-tuple-element.32.keep_ref, f32[4,128,256]{2,1,0:T(8,128)} %copy-done.6), custom_call_target="tpu_custom_call" | custom-call | flops 131072 | bytes 1572864 | tf_op jit(solution)/shard_map/pallas_call | solution.py:260
  76.4 1.7 %collective-permute-start.10 = (f32[128,256]{1,0:T(8,128)}, f32[128,256]{1,0:T(8,128)S(1)}, u32[]{:S(2)}, u32[]{:S(2)}) collective-permute-start(f32[128,256]{1,0:T(8,128)} %get-tuple-element.41), channel_id=1, source_target_pairs={{0,4},{1,5},{2,6},{3,7},{4,0},{5,1},{6,2},{7,3},{8,12},{9,13},{10,... | collective-permute-start | bytes 393224 | tf_op jit(solution)/shard_map/ppermute | solution.py:268
  78.0 1.9 %collective-permute-start.11 = (f32[128,256]{1,0:T(8,128)}, f32[128,256]{1,0:T(8,128)S(1)}, u32[]{:S(2)}, u32[]{:S(2)}) collective-permute-start(f32[128,256]{1,0:T(8,128)} %get-tuple-element.42), channel_id=1, source_target_pairs={{0,6},{1,7},{2,4},{3,5},{4,2},{5,3},{6,0},{7,1},{8,14},{9,15},{10,... | collective-permute-start | bytes 393224 | tf_op jit(solution)/shard_map/ppermute | solution.py:268
  80.5 15.2 %shard_map.65.refs_7_ = bf16[24,512,1024]{2,1,0:T(8,128)(2,1)} custom-call(bf16[128,512]{1,0:T(8,128)(2,1)} %bitcast.20, bf16[128,512]{1,0:T(8,128)(2,1)} %copy-done.2, bf16[128,512]{1,0:T(8,128)(2,1)} %copy-done.3, bf16[128,512]{1,0:T(8,128)(2,1)} %copy-done.4, s32[2]{0:T(128)} %pad_add_fusion.refs_4_.refs_2_, ...), custom_call_target="tpu_custom_call", output_to_operand_aliasing={{}: (7, {})} | custom-call | flops 8589934592 | bytes 8388608 | tf_op jit(solution)/shard_map/pallas_call | solution.py:238
  95.7 0.8 copy-done.5
  96.5 2.0 %shard_map.66 = (f32[128,256]{1,0:T(8,128)}, f32[128,256]{1,0:T(8,128)}, f32[128,256]{1,0:T(8,128)}, f32[128,256]{1,0:T(8,128)}) custom-call(f32[4,128,256]{2,1,0:T(8,128)} %get-tuple-element.36.keep_ref, f32[4,128,256]{2,1,0:T(8,128)} %copy-done.5), custom_call_target="tpu_custom_call" | custom-call | flops 131072 | bytes 1572864 | tf_op jit(solution)/shard_map/pallas_call | solution.py:260
  98.5 1.5 %collective-permute-start.12 = (f32[128,256]{1,0:T(8,128)}, f32[128,256]{1,0:T(8,128)S(1)}, u32[]{:S(2)}, u32[]{:S(2)}) collective-permute-start(f32[128,256]{1,0:T(8,128)} %get-tuple-element.43), channel_id=1, source_target_pairs={{0,2},{1,3},{2,0},{3,1},{4,6},{5,7},{6,4},{7,5},{8,10},{9,11},{10,... | collective-permute-start | bytes 393224 | tf_op jit(solution)/shard_map/ppermute | solution.py:268
  100.0 2.0 %collective-permute-start.13 = (f32[128,256]{1,0:T(8,128)}, f32[128,256]{1,0:T(8,128)S(1)}, u32[]{:S(2)}, u32[]{:S(2)}) collective-permute-start(f32[128,256]{1,0:T(8,128)} %get-tuple-element.44), channel_id=1, source_target_pairs={{0,4},{1,5},{2,6},{3,7},{4,0},{5,1},{6,2},{7,3},{8,12},{9,13},{10,... | collective-permute-start | bytes 393224 | tf_op jit(solution)/shard_map/ppermute | solution.py:268
  102.0 20.3 %shard_map.67 = bf16[24,512,1024]{2,1,0:T(8,128)(2,1)} custom-call(bf16[128,512]{1,0:T(8,128)(2,1)} %bitcast.21, bf16[128,512]{1,0:T(8,128)(2,1)} %copy-done.2, bf16[128,512]{1,0:T(8,128)(2,1)} %copy-done.3, bf16[128,512]{1,0:T(8,128)(2,1)} %copy-done.4, s32[2]{0:T(128)} %pad_add_fusion.refs_4_.refs_2_, ...), custom_call_target="tpu_custom_call", output_to_operand_aliasing={{}: (7, {})} | custom-call | flops 12884901888 | bytes 12582912 | tf_op jit(solution)/shard_map/pallas_call | solution.py:238
  122.4 1.0 collective-permute-start.14
  123.4 5.8 %collective-permute-done.14 = f32[128,256]{1,0:T(8,128)S(1)} collective-permute-done((f32[128,256]{1,0:T(8,128)S(1)}, f32[128,256]{1,0:T(8,128)S(1)}, u32[]{:S(2)}, u32[]{:S(2)}) %collective-permute-start.14) | collective-permute-done | bytes 131104 | tf_op jit(solution)/shard_map/ppermute | solution.py:268
  (46 shorter events, 5.2 us)
Async XLA Ops:
  1.6 11.5 %copy-start = (bf16[16,8,4,128]{3,1,2,0:T(8,128)(2,1)}, bf16[16,8,4,128]{3,1,2,0:T(8,128)(2,1)S(1)}, u32[]{:S(2)}) copy-start(bf16[16,8,4,128]{3,1,2,0:T(8,128)(2,1)S(1)} %copy.13) | copy-start | bytes 393220
  1.6 11.5 %collective-permute-start = (bf16[128,512]{1,0:T(8,128)(2,1)S(1)}, bf16[128,512]{1,0:T(8,128)(2,1)S(1)}, u32[]{:S(2)}, u32[]{:S(2)}) collective-permute-start(bf16[128,512]{1,0:T(8,128)(2,1)S(1)} %bitcast.14), channel_id=1, source_target_pairs={{0,8},{8,0},{16,24},{24,16},{1,9},{9,1},{17,25},{25,17},{2,10},{10... | collective-permute-start | bytes 393224 | tf_op jit(solution)/shard_map/ppermute | solution.py:268
  2.1 11.0 %collective-permute-start.1 = (bf16[128,512]{1,0:T(8,128)(2,1)S(1)}, bf16[128,512]{1,0:T(8,128)(2,1)S(1)}, u32[]{:S(2)}, u32[]{:S(2)}) collective-permute-start(bf16[128,512]{1,0:T(8,128)(2,1)S(1)} %bitcast.15), channel_id=1, source_target_pairs={{0,16},{8,24},{16,0},{24,8},{1,17},{9,25},{17,1},{25,9},{2,18},{10... | collective-permute-start | bytes 393224 | tf_op jit(solution)/shard_map/ppermute | solution.py:268
  4.7 8.4 %collective-permute-start.2 = (bf16[128,512]{1,0:T(8,128)(2,1)S(1)}, bf16[128,512]{1,0:T(8,128)(2,1)S(1)}, u32[]{:S(2)}, u32[]{:S(2)}) collective-permute-start(bf16[128,512]{1,0:T(8,128)(2,1)S(1)} %bitcast.16), channel_id=1, source_target_pairs={{0,24},{8,16},{16,8},{24,0},{1,25},{9,17},{17,9},{25,1},{2,26},{10... | collective-permute-start | bytes 393224 | tf_op jit(solution)/shard_map/ppermute | solution.py:268
  5.6 29.4 %collective-permute-start.3 = (bf16[128,512]{1,0:T(8,128)(2,1)S(1)}, bf16[128,512]{1,0:T(8,128)(2,1)S(1)}, u32[]{:S(2)}, u32[]{:S(2)}) collective-permute-start(bf16[128,512]{1,0:T(8,128)(2,1)S(1)} %bitcast.22), channel_id=1, source_target_pairs={{0,2},{1,3},{2,0},{3,1},{4,6},{5,7},{6,4},{7,5},{8,10},{9,11},{10,... | collective-permute-start | bytes 393224 | tf_op jit(solution)/shard_map/ppermute | solution.py:268
  7.5 27.6 %collective-permute-start.4 = (bf16[128,512]{1,0:T(8,128)(2,1)S(1)}, bf16[128,512]{1,0:T(8,128)(2,1)S(1)}, u32[]{:S(2)}, u32[]{:S(2)}) collective-permute-start(bf16[128,512]{1,0:T(8,128)(2,1)S(1)} %bitcast.23), channel_id=1, source_target_pairs={{0,4},{1,5},{2,6},{3,7},{4,0},{5,1},{6,2},{7,3},{8,12},{9,13},{10,... | collective-permute-start | bytes 393224 | tf_op jit(solution)/shard_map/ppermute | solution.py:268
  13.1 22.0 %collective-permute-start.5 = (bf16[128,512]{1,0:T(8,128)(2,1)S(1)}, bf16[128,512]{1,0:T(8,128)(2,1)S(1)}, u32[]{:S(2)}, u32[]{:S(2)}) collective-permute-start(bf16[128,512]{1,0:T(8,128)(2,1)S(1)} %bitcast.24), channel_id=1, source_target_pairs={{0,6},{1,7},{2,4},{3,5},{4,2},{5,3},{6,0},{7,1},{8,14},{9,15},{10,... | collective-permute-start | bytes 393224 | tf_op jit(solution)/shard_map/ppermute | solution.py:268
  13.1 0.7 copy-start.3
  35.2 24.5 %copy-start.1 = (bf16[4,128,512]{2,1,0:T(8,128)(2,1)}, bf16[4,128,512]{2,1,0:T(8,128)(2,1)S(1)}, u32[]{:S(2)}) copy-start(bf16[4,128,512]{2,1,0:T(8,128)(2,1)S(1)} %pad_maximum_fusion.refs_0_) | copy-start | bytes 1572868
  35.2 24.5 %collective-permute-start.6 = (bf16[4,128,512]{2,1,0:T(8,128)(2,1)S(1)}, bf16[4,128,512]{2,1,0:T(8,128)(2,1)S(1)}, u32[]{:S(2)}, u32[]{:S(2)}) collective-permute-start(bf16[4,128,512]{2,1,0:T(8,128)(2,1)S(1)} %pad_maximum_fusion.refs_0_), channel_id=1, source_target_pairs={{0,1},{1,0},{2,3},{3,2},{4,5},{5,4},{6,7},{7,6},{8,9},{9,8},{10,11... | collective-permute-start | bytes 1572872 | tf_op jit(solution)/shard_map/ppermute | solution.py:268
  37.0 36.6 %collective-permute-start.7 = (f32[4,128,256]{2,1,0:T(8,128)}, f32[4,128,256]{2,1,0:T(8,128)S(1)}, u32[]{:S(2)}, u32[]{:S(2)}) collective-permute-start(f32[4,128,256]{2,1,0:T(8,128)} %get-tuple-element.33), channel_id=1, source_target_pairs={{0,1},{1,0},{2,3},{3,2},{4,5},{5,4},{6,7},{7,6},{8,9},{9,8},{10,11... | collective-permute-start | bytes 1572872 | tf_op jit(solution)/shard_map/ppermute | solution.py:268
  57.9 37.8 %collective-permute-start.8 = (f32[4,128,256]{2,1,0:T(8,128)}, f32[4,128,256]{2,1,0:T(8,128)S(1)}, u32[]{:S(2)}, u32[]{:S(2)}) collective-permute-start(f32[4,128,256]{2,1,0:T(8,128)} %get-tuple-element.37), channel_id=1, source_target_pairs={{0,1},{1,0},{2,3},{3,2},{4,5},{5,4},{6,7},{7,6},{8,9},{9,8},{10,11... | collective-permute-start | bytes 1572872 | tf_op jit(solution)/shard_map/ppermute | solution.py:268
  59.7 0.8 copy-start.7
  73.5 0.8 copy-start.6
  76.4 46.0 %collective-permute-start.10 = (f32[128,256]{1,0:T(8,128)}, f32[128,256]{1,0:T(8,128)S(1)}, u32[]{:S(2)}, u32[]{:S(2)}) collective-permute-start(f32[128,256]{1,0:T(8,128)} %get-tuple-element.41), channel_id=1, source_target_pairs={{0,4},{1,5},{2,6},{3,7},{4,0},{5,1},{6,2},{7,3},{8,12},{9,13},{10,... | collective-permute-start | bytes 393224 | tf_op jit(solution)/shard_map/ppermute | solution.py:268
  78.0 45.3 %collective-permute-start.11 = (f32[128,256]{1,0:T(8,128)}, f32[128,256]{1,0:T(8,128)S(1)}, u32[]{:S(2)}, u32[]{:S(2)}) collective-permute-start(f32[128,256]{1,0:T(8,128)} %get-tuple-element.42), channel_id=1, source_target_pairs={{0,6},{1,7},{2,4},{3,5},{4,2},{5,3},{6,0},{7,1},{8,14},{9,15},{10,... | collective-permute-start | bytes 393224 | tf_op jit(solution)/shard_map/ppermute | solution.py:268
  80.0 43.4 %collective-permute-start.9 = (f32[128,256]{1,0:T(8,128)}, f32[128,256]{1,0:T(8,128)S(1)}, u32[]{:S(2)}, u32[]{:S(2)}) collective-permute-start(f32[128,256]{1,0:T(8,128)} %get-tuple-element.40), channel_id=1, source_target_pairs={{0,2},{1,3},{2,0},{3,1},{4,6},{5,7},{6,4},{7,5},{8,10},{9,11},{10,... | collective-permute-start | bytes 393224 | tf_op jit(solution)/shard_map/ppermute | solution.py:268
  95.7 0.8 copy-start.5
  98.5 24.9 %collective-permute-start.12 = (f32[128,256]{1,0:T(8,128)}, f32[128,256]{1,0:T(8,128)S(1)}, u32[]{:S(2)}, u32[]{:S(2)}) collective-permute-start(f32[128,256]{1,0:T(8,128)} %get-tuple-element.43), channel_id=1, source_target_pairs={{0,2},{1,3},{2,0},{3,1},{4,6},{5,7},{6,4},{7,5},{8,10},{9,11},{10,... | collective-permute-start | bytes 393224 | tf_op jit(solution)/shard_map/ppermute | solution.py:268
  100.0 23.4 %collective-permute-start.13 = (f32[128,256]{1,0:T(8,128)}, f32[128,256]{1,0:T(8,128)S(1)}, u32[]{:S(2)}, u32[]{:S(2)}) collective-permute-start(f32[128,256]{1,0:T(8,128)} %get-tuple-element.44), channel_id=1, source_target_pairs={{0,4},{1,5},{2,6},{3,7},{4,0},{5,1},{6,2},{7,3},{8,12},{9,13},{10,... | collective-permute-start | bytes 393224 | tf_op jit(solution)/shard_map/ppermute | solution.py:268
  102.0 20.4 %copy-start.10 = (f32[128,256]{1,0:T(8,128)S(1)}, f32[128,256]{1,0:T(8,128)}, u32[]{:S(2)}) copy-start(f32[128,256]{1,0:T(8,128)} %get-tuple-element.45) | copy-start | bytes 393220
  102.0 21.3 %copy-start.8 = (f32[128,256]{1,0:T(8,128)S(1)}, f32[128,256]{1,0:T(8,128)}, u32[]{:S(2)}) copy-start(f32[128,256]{1,0:T(8,128)} %get-tuple-element.34) | copy-start | bytes 393220
  102.0 27.2 %copy-start.9 = (f32[128,256]{1,0:T(8,128)S(1)}, f32[128,256]{1,0:T(8,128)}, u32[]{:S(2)}) copy-start(f32[128,256]{1,0:T(8,128)} %get-tuple-element.38) | copy-start | bytes 393220
  122.4 6.8 %collective-permute-start.14 = (f32[128,256]{1,0:T(8,128)S(1)}, f32[128,256]{1,0:T(8,128)S(1)}, u32[]{:S(2)}, u32[]{:S(2)}) collective-permute-start(f32[128,256]{1,0:T(8,128)S(1)} %copy-done.10), channel_id=1, source_target_pairs={{0,6},{1,7},{2,4},{3,5},{4,2},{5,3},{6,0},{7,1},{8,14},{9,15},{10,... | collective-permute-start | bytes 393224 | tf_op jit(solution)/shard_map/ppermute | solution.py:268
  (2 other events, 1.3 us)

commit v3 on v0

v3 whole, which is shorter than its diff:
```python
import functools

import jax
import jax.numpy as jnp
from jax import lax
from jax.experimental import pallas as pl
from jax.experimental.pallas import tpu as pltpu
from jax.sharding import PartitionSpec as P

BF16 = jnp.bfloat16
F16 = jnp.float16
F32 = jnp.float32
F8 = jnp.float8_e4m3fn
MIB = 1024 * 1024
TINY = 1e-30


def split(wide):
    high = wide.astype(BF16)
    return high, wide - high.astype(F32)


def dot(left, right):
    return jnp.dot(left, right, preferred_element_type=F32)


def call(body, cost, limit, **kwargs):
    flops, moved = cost
    return pl.pallas_call(
        body,
        compiler_params=pltpu.CompilerParams(vmem_limit_bytes=limit * MIB),
        cost_estimate=pl.CostEstimate(flops=flops, bytes_accessed=moved, transcendentals=0),
        **kwargs,
    )


def whole(array):
    return pl.BlockSpec(array.shape, lambda i: (0,) * len(array.shape))


def largest(array):
    return jnp.max(jnp.abs(array.astype(F32)), keepdims=True)


def spot(axis, flip, block, count, base=0):
    if count == 1:
        return slice(base, base + block)
    return pl.ds(pl.multiple_of(base + (lax.axis_index(axis) ^ flip) * block, block), block)


def table_kernel(filters_ref, rows_ref):
    count, length = filters_ref.shape
    source = lax.broadcasted_iota(jnp.int32, (length, length), 0)
    token = lax.broadcasted_iota(jnp.int32, (length, length), 1)
    for k in range(count):
        spread = jnp.broadcast_to(filters_ref[k : k + 1, :], (length, length))
        shifted = pltpu.roll(spread, 0, 1, stride=1, stride_axis=0)
        high, low = split(jnp.where(token >= source, shifted, 0.0))
        rows_ref[k, :, :length] = high
        rows_ref[k, :, length:] = low.astype(BF16)


def make_tables(filters):
    count, length = filters.shape
    return call(
        table_kernel,
        (count * length * length * 4, count * length * length * 4),
        8,
        out_shape=jax.ShapeDtypeStruct((count, length, 2 * length), BF16),
    )(filters)


def back_kernel(cin_count, *refs):
    pieces = refs[:cin_count]
    rows_ref, matrix_ref, out, grads, parts, total = refs[cin_count:]
    step = pl.program_id(0)
    _, length, _ = rows_ref.shape
    out_width = matrix_ref.shape[1]
    seqs = grads.shape[1] // out_width
    tokens = seqs * length

    @pl.when(step == 0)
    def _():
        total[...] = jnp.zeros_like(total)
        block = pieces[0].shape[0]
        for b in range(seqs):
            for r, piece in enumerate(pieces):
                turned = piece[:, b * length : (b + 1) * length].astype(F32).T.astype(BF16)
                columns = spot("cin", r, block, cin_count, b * out_width)
                grads[:length, columns] = turned
                grads[length:, columns] = turned

    table = rows_ref[pl.ds(2 * step, 2)].reshape(2 * length, 2 * length)
    for b in range(seqs):
        high, low = split(dot(table, grads[:, b * out_width : (b + 1) * out_width]))
        low = low.astype(BF16)
        for k in range(2):
            source, columns = slice(k * length, (k + 1) * length), slice(k * out_width, (k + 1) * out_width)
            parts[b * length : (b + 1) * length, columns] = high[source]
            parts[tokens + b * length : tokens + (b + 1) * length, columns] = low[source]
    matrix = matrix_ref[...].reshape(2 * out_width, -1)
    total[...] += dot(parts[:tokens], matrix) + dot(parts[tokens:], matrix)

    @pl.when(step == pl.num_programs(0) - 1)
    def _():
        summed = total[...]
        exponent = jnp.floor(jnp.log2(jnp.maximum(largest(summed), TINY))) + 1.0
        summed = summed * jnp.exp2(14.0 - exponent)
        block = out.shape[1] - 8
        turned = [] if block % 128 == 0 else [summed.T]
        for j in range(out.shape[0]):
            place = slice(j * block, (j + 1) * block)
            out[j, :block] = turned[0][place] if turned else summed[:, place].T
            out[j, block:] = jnp.broadcast_to(exponent, (8, tokens))


def back_sums(pieces, rows, matrices, cout):
    count, out_width, in_width = matrices.shape
    length = rows.shape[1]
    tokens = pieces[0].shape[1]
    seqs = tokens // length
    out = jax.ShapeDtypeStruct((cout, in_width // cout + 8, tokens), F32)
    return call(
        functools.partial(back_kernel, len(pieces)),
        (4 * count * out_width * in_width * tokens, 2 * matrices.size),
        32,
        out_shape=out,
        grid=(count // 2,),
        in_specs=[whole(piece) for piece in pieces]
        + [whole(rows), pl.BlockSpec((2, out_width, in_width), lambda i: (i, 0, 0))],
        out_specs=whole(out),
        scratch_shapes=[
            pltpu.VMEM((2 * length, seqs * out_width), BF16),
            pltpu.VMEM((2 * tokens, 2 * out_width), BF16),
            pltpu.VMEM((tokens, in_width), F32),
        ],
    )(*pieces, rows, matrices)


def matrix_kernel(cin_count, input_count, cout_count, *refs):
    pieces = refs[:cin_count]
    input_pieces = refs[cin_count : cin_count + input_count]
    rows_ref, out_ref, grads, inputs, inputs8, parts, parts8, bounds = refs[cin_count + input_count :]
    step = pl.program_id(0)
    _, length, _ = rows_ref.shape
    tokens = inputs.shape[0]
    seqs = tokens // length
    out_width = out_ref.shape[1]

    @pl.when(step == 0)
    def _():
        block = pieces[0].shape[0]
        for r, piece in enumerate(pieces):
            for b in range(seqs):
                rows = spot("cin", r, block, cin_count, b * out_width)
                part = piece[:, b * length : (b + 1) * length]
                grads[rows, :length] = part
                grads[rows, length:] = part
        gmax = functools.reduce(jnp.maximum, [largest(piece[...]) for piece in pieces])
        xmax = functools.reduce(jnp.maximum, [largest(piece[half]) for piece in input_pieces for half in range(piece.shape[0])])
        xmax = jnp.maximum(xmax, TINY)
        bounds[0:1, :] = jnp.broadcast_to(gmax, (1, length))
        bounds[1:2, :] = jnp.broadcast_to(xmax, (1, length))
        block = input_pieces[0].shape[1]
        for r, piece in enumerate(input_pieces):
            for half in range(piece.shape[0]):
                columns = spot("cout", 2 * r + half, block, cout_count)
                turned = piece[half].astype(F32).T
                inputs[:, columns] = turned.astype(BF16)
                inputs8[:, columns] = (turned * (256.0 / xmax)).astype(F8)

    table = rows_ref[pl.ds(2 * step, 2)]
    reach = [
        jnp.maximum(jnp.sum(jnp.abs(table[k, 0:1, :length].astype(F32)), keepdims=True) * bounds[0:1, 0:1], TINY)
        for k in range(2)
    ]
    table = table.reshape(2 * length, 2 * length)
    for b in range(seqs):
        place = slice(b * length, (b + 1) * length)
        filtered = lax.dot_general(
            grads[b * out_width : (b + 1) * out_width], table, (((1,), (1,)), ((), ())), preferred_element_type=F32
        )
        high, low = split(filtered)
        for k in range(2):
            source = slice(k * length, (k + 1) * length)
            rows = slice(k * out_width, (k + 1) * out_width)
            parts[rows, place] = high[:, source]
            parts8[rows, place] = (low[:, source] * (65536.0 / reach[k])).astype(F8)
    for k in range(2):
        rows = slice(k * out_width, (k + 1) * out_width)
        back = (reach[k] / 65536.0) * (bounds[1:2, 0:1] / 256.0)
        product = dot(parts[rows], inputs[...]) + dot(parts8[rows], inputs8[...]) * back
        out_ref[k] = product.astype(BF16)


def matrix_sums(pieces, input_pieces, rows, cout_count, shape):
    count, out_width, in_width = shape
    length = rows.shape[1]
    tokens = pieces[0].shape[1]
    seqs = tokens // length
    return call(
        functools.partial(matrix_kernel, len(pieces), len(input_pieces), cout_count),
        (3 * count * out_width * in_width * tokens, 2 * count * out_width * in_width),
        32,
        out_shape=jax.ShapeDtypeStruct(shape, BF16),
        grid=(count // 2,),
        in_specs=[whole(piece) for piece in (*pieces, *input_pieces)] + [whole(rows)],
        out_specs=pl.BlockSpec((2, out_width, in_width), lambda i: (i, 0, 0)),
        scratch_shapes=[
            pltpu.VMEM((seqs * out_width, 2 * length), BF16),
            pltpu.VMEM((tokens, in_width), BF16),
            pltpu.VMEM((tokens, in_width), F8),
            pltpu.VMEM((2 * out_width, tokens), BF16),
            pltpu.VMEM((2 * out_width, tokens), F8),
            pltpu.VMEM((8, length), F32),
        ],
    )(*pieces, *input_pieces, rows)


def exchange(array, axis, count, flip):
    return lax.ppermute(array, axis, [(i, i ^ flip) for i in range(count)])


def shards(cin, cout, inputs, cotangent, matrices, filters):
    own, seq_count, length = inputs.shape
    tokens = seq_count * length
    flat_grads = cotangent.reshape(-1, tokens)
    if cin & (cin - 1) or flat_grads.shape[0] % 128:
        pieces = [lax.all_gather(flat_grads, "cin", axis=0, tiled=True)]
    else:
        pieces = [flat_grads] + [exchange(flat_grads, "cin", cin, flip) for flip in range(1, cin)]
    rows = make_tables(filters)
    flat_inputs = inputs.reshape(-1, tokens)
    if cout < 2 or cout & (cout - 1) or own % 128:
        input_pieces = [lax.all_gather(flat_inputs, "cout", axis=0, tiled=True)[None]]
        cout_count = 1
    else:
        both = jnp.stack([flat_inputs, exchange(flat_inputs, "cout", cout, 1)])
        input_pieces = [both] + [exchange(both, "cout", cout, flip) for flip in range(2, cout, 2)]
        cout_count = cout

    blocks = back_sums(pieces, rows, matrices, cout).astype(F16)
    came = lax.all_to_all(blocks, "cout", 0, 0, tiled=True).astype(F32)
    matrix_grads = matrix_sums(pieces, input_pieces, rows, cout_count, matrices.shape)
    scales = jnp.exp2(came[:, own : own + 1] - 14.0)
    input_grads = jnp.sum(came[:, :own] * scales, axis=0).astype(BF16)
    return (matrix_grads, input_grads.reshape(own, seq_count, length))


def solution(mesh):
    placed = (
        P(("cin", "cout"), None, None),
        P(("cout", "cin"), None, None),
        P(None, "cout", "cin"),
        P(),
    )
    return jax.shard_map(
        functools.partial(shards, mesh.shape["cin"], mesh.shape["cout"]),
        mesh=mesh,
        in_specs=placed,
        out_specs=(P(None, "cout", "cin"), P(("cin", "cout"), None, None)),
        check_vma=False,
    )
```

time: 838 us -> 87.2 us (0.10)
  matrix products: 364 us -> 0 us
  local copies, waits for them, and re-layouts: 259 us -> 4.21 us
  waiting for transfers between devices: 102 us -> 0.11 us
  other arithmetic: 82.7 us -> 3.14 us
  Pallas kernels: 0 us -> 64.4 us
  starting transfers between devices: 0.08 us -> 14.3 us
  between operations: 14.1 us -> 0.73 us
  blocking collectives: 8.83 us -> 0 us
    dot_general x96 -> x0, matrix products: 364 us -> none  [the longest x24 129 us: per_filter(): jnp.dot(grads_wide, filtered.T, precision=highest).astype(jnp.bfloat16)]
    reshape x97 -> x0, local copies, waits for them, and re-layouts: 127 us -> none  [the longest x24 41.6 us: per_filter(): return (carried + pulled.reshape(in_width, -1), matrix_grad)]
    add x24 -> x0, other arithmetic: 80.4 us -> none  [per_filter(): return (carried + pulled.reshape(in_width, -1), matrix_grad)]
    reduce_scatter x1 -> x0, waiting for transfers between devices: 66.5 us -> none  [shards(): lax.psum_scatter(partial_sum, 'cout', scatter_dimension=0, tiled=True)]
    pallas_call x0 -> x3, Pallas kernels: none -> 64.4 us  [the longest x1 34.5 us: back_sums(): call(functools.partial(back_kernel, len(pieces)), (4 * count * out_width...]
    dot_general x24 -> x0, local copies, waits for them, and re-layouts: 45.8 us -> none  [per_filter(): jnp.dot(inputs_wide.reshape(-1, length), upper_table, precision=highest)]
    dynamic_update_slice x48 -> x0, local copies, waits for them, and re-layouts: 37.7 us -> none  [shards(): lax.scan(per_filter, start_sum, (filters, matrices))]
    all_gather x1 -> x0, waiting for transfers between devices: 34.8 us -> none  [shards(): inputs_all = lax.all_gather(inputs, 'cout', axis=0, tiled=True)]
  transfers between devices with their start and end apart: 2 -> 8, of which waited for: 2 -> 1; matrix products, arithmetic and copies ran while one was open for 0% -> 4% of each run, Pallas kernels for 0% -> 74%
where the time goes in v3:
time: 87.2 us; the launch traced here: 86.9 us
  Pallas kernels  64.4 us (74%)
  starting transfers between devices  14.3 us (16%)
  local copies, waits for them, and re-layouts  4.21 us (5%)
  other arithmetic  3.14 us (4%)
    pallas_call x1, Pallas kernels, back_sums(): call(functools.partial(back_kernel, len(pieces)), (4 * count * out_width...  34.5 us
    pallas_call x1, Pallas kernels, matrix_sums(): call(functools.partial(matrix_kernel, len(pieces), len(input_pieces), cou...  29.5 us
    ppermute x7, starting transfers between devices, exchange(): return lax.ppermute(array, axis, [(i, i ^ flip) for i in range(count)])  9.41 us
    all_to_all x1, starting transfers between devices, shards(): came = lax.all_to_all(blocks, 'cout', 0, 0, tiled=True).astype(F32)  4.88 us
    unnamed x5, local copies, waits for them, and re-layouts  2.55 us
  transfers between devices with their start and end apart: 8, of which 1 were waited for; matrix products, arithmetic and copies ran while one was open for 4% of the time, Pallas kernels for 74%

profile of v3, /device:TPU:0, one launch (start us, length us, event | category | flops | bytes accessed | tf_op | source)
XLA Modules:
  0.0 86.9 jit_solution(13305434646637008704)
XLA Ops:
  0.6 0.9 %copy.12 = bf16[16,8,4,128]{3,1,2,0:T(8,128)(2,1)S(1)} copy(bf16[16,8,4,128]{3,2,1,0:T(4,128)(2,1)} %bitcast.17) | data formatting | bytes 262144
  1.6 3.0 %collective-permute-start.3 = (bf16[128,512]{1,0:T(8,128)(2,1)S(1)}, bf16[128,512]{1,0:T(8,128)(2,1)S(1)}, u32[]{:S(2)}, u32[]{:S(2)}) collective-permute-start(bf16[128,512]{1,0:T(8,128)(2,1)S(1)} %bitcast.19), channel_id=1, source_target_pairs={{0,1},{1,0},{2,3},{3,2},{4,5},{5,4},{6,7},{7,6},{8,9},{9,8},{10,11... | collective-permute-start | bytes 393224 | tf_op jit(solution)/shard_map/ppermute | solution.py:221
  4.6 0.9 %copy.13 = bf16[16,8,4,128]{3,1,2,0:T(8,128)(2,1)S(1)} copy(bf16[16,8,4,128]{3,2,1,0:T(4,128)(2,1)} %bitcast.18) | data formatting | bytes 262144
  5.5 0.7 collective-permute-start.2
  6.2 0.9 %collective-permute-start.1 = (bf16[128,512]{1,0:T(8,128)(2,1)S(1)}, bf16[128,512]{1,0:T(8,128)(2,1)S(1)}, u32[]{:S(2)}, u32[]{:S(2)}) collective-permute-start(bf16[128,512]{1,0:T(8,128)(2,1)S(1)} %bitcast.13), channel_id=1, source_target_pairs={{0,16},{8,24},{16,0},{24,8},{1,17},{9,25},{17,1},{25,9},{2,18},{10... | collective-permute-start | bytes 393224 | tf_op jit(solution)/shard_map/ppermute | solution.py:221
  7.2 0.3 collective-permute-start
  7.4 1.0 %stack_reshape.3 = bf16[1,128,512]{2,1,0:T(8,128)(2,1)S(1)} reshape(bf16[128,4,128]{2,1,0:T(4,128)(2,1)} %param.4) | data formatting | bytes 262144 | tf_op jit(solution)/shard_map/stack;reshape | solution.py:238
  8.4 0.0 copy-start
  8.4 0.7 copy-done
  9.1 0.5 shard_map.59.refs_8_.refs_4_
  9.6 0.0 collective-permute-done.3
  9.6 3.7 %collective-permute-start.6 = (bf16[2,128,512]{2,1,0:T(8,128)(2,1)S(1)}, bf16[2,128,512]{2,1,0:T(8,128)(2,1)S(1)}, u32[]{:S(2)}, u32[]{:S(2)}) collective-permute-start(bf16[2,128,512]{2,1,0:T(8,128)(2,1)S(1)} %pad_maximum_fusion.refs_4_), channel_id=1, source_target_pairs={{0,6},{1,7},{2,4},{3,5},{4,2},{5,3},{6,0},{7,1},{8,14},{9,15},{10,... | collective-permute-start | bytes 786440 | tf_op jit(solution)/shard_map/ppermute | solution.py:221
  13.3 0.0 collective-permute-start.5
  13.3 0.0 collective-permute-done.2.refs_3_
  13.3 0.8 collective-permute-start.4
  14.1 0.1 collective-permute-done.1.refs_2_
  14.2 0.0 collective-permute-done.refs_1_
  14.2 34.5 %shard_map.61 = f32[8,136,512]{2,1,0:T(8,128)S(1)} custom-call(bf16[128,512]{1,0:T(8,128)(2,1)S(1)} %bitcast.15, bf16[128,512]{1,0:T(8,128)(2,1)S(1)} %collective-permute-done.refs_1_, bf16[128,512]{1,0:T(8,128)(2,1)S(1)} %collective-permute-done.1.refs_2_, bf16[128,512]{1,0:T(8,128)(2,1)S(1)} %collective-permute-done.2.refs_3_, ...), custom_call_target="tpu_custom_call" | custom-call | flops 25769803776 | bytes 25165824 | tf_op jit(solution)/shard_map/pallas_call | solution.py:123
  48.7 1.3 %convert_element_type.13 = f16[8,136,512]{2,1,0:T(8,128)(2,1)} convert(f32[8,136,512]{2,1,0:T(8,128)S(1)} %shard_map.61) | non-fusion elementwise | flops 557056 | bytes 3342336 | tf_op jit(solution)/shard_map/convert_element_type | solution.py:242
  50.0 4.9 %all-to-all-start = ((f16[8,136,512]{2,1,0:T(8,128)(2,1)}), f16[8,136,512]{2,1,0:T(8,128)(2,1)}, u32[]{:S(2)}, u32[]{:S(2)}) async-start(f16[8,136,512]{2,1,0:T(8,128)(2,1)} %convert_element_type.13), calls=%async_computation | async-start | bytes 2228224 | tf_op jit(solution)/shard_map/all_to_all | solution.py:243
  54.9 29.5 %shard_map.60 = bf16[24,512,1024]{2,1,0:T(8,128)(2,1)} custom-call(bf16[128,512]{1,0:T(8,128)(2,1)S(1)} %bitcast.16, bf16[128,512]{1,0:T(8,128)(2,1)S(1)} %collective-permute-done.refs_1_, bf16[128,512]{1,0:T(8,128)(2,1)S(1)} %collective-permute-done.1.refs_2_, bf16[128,512]{1,0:T(8,128)(2,1)S(1)} %collective-permute-done.2.refs_3_, ...), custom_call_target="tpu_custom_call" | custom-call | flops 19327352832 | bytes 25165824 | tf_op jit(solution)/shard_map/pallas_call | solution.py:201
  84.4 1.5 %convert_element_type.14 = f32[8,136,512]{2,1,0:T(8,128)S(1)} convert(f16[8,136,512]{2,1,0:T(8,128)(2,1)} %all-to-all-done) | non-fusion elementwise | flops 557056 | bytes 3342336 | tf_op jit(solution)/shard_map/convert_element_type | solution.py:243
  86.0 0.3 fusion
  86.2 0.7 convert_element_type.16
  (7 shorter events, 0.1 us)
Async XLA Ops:
  1.6 8.0 %collective-permute-start.3 = (bf16[128,512]{1,0:T(8,128)(2,1)S(1)}, bf16[128,512]{1,0:T(8,128)(2,1)S(1)}, u32[]{:S(2)}, u32[]{:S(2)}) collective-permute-start(bf16[128,512]{1,0:T(8,128)(2,1)S(1)} %bitcast.19), channel_id=1, source_target_pairs={{0,1},{1,0},{2,3},{3,2},{4,5},{5,4},{6,7},{7,6},{8,9},{9,8},{10,11... | collective-permute-start | bytes 393224 | tf_op jit(solution)/shard_map/ppermute | solution.py:221
  5.5 7.8 %collective-permute-start.2 = (bf16[128,512]{1,0:T(8,128)(2,1)S(1)}, bf16[128,512]{1,0:T(8,128)(2,1)S(1)}, u32[]{:S(2)}, u32[]{:S(2)}) collective-permute-start(bf16[128,512]{1,0:T(8,128)(2,1)S(1)} %bitcast.12), channel_id=1, source_target_pairs={{0,24},{8,16},{16,8},{24,0},{1,25},{9,17},{17,9},{25,1},{2,26},{10... | collective-permute-start | bytes 393224 | tf_op jit(solution)/shard_map/ppermute | solution.py:221
  6.2 8.0 %collective-permute-start.1 = (bf16[128,512]{1,0:T(8,128)(2,1)S(1)}, bf16[128,512]{1,0:T(8,128)(2,1)S(1)}, u32[]{:S(2)}, u32[]{:S(2)}) collective-permute-start(bf16[128,512]{1,0:T(8,128)(2,1)S(1)} %bitcast.13), channel_id=1, source_target_pairs={{0,16},{8,24},{16,0},{24,8},{1,17},{9,25},{17,1},{25,9},{2,18},{10... | collective-permute-start | bytes 393224 | tf_op jit(solution)/shard_map/ppermute | solution.py:221
  7.2 7.0 %collective-permute-start = (bf16[128,512]{1,0:T(8,128)(2,1)S(1)}, bf16[128,512]{1,0:T(8,128)(2,1)S(1)}, u32[]{:S(2)}, u32[]{:S(2)}) collective-permute-start(bf16[128,512]{1,0:T(8,128)(2,1)S(1)} %bitcast.14), channel_id=1, source_target_pairs={{0,8},{8,0},{16,24},{24,16},{1,9},{9,1},{17,25},{25,17},{2,10},{10... | collective-permute-start | bytes 393224 | tf_op jit(solution)/shard_map/ppermute | solution.py:221
  8.4 0.7 copy-start
  9.6 45.2 %collective-permute-start.6 = (bf16[2,128,512]{2,1,0:T(8,128)(2,1)S(1)}, bf16[2,128,512]{2,1,0:T(8,128)(2,1)S(1)}, u32[]{:S(2)}, u32[]{:S(2)}) collective-permute-start(bf16[2,128,512]{2,1,0:T(8,128)(2,1)S(1)} %pad_maximum_fusion.refs_4_), channel_id=1, source_target_pairs={{0,6},{1,7},{2,4},{3,5},{4,2},{5,3},{6,0},{7,1},{8,14},{9,15},{10,... | collective-permute-start | bytes 786440 | tf_op jit(solution)/shard_map/ppermute | solution.py:221
  13.3 41.6 %collective-permute-start.5 = (bf16[2,128,512]{2,1,0:T(8,128)(2,1)S(1)}, bf16[2,128,512]{2,1,0:T(8,128)(2,1)S(1)}, u32[]{:S(2)}, u32[]{:S(2)}) collective-permute-start(bf16[2,128,512]{2,1,0:T(8,128)(2,1)S(1)} %pad_maximum_fusion.refs_4_), channel_id=1, source_target_pairs={{0,4},{1,5},{2,6},{3,7},{4,0},{5,1},{6,2},{7,3},{8,12},{9,13},{10,... | collective-permute-start | bytes 786440 | tf_op jit(solution)/shard_map/ppermute | solution.py:221
  13.3 41.6 %collective-permute-start.4 = (bf16[2,128,512]{2,1,0:T(8,128)(2,1)S(1)}, bf16[2,128,512]{2,1,0:T(8,128)(2,1)S(1)}, u32[]{:S(2)}, u32[]{:S(2)}) collective-permute-start(bf16[2,128,512]{2,1,0:T(8,128)(2,1)S(1)} %pad_maximum_fusion.refs_4_), channel_id=1, source_target_pairs={{0,2},{1,3},{2,0},{3,1},{4,6},{5,7},{6,4},{7,5},{8,10},{9,11},{10,... | collective-permute-start | bytes 786440 | tf_op jit(solution)/shard_map/ppermute | solution.py:221
  50.0 34.4 %all-to-all-start = ((f16[8,136,512]{2,1,0:T(8,128)(2,1)}), f16[8,136,512]{2,1,0:T(8,128)(2,1)}, u32[]{:S(2)}, u32[]{:S(2)}) async-start(f16[8,136,512]{2,1,0:T(8,128)(2,1)} %convert_element_type.13), calls=%async_computation | async-start | bytes 2228224 | tf_op jit(solution)/shard_map/all_to_all | solution.py:243

commit v4 on v3

--- a/solution.py
+++ b/solution.py
@@ -46,6 +46,12 @@
     if count == 1:
         return slice(base, base + block)
     return pl.ds(pl.multiple_of(base + (lax.axis_index(axis) ^ flip) * block, block), block)
+
+
+def reach_of(table, gmax):
+    length = table.shape[1]
+    sums = [jnp.sum(jnp.abs(table[k, 0:1, :length].astype(F32)), keepdims=True) for k in range(2)]
+    return [jnp.maximum(total * gmax, TINY) for total in sums]
 
 
 def table_kernel(filters_ref, rows_ref):
@@ -72,7 +78,7 @@
 
 def back_kernel(cin_count, *refs):
     pieces = refs[:cin_count]
-    rows_ref, matrix_ref, out, grads, parts, total = refs[cin_count:]
+    rows_ref, matrix_ref, out, grads, parts, parts8, total, bounds = refs[cin_count:]
     step = pl.program_id(0)
     _, length, _ = rows_ref.shape
     out_width = matrix_ref.shape[1]
@@ -89,17 +95,26 @@
                 columns = spot("cin", r, block, cin_count, b * out_width)
                 grads[:length, columns] = turned
                 grads[length:, columns] = turned
-
-    table = rows_ref[pl.ds(2 * step, 2)].reshape(2 * length, 2 * length)
+        gmax = functools.reduce(jnp.maximum, [largest(piece[...]) for piece in pieces])
+        bounds[...] = jnp.broadcast_to(gmax, bounds.shape)
+
+    matrix = matrix_ref[...].reshape(2 * out_width, -1)
+    peak = jnp.max(jnp.abs(matrix).reshape(-1, 16, matrix.shape[1]), axis=0)
+    matrix_scale = (256.0 / jnp.maximum(largest(peak), TINY)).astype(BF16)
+    matrix8 = (matrix * matrix_scale).astype(F8)
+    table = rows_ref[pl.ds(2 * step, 2)]
+    reach = reach_of(table, bounds[0:1, 0:1])
+    reach = jnp.maximum(reach[0], reach[1])
+    table = table.reshape(2 * length, 2 * length)
     for b in range(seqs):
         high, low = split(dot(table, grads[:, b * out_width : (b + 1) * out_width]))
-        low = low.astype(BF16)
+        low = (low * (65536.0 / reach)).astype(F8)
         for k in range(2):
             source, columns = slice(k * length, (k + 1) * length), slice(k * out_width, (k + 1) * out_width)
             parts[b * length : (b + 1) * length, columns] = high[source]
-            parts[tokens + b * length : tokens + (b + 1) * length, columns] = low[source]
-    matrix = matrix_ref[...].reshape(2 * out_width, -1)
-    total[...] += dot(parts[:tokens], matrix) + dot(parts[tokens:], matrix)
+            parts8[b * length : (b + 1) * length, columns] = low[source]
+    back = (reach / 65536.0) / matrix_scale.astype(F32)
+    total[...] += dot(parts[...], matrix) + dot(parts8[...], matrix8) * back
 
     @pl.when(step == pl.num_programs(0) - 1)
     def _():
@@ -131,8 +146,10 @@
         out_specs=whole(out),
         scratch_shapes=[
             pltpu.VMEM((2 * length, seqs * out_width), BF16),
-            pltpu.VMEM((2 * tokens, 2 * out_width), BF16),
+            pltpu.VMEM((tokens, 2 * out_width), BF16),
+            pltpu.VMEM((tokens, 2 * out_width), F8),
             pltpu.VMEM((tokens, in_width), F32),
+            pltpu.VMEM((8, length), F32),
         ],
     )(*pieces, rows, matrices)
 
@@ -169,28 +186,36 @@
                 inputs[:, columns] = turned.astype(BF16)
                 inputs8[:, columns] = (turned * (256.0 / xmax)).astype(F8)
 
-    table = rows_ref[pl.ds(2 * step, 2)]
-    reach = [
-        jnp.maximum(jnp.sum(jnp.abs(table[k, 0:1, :length].astype(F32)), keepdims=True) * bounds[0:1, 0:1], TINY)
-        for k in range(2)
-    ]
-    table = table.reshape(2 * length, 2 * length)
-    for b in range(seqs):
-        place = slice(b * length, (b + 1) * length)
-        filtered = lax.dot_general(
-            grads[b * out_width : (b + 1) * out_width], table, (((1,), (1,)), ((), ())), preferred_element_type=F32
-        )
-        high, low = split(filtered)
+    def pair(p, _):
+        table = rows_ref[pl.ds(4 * step + 2 * p, 2)]
+        reach = reach_of(table, bounds[0:1, 0:1])
+        table = table.reshape(2 * length, 2 * length)
         for k in range(2):
-            source = slice(k * length, (k + 1) * length)
-            rows = slice(k * out_width, (k + 1) * out_width)
-            parts[rows, place] = high[:, source]
-            parts8[rows, place] = (low[:, source] * (65536.0 / reach[k])).astype(F8)
-    for k in range(2):
-        rows = slice(k * out_width, (k + 1) * out_width)
-        back = (reach[k] / 65536.0) * (bounds[1:2, 0:1] / 256.0)
-        product = dot(parts[rows], inputs[...]) + dot(parts8[rows], inputs8[...]) * back
-        out_ref[k] = product.astype(BF16)
+            back = (reach[k] / 65536.0) * (bounds[1:2, 0:1] / 256.0)
+            bounds[2 + k : 3 + k, :] = jnp.broadcast_to(back, (1, length))
+
+        def sequence(b, _):
+            place = pl.ds(pl.multiple_of(b * length, length), length)
+            source = grads[pl.ds(pl.multiple_of(b * out_width, out_width), out_width)]
+            filtered = lax.dot_general(source, table, (((1,), (1,)), ((), ())), preferred_element_type=F32)
+            high, low = split(filtered)
+            for k in range(2):
+                columns = slice(k * length, (k + 1) * length)
+                parts[k, :, place] = high[:, columns]
+                parts8[k, :, place] = (low[:, columns] * (65536.0 / reach[k])).astype(F8)
+            return _
+
+        lax.fori_loop(0, seqs, sequence, 0)
+
+        def product(k, _):
+            back = bounds[pl.ds(2 + k, 1), 0:1]
+            total = dot(parts[k], inputs[...]) + dot(parts8[k], inputs8[...]) * back
+            out_ref[2 * p + k] = total.astype(BF16)
+            return _
+
+        return lax.fori_loop(0, 2, product, 0)
+
+    lax.fori_loop(0, 2, pair, 0)
 
 
 def matrix_sums(pieces, input_pieces, rows, cout_count, shape):
@@ -203,15 +228,15 @@
         (3 * count * out_width * in_width * tokens, 2 * count * out_width * in_width),
         32,
         out_shape=jax.ShapeDtypeStruct(shape, BF16),
-        grid=(count // 2,),
+        grid=(count // 4,),
         in_specs=[whole(piece) for piece in (*pieces, *input_pieces)] + [whole(rows)],
-        out_specs=pl.BlockSpec((2, out_width, in_width), lambda i: (i, 0, 0)),
+        out_specs=pl.BlockSpec((4, out_width, in_width), lambda i: (i, 0, 0)),
         scratch_shapes=[
             pltpu.VMEM((seqs * out_width, 2 * length), BF16),
             pltpu.VMEM((tokens, in_width), BF16),
             pltpu.VMEM((tokens, in_width), F8),
-            pltpu.VMEM((2 * out_width, tokens), BF16),
-            pltpu.VMEM((2 * out_width, tokens), F8),
+            pltpu.VMEM((2, out_width, tokens), BF16),
+            pltpu.VMEM((2, out_width, tokens), F8),
             pltpu.VMEM((8, length), F32),
         ],
     )(*pieces, *input_pieces, rows)
@@ -229,21 +254,21 @@
         pieces = [lax.all_gather(flat_grads, "cin", axis=0, tiled=True)]
     else:
         pieces = [flat_grads] + [exchange(flat_grads, "cin", cin, flip) for flip in range(1, cin)]
-    rows = make_tables(filters)
+    rows = make_tables(lax.optimization_barrier((filters, flat_grads))[0])
     flat_inputs = inputs.reshape(-1, tokens)
     if cout < 2 or cout & (cout - 1) or own % 128:
         input_pieces = [lax.all_gather(flat_inputs, "cout", axis=0, tiled=True)[None]]
         cout_count = 1
     else:
-        both = jnp.stack([flat_inputs, exchange(flat_inputs, "cout", cout, 1)])
+        both = jnp.concatenate([flat_inputs, exchange(flat_inputs, "cout", cout, 1)]).reshape(2, own, tokens)
         input_pieces = [both] + [exchange(both, "cout", cout, flip) for flip in range(2, cout, 2)]
         cout_count = cout
 
     blocks = back_sums(pieces, rows, matrices, cout).astype(F16)
-    came = lax.all_to_all(blocks, "cout", 0, 0, tiled=True).astype(F32)
+    came = lax.all_to_all(blocks, "cout", 0, 0, tiled=True)
     matrix_grads = matrix_sums(pieces, input_pieces, rows, cout_count, matrices.shape)
-    scales = jnp.exp2(came[:, own : own + 1] - 14.0)
-    input_grads = jnp.sum(came[:, :own] * scales, axis=0).astype(BF16)
+    scales = jnp.exp2(came[:, own : own + 1].astype(F32) - 14.0)
+    input_grads = jnp.sum(came[:, :own].astype(F32) * scales, axis=0).astype(BF16)
     return (matrix_grads, input_grads.reshape(own, seq_count, length))
 
 

time: 87.2 us -> 98.4 us (1.13)
  Pallas kernels: 64.4 us -> 75.1 us
    pallas_call x1, Pallas kernels: 29.5 us -> 43.1 us  [matrix_sums(): call(functools.partial(matrix_kernel, len(pieces), len(input_pieces), cou...]
    pallas_call x1, Pallas kernels: 34.5 us -> 31.5 us  [back_sums(): call(functools.partial(back_kernel, len(pieces)), (4 * count * out_width...]
    convert_element_type x1 -> x0, other arithmetic: 1.55 us -> none  [shards(): came = lax.all_to_all(blocks, 'cout', 0, 0, tiled=True).astype(F32)]
    reduce_sum x1, other arithmetic: 0.26 us -> 1.44 us  [shards(): jnp.sum(came[:, :own].astype(F32) * scales, axis=0).astype(BF16)]
  transfers between devices with their start and end apart: 8 -> 8, of which waited for: 1 -> 1; matrix products, arithmetic and copies ran while one was open for 4% -> 2% of each run, Pallas kernels for 74% -> 77%
where the time goes in v4:
time: 98.4 us; the launch traced here: 98 us
  Pallas kernels  75.1 us (76%)
  starting transfers between devices  14.3 us (15%)
  other arithmetic  3.61 us (4%)
  local copies, waits for them, and re-layouts  3.25 us (3%)
  waiting for transfers between devices  1.08 us (1%)
    pallas_call x1, Pallas kernels, matrix_sums(): call(functools.partial(matrix_kernel, len(pieces), len(input_pieces), cou...  43.1 us
    pallas_call x1, Pallas kernels, back_sums(): call(functools.partial(back_kernel, len(pieces)), (4 * count * out_width...  31.5 us
    ppermute x7, starting transfers between devices, exchange(): return lax.ppermute(array, axis, [(i, i ^ flip) for i in range(count)])  9.41 us
    all_to_all x1, starting transfers between devices, shards(): came = lax.all_to_all(blocks, 'cout', 0, 0, tiled=True)  4.87 us
    unnamed x5, local copies, waits for them, and re-layouts  2.56 us
  transfers between devices with their start and end apart: 8, of which 1 were waited for; matrix products, arithmetic and copies ran while one was open for 2% of the time, Pallas kernels for 77%

profile of v4, /device:TPU:0, one launch (start us, length us, event | category | flops | bytes accessed | tf_op | source)
XLA Modules:
  0.0 98.0 jit_solution(10477399350180401433)
XLA Ops:
  0.6 0.9 copy.12
  1.6 3.0 %collective-permute-start.3 = (bf16[128,512]{1,0:T(8,128)(2,1)S(1)}, bf16[128,512]{1,0:T(8,128)(2,1)S(1)}, u32[]{:S(2)}, u32[]{:S(2)}) collective-permute-start(bf16[128,512]{1,0:T(8,128)(2,1)S(1)} %bitcast.21), channel_id=1, source_target_pairs={{0,1},{1,0},{2,3},{3,2},{4,5},{5,4},{6,7},{7,6},{8,9},{9,8},{10,11... | collective-permute-start | bytes 393224 | tf_op jit(solution)/shard_map/ppermute | solution.py:246
  4.6 0.9 copy.13
  5.5 0.7 collective-permute-start.2
  6.2 0.9 collective-permute-start.1
  7.2 0.3 collective-permute-start
  7.4 0.7 copy-done
  8.2 0.5 shard_map.59.refs_8_.refs_4_
  8.6 0.0 collective-permute-done.3
  8.7 3.7 %collective-permute-start.6 = (bf16[2,128,512]{2,1,0:T(8,128)(2,1)S(1)}, bf16[2,128,512]{2,1,0:T(8,128)(2,1)S(1)}, u32[]{:S(2)}, u32[]{:S(2)}) collective-permute-start(bf16[2,128,512]{2,1,0:T(8,128)(2,1)S(1)} %bitcast.12), channel_id=1, source_target_pairs={{0,6},{1,7},{2,4},{3,5},{4,2},{5,3},{6,0},{7,1},{8,14},{9,15},{10,... | collective-permute-start | bytes 786440 | tf_op jit(solution)/shard_map/ppermute | solution.py:246
  12.3 0.0 collective-permute-start.5
  12.3 0.8 collective-permute-start.4
  13.1 1.1 %collective-permute-done.1.refs_2_ = bf16[128,512]{1,0:T(8,128)(2,1)S(1)} collective-permute-done((bf16[128,512]{1,0:T(8,128)(2,1)S(1)}, bf16[128,512]{1,0:T(8,128)(2,1)S(1)}, u32[]{:S(2)}, u32[]{:S(2)}) %collective-permute-start.1) | collective-permute-done | bytes 131104 | tf_op jit(solution)/shard_map/ppermute | solution.py:246
  14.2 0.0 collective-permute-done.refs_1_
  14.2 31.5 %shard_map.61 = f32[8,136,512]{2,1,0:T(8,128)S(1)} custom-call(bf16[128,512]{1,0:T(8,128)(2,1)S(1)} %bitcast.19, bf16[128,512]{1,0:T(8,128)(2,1)S(1)} %collective-permute-done.refs_1_, bf16[128,512]{1,0:T(8,128)(2,1)S(1)} %collective-permute-done.1.refs_2_, bf16[128,512]{1,0:T(8,128)(2,1)S(1)} %collective-permute-done.2.refs_3_, ...), custom_call_target="tpu_custom_call" | custom-call | flops 25769803776 | bytes 25165824 | tf_op jit(solution)/shard_map/pallas_call | solution.py:138
  45.7 1.3 %convert_element_type.16 = f16[8,136,512]{2,1,0:T(8,128)(2,1)} convert(f32[8,136,512]{2,1,0:T(8,128)S(1)} %shard_map.61) | non-fusion elementwise | flops 557056 | bytes 3342336 | tf_op jit(solution)/shard_map/convert_element_type | solution.py:267
  47.0 4.9 %all-to-all-start = ((f16[8,136,512]{2,1,0:T(8,128)(2,1)}), f16[8,136,512]{2,1,0:T(8,128)(2,1)}, u32[]{:S(2)}, u32[]{:S(2)}) async-start(f16[8,136,512]{2,1,0:T(8,128)(2,1)} %convert_element_type.16), calls=%async_computation | async-start | bytes 2228224 | tf_op jit(solution)/shard_map/all_to_all | solution.py:268
  51.8 0.0 collective-permute-done.5.refs_6_
  51.8 0.0 collective-permute-done.4.refs_5_
  51.8 43.1 %shard_map.60 = bf16[24,512,1024]{2,1,0:T(8,128)(2,1)} custom-call(bf16[128,512]{1,0:T(8,128)(2,1)S(1)} %bitcast.20, bf16[128,512]{1,0:T(8,128)(2,1)S(1)} %collective-permute-done.refs_1_, bf16[128,512]{1,0:T(8,128)(2,1)S(1)} %collective-permute-done.1.refs_2_, bf16[128,512]{1,0:T(8,128)(2,1)S(1)} %collective-permute-done.2.refs_3_, ...), custom_call_target="tpu_custom_call" | custom-call | flops 19327352832 | bytes 25165824 | tf_op jit(solution)/shard_map/pallas_call | solution.py:226
  95.0 0.0 all-to-all-done
  95.0 0.9 fusion.2
  95.9 1.4 %multiply_reduce_fusion = bf16[128,512]{1,0:T(8,128)(2,1)S(1)} fusion(f16[8,136,512]{2,1,0:T(8,128)(2,1)} %all-to-all-done, f32[8,512]{1,0:T(8,128)S(1)} %bitcast.25), kind=kLoop, calls=%fused_computation | loop fusion | flops 1507328 | bytes 1196032 | tf_op jit(solution)/shard_map/reduce_sum | solution.py:271
  97.3 0.7 convert_element_type.20
  (5 shorter events, 0.0 us)
Async XLA Ops:
  1.6 7.1 %collective-permute-start.3 = (bf16[128,512]{1,0:T(8,128)(2,1)S(1)}, bf16[128,512]{1,0:T(8,128)(2,1)S(1)}, u32[]{:S(2)}, u32[]{:S(2)}) collective-permute-start(bf16[128,512]{1,0:T(8,128)(2,1)S(1)} %bitcast.21), channel_id=1, source_target_pairs={{0,1},{1,0},{2,3},{3,2},{4,5},{5,4},{6,7},{7,6},{8,9},{9,8},{10,11... | collective-permute-start | bytes 393224 | tf_op jit(solution)/shard_map/ppermute | solution.py:246
  5.5 6.8 %collective-permute-start.2 = (bf16[128,512]{1,0:T(8,128)(2,1)S(1)}, bf16[128,512]{1,0:T(8,128)(2,1)S(1)}, u32[]{:S(2)}, u32[]{:S(2)}) collective-permute-start(bf16[128,512]{1,0:T(8,128)(2,1)S(1)} %bitcast.16), channel_id=1, source_target_pairs={{0,24},{8,16},{16,8},{24,0},{1,25},{9,17},{17,9},{25,1},{2,26},{10... | collective-permute-start | bytes 393224 | tf_op jit(solution)/shard_map/ppermute | solution.py:246
  6.2 8.0 %collective-permute-start.1 = (bf16[128,512]{1,0:T(8,128)(2,1)S(1)}, bf16[128,512]{1,0:T(8,128)(2,1)S(1)}, u32[]{:S(2)}, u32[]{:S(2)}) collective-permute-start(bf16[128,512]{1,0:T(8,128)(2,1)S(1)} %bitcast.17), channel_id=1, source_target_pairs={{0,16},{8,24},{16,0},{24,8},{1,17},{9,25},{17,1},{25,9},{2,18},{10... | collective-permute-start | bytes 393224 | tf_op jit(solution)/shard_map/ppermute | solution.py:246
  7.2 7.0 %collective-permute-start = (bf16[128,512]{1,0:T(8,128)(2,1)S(1)}, bf16[128,512]{1,0:T(8,128)(2,1)S(1)}, u32[]{:S(2)}, u32[]{:S(2)}) collective-permute-start(bf16[128,512]{1,0:T(8,128)(2,1)S(1)} %bitcast.18), channel_id=1, source_target_pairs={{0,8},{8,0},{16,24},{24,16},{1,9},{9,1},{17,25},{25,17},{2,10},{10... | collective-permute-start | bytes 393224 | tf_op jit(solution)/shard_map/ppermute | solution.py:246
  7.4 0.7 copy-start
  8.7 43.2 %collective-permute-start.6 = (bf16[2,128,512]{2,1,0:T(8,128)(2,1)S(1)}, bf16[2,128,512]{2,1,0:T(8,128)(2,1)S(1)}, u32[]{:S(2)}, u32[]{:S(2)}) collective-permute-start(bf16[2,128,512]{2,1,0:T(8,128)(2,1)S(1)} %bitcast.12), channel_id=1, source_target_pairs={{0,6},{1,7},{2,4},{3,5},{4,2},{5,3},{6,0},{7,1},{8,14},{9,15},{10,... | collective-permute-start | bytes 786440 | tf_op jit(solution)/shard_map/ppermute | solution.py:246
  12.3 39.5 %collective-permute-start.5 = (bf16[2,128,512]{2,1,0:T(8,128)(2,1)S(1)}, bf16[2,128,512]{2,1,0:T(8,128)(2,1)S(1)}, u32[]{:S(2)}, u32[]{:S(2)}) collective-permute-start(bf16[2,128,512]{2,1,0:T(8,128)(2,1)S(1)} %bitcast.13), channel_id=1, source_target_pairs={{0,4},{1,5},{2,6},{3,7},{4,0},{5,1},{6,2},{7,3},{8,12},{9,13},{10,... | collective-permute-start | bytes 786440 | tf_op jit(solution)/shard_map/ppermute | solution.py:246
  12.3 39.5 %collective-permute-start.4 = (bf16[2,128,512]{2,1,0:T(8,128)(2,1)S(1)}, bf16[2,128,512]{2,1,0:T(8,128)(2,1)S(1)}, u32[]{:S(2)}, u32[]{:S(2)}) collective-permute-start(bf16[2,128,512]{2,1,0:T(8,128)(2,1)S(1)} %bitcast.14), channel_id=1, source_target_pairs={{0,2},{1,3},{2,0},{3,1},{4,6},{5,7},{6,4},{7,5},{8,10},{9,11},{10,... | collective-permute-start | bytes 786440 | tf_op jit(solution)/shard_map/ppermute | solution.py:246
  47.0 48.0 %all-to-all-start = ((f16[8,136,512]{2,1,0:T(8,128)(2,1)}), f16[8,136,512]{2,1,0:T(8,128)(2,1)}, u32[]{:S(2)}, u32[]{:S(2)}) async-start(f16[8,136,512]{2,1,0:T(8,128)(2,1)} %convert_element_type.16), calls=%async_computation | async-start | bytes 2228224 | tf_op jit(solution)/shard_map/all_to_all | solution.py:268

commit v5 on v4

--- a/solution.py
+++ b/solution.py
@@ -12,7 +12,8 @@
 F32 = jnp.float32
 F8 = jnp.float8_e4m3fn
 MIB = 1024 * 1024
-TINY = 1e-30
+TINY = 1e-18
+RANGE = 2.0**24
 
 
 def split(wide):
@@ -51,28 +52,35 @@
 def reach_of(table, gmax):
     length = table.shape[1]
     sums = [jnp.sum(jnp.abs(table[k, 0:1, :length].astype(F32)), keepdims=True) for k in range(2)]
-    return [jnp.maximum(total * gmax, TINY) for total in sums]
-
-
-def table_kernel(filters_ref, rows_ref):
+    return [jnp.maximum(total, TINY) * jnp.maximum(gmax, TINY) for total in sums]
+
+
+def table_kernel(filters_ref, rows_ref, columns_ref):
     count, length = filters_ref.shape
     source = lax.broadcasted_iota(jnp.int32, (length, length), 0)
     token = lax.broadcasted_iota(jnp.int32, (length, length), 1)
     for k in range(count):
         spread = jnp.broadcast_to(filters_ref[k : k + 1, :], (length, length))
         shifted = pltpu.roll(spread, 0, 1, stride=1, stride_axis=0)
-        high, low = split(jnp.where(token >= source, shifted, 0.0))
+        upper = jnp.where(token >= source, shifted, 0.0)
+        high, low = split(upper)
         rows_ref[k, :, :length] = high
         rows_ref[k, :, length:] = low.astype(BF16)
+        high, low = split(upper.T)
+        columns_ref[k // 2, :length, k % 2 * length : (k % 2 + 1) * length] = high
+        columns_ref[k // 2, length:, k % 2 * length : (k % 2 + 1) * length] = low.astype(BF16)
 
 
 def make_tables(filters):
     count, length = filters.shape
     return call(
         table_kernel,
-        (count * length * length * 4, count * length * length * 4),
-        8,
-        out_shape=jax.ShapeDtypeStruct((count, length, 2 * length), BF16),
+        (count * length * length * 4, count * length * length * 8),
+        16,
+        out_shape=(
+            jax.ShapeDtypeStruct((count, length, 2 * length), BF16),
+            jax.ShapeDtypeStruct((count // 2, 2 * length, 2 * length), BF16),
+        ),
     )(filters)
 
 
@@ -100,21 +108,21 @@
 
     matrix = matrix_ref[...].reshape(2 * out_width, -1)
     peak = jnp.max(jnp.abs(matrix).reshape(-1, 16, matrix.shape[1]), axis=0)
-    matrix_scale = (256.0 / jnp.maximum(largest(peak), TINY)).astype(BF16)
+    peak = jnp.maximum(largest(peak), TINY)
+    matrix_scale = (256.0 / peak).astype(BF16)
     matrix8 = (matrix * matrix_scale).astype(F8)
     table = rows_ref[pl.ds(2 * step, 2)]
     reach = reach_of(table, bounds[0:1, 0:1])
-    reach = jnp.maximum(reach[0], reach[1])
+    reach = jnp.maximum(reach[0], reach[1]) * peak
     table = table.reshape(2 * length, 2 * length)
     for b in range(seqs):
-        high, low = split(dot(table, grads[:, b * out_width : (b + 1) * out_width]))
-        low = (low * (65536.0 / reach)).astype(F8)
+        high, low = split(dot(table, grads[:, b * out_width : (b + 1) * out_width]) * (RANGE / reach))
+        low = (low / matrix_scale.astype(F32)).astype(F8)
         for k in range(2):
             source, columns = slice(k * length, (k + 1) * length), slice(k * out_width, (k + 1) * out_width)
             parts[b * length : (b + 1) * length, columns] = high[source]
             parts8[b * length : (b + 1) * length, columns] = low[source]
-    back = (reach / 65536.0) / matrix_scale.astype(F32)
-    total[...] += dot(parts[...], matrix) + dot(parts8[...], matrix8) * back
+    total[...] += (dot(parts[...], matrix) + dot(parts8[...], matrix8)) * (reach / RANGE)
 
     @pl.when(step == pl.num_programs(0) - 1)
     def _():
@@ -157,7 +165,7 @@
 def matrix_kernel(cin_count, input_count, cout_count, *refs):
     pieces = refs[:cin_count]
     input_pieces = refs[cin_count : cin_count + input_count]
-    rows_ref, out_ref, grads, inputs, inputs8, parts, parts8, bounds = refs[cin_count + input_count :]
+    rows_ref, columns_ref, out_ref, grads, inputs, inputs8, parts, parts8, bounds = refs[cin_count + input_count :]
     step = pl.program_id(0)
     _, length, _ = rows_ref.shape
     tokens = inputs.shape[0]
@@ -186,39 +194,22 @@
                 inputs[:, columns] = turned.astype(BF16)
                 inputs8[:, columns] = (turned * (256.0 / xmax)).astype(F8)
 
-    def pair(p, _):
-        table = rows_ref[pl.ds(4 * step + 2 * p, 2)]
-        reach = reach_of(table, bounds[0:1, 0:1])
-        table = table.reshape(2 * length, 2 * length)
+    xmax = bounds[1:2, 0:1]
+    reach = [bound * xmax for bound in reach_of(rows_ref[pl.ds(2 * step, 2)], bounds[0:1, 0:1])]
+    table = columns_ref[step]
+    for b in range(seqs):
+        place = slice(b * length, (b + 1) * length)
+        filtered = dot(grads[b * out_width : (b + 1) * out_width], table)
         for k in range(2):
-            back = (reach[k] / 65536.0) * (bounds[1:2, 0:1] / 256.0)
-            bounds[2 + k : 3 + k, :] = jnp.broadcast_to(back, (1, length))
-
-        def sequence(b, _):
-            place = pl.ds(pl.multiple_of(b * length, length), length)
-            source = grads[pl.ds(pl.multiple_of(b * out_width, out_width), out_width)]
-            filtered = lax.dot_general(source, table, (((1,), (1,)), ((), ())), preferred_element_type=F32)
-            high, low = split(filtered)
-            for k in range(2):
-                columns = slice(k * length, (k + 1) * length)
-                parts[k, :, place] = high[:, columns]
-                parts8[k, :, place] = (low[:, columns] * (65536.0 / reach[k])).astype(F8)
-            return _
-
-        lax.fori_loop(0, seqs, sequence, 0)
-
-        def product(k, _):
-            back = bounds[pl.ds(2 + k, 1), 0:1]
-            total = dot(parts[k], inputs[...]) + dot(parts8[k], inputs8[...]) * back
-            out_ref[2 * p + k] = total.astype(BF16)
-            return _
-
-        return lax.fori_loop(0, 2, product, 0)
-
-    lax.fori_loop(0, 2, pair, 0)
-
-
-def matrix_sums(pieces, input_pieces, rows, cout_count, shape):
+            high, low = split(filtered[:, k * length : (k + 1) * length] * (RANGE / reach[k]))
+            parts[k, :, place] = high
+            parts8[k, :, place] = (low * (xmax / 256.0)).astype(F8)
+    for k in range(2):
+        total = dot(parts[k], inputs[...]) + dot(parts8[k], inputs8[...])
+        out_ref[k] = (total * (reach[k] / RANGE)).astype(BF16)
+
+
+def matrix_sums(pieces, input_pieces, rows, columns, cout_count, shape):
     count, out_width, in_width = shape
     length = rows.shape[1]
     tokens = pieces[0].shape[1]
@@ -228,9 +219,9 @@
         (3 * count * out_width * in_width * tokens, 2 * count * out_width * in_width),
         32,
         out_shape=jax.ShapeDtypeStruct(shape, BF16),
-        grid=(count // 4,),
-        in_specs=[whole(piece) for piece in (*pieces, *input_pieces)] + [whole(rows)],
-        out_specs=pl.BlockSpec((4, out_width, in_width), lambda i: (i, 0, 0)),
+        grid=(count // 2,),
+        in_specs=[whole(piece) for piece in (*pieces, *input_pieces)] + [whole(rows), whole(columns)],
+        out_specs=pl.BlockSpec((2, out_width, in_width), lambda i: (i, 0, 0)),
         scratch_shapes=[
             pltpu.VMEM((seqs * out_width, 2 * length), BF16),
             pltpu.VMEM((tokens, in_width), BF16),
@@ -239,7 +230,7 @@
             pltpu.VMEM((2, out_width, tokens), F8),
             pltpu.VMEM((8, length), F32),
         ],
-    )(*pieces, *input_pieces, rows)
+    )(*pieces, *input_pieces, rows, columns)
 
 
 def exchange(array, axis, count, flip):
@@ -254,7 +245,7 @@
         pieces = [lax.all_gather(flat_grads, "cin", axis=0, tiled=True)]
     else:
         pieces = [flat_grads] + [exchange(flat_grads, "cin", cin, flip) for flip in range(1, cin)]
-    rows = make_tables(lax.optimization_barrier((filters, flat_grads))[0])
+    rows, columns = make_tables(lax.optimization_barrier((filters, flat_grads))[0])
     flat_inputs = inputs.reshape(-1, tokens)
     if cout < 2 or cout & (cout - 1) or own % 128:
         input_pieces = [lax.all_gather(flat_inputs, "cout", axis=0, tiled=True)[None]]
@@ -266,7 +257,7 @@
 
     blocks = back_sums(pieces, rows, matrices, cout).astype(F16)
     came = lax.all_to_all(blocks, "cout", 0, 0, tiled=True)
-    matrix_grads = matrix_sums(pieces, input_pieces, rows, cout_count, matrices.shape)
+    matrix_grads = matrix_sums(pieces, input_pieces, rows, columns, cout_count, matrices.shape)
     scales = jnp.exp2(came[:, own : own + 1].astype(F32) - 14.0)
     input_grads = jnp.sum(came[:, :own].astype(F32) * scales, axis=0).astype(BF16)
     return (matrix_grads, input_grads.reshape(own, seq_count, length))

time: 98.4 us -> 90.4 us (0.919)
  Pallas kernels: 75.1 us -> 65.1 us
  local copies, waits for them, and re-layouts: 3.25 us -> 5.97 us
    pallas_call x1, Pallas kernels: 43.1 us -> 31.4 us  [matrix_sums(): call(functools.partial(matrix_kernel, len(pieces), len(input_pieces), cou...]
    unnamed x5 -> x17, local copies, waits for them, and re-layouts: 2.56 us -> 5.28 us
    pallas_call x1, Pallas kernels: 31.5 us -> 32.8 us  [back_sums(): call(functools.partial(back_kernel, len(pieces)), (4 * count * out_width...]
  transfers between devices with their start and end apart: 8 -> 8, of which waited for: 1 -> 1; matrix products, arithmetic and copies ran while one was open for 2% -> 2% of each run, Pallas kernels for 77% -> 72%
where the time goes in v5:
time: 90.4 us; the launch traced here: 90 us
  Pallas kernels  65.1 us (72%)
  starting transfers between devices  14.3 us (16%)
  local copies, waits for them, and re-layouts  5.97 us (7%)
  other arithmetic  3.59 us (4%)
    pallas_call x1, Pallas kernels, back_sums(): call(functools.partial(back_kernel, len(pieces)), (4 * count * out_width...  32.8 us
    pallas_call x1, Pallas kernels, matrix_sums(): call(functools.partial(matrix_kernel, len(pieces), len(input_pieces), cou...  31.4 us
    ppermute x7, starting transfers between devices, exchange(): return lax.ppermute(array, axis, [(i, i ^ flip) for i in range(count)])  9.42 us
    unnamed x17, local copies, waits for them, and re-layouts  5.28 us
    all_to_all x1, starting transfers between devices, shards(): came = lax.all_to_all(blocks, 'cout', 0, 0, tiled=True)  4.88 us
  transfers between devices with their start and end apart: 8, of which 1 were waited for; matrix products, arithmetic and copies ran while one was open for 2% of the time, Pallas kernels for 72%

profile of v5, /device:TPU:0, one launch (start us, length us, event | category | flops | bytes accessed | tf_op | source)
XLA Modules:
  0.0 90.0 jit_solution(10294812447529004734)
XLA Ops:
  0.6 0.9 %copy.12 = bf16[16,8,4,128]{3,1,2,0:T(8,128)(2,1)S(1)} copy(bf16[16,8,4,128]{3,2,1,0:T(4,128)(2,1)} %bitcast.23) | data formatting | bytes 262144
  1.6 3.0 %collective-permute-start.3 = (bf16[128,512]{1,0:T(8,128)(2,1)S(1)}, bf16[128,512]{1,0:T(8,128)(2,1)S(1)}, u32[]{:S(2)}, u32[]{:S(2)}) collective-permute-start(bf16[128,512]{1,0:T(8,128)(2,1)S(1)} %bitcast.21), channel_id=1, source_target_pairs={{0,1},{1,0},{2,3},{3,2},{4,5},{5,4},{6,7},{7,6},{8,9},{9,8},{10,11... | collective-permute-start | bytes 393224 | tf_op jit(solution)/shard_map/ppermute | solution.py:237
  4.6 0.9 %copy.13 = bf16[16,8,4,128]{3,1,2,0:T(8,128)(2,1)S(1)} copy(bf16[16,8,4,128]{3,2,1,0:T(4,128)(2,1)} %bitcast.24) | data formatting | bytes 262144
  5.5 0.1 collective-permute-start
  5.6 1.6 %collective-permute-start.1 = (bf16[128,512]{1,0:T(8,128)(2,1)S(1)}, bf16[128,512]{1,0:T(8,128)(2,1)S(1)}, u32[]{:S(2)}, u32[]{:S(2)}) collective-permute-start(bf16[128,512]{1,0:T(8,128)(2,1)S(1)} %bitcast.17), channel_id=1, source_target_pairs={{0,16},{8,24},{16,0},{24,8},{1,17},{9,25},{17,1},{25,9},{2,18},{10... | collective-permute-start | bytes 393224 | tf_op jit(solution)/shard_map/ppermute | solution.py:237
  7.2 0.3 collective-permute-start.2
  7.5 0.7 copy-done
  8.2 0.9 shard_map.59
  9.1 1.6 %collective-permute-start.4 = (bf16[2,128,512]{2,1,0:T(8,128)(2,1)S(1)}, bf16[2,128,512]{2,1,0:T(8,128)(2,1)}, u32[]{:S(2)}, u32[]{:S(2)}) collective-permute-start(bf16[2,128,512]{2,1,0:T(8,128)(2,1)S(1)} %bitcast.12), channel_id=1, source_target_pairs={{0,2},{1,3},{2,0},{3,1},{4,6},{5,7},{6,4},{7,5},{8,10},{9,11},{10,... | collective-permute-start | bytes 786440 | tf_op jit(solution)/shard_map/ppermute | solution.py:237
  10.7 2.6 %collective-permute-start.5 = (bf16[2,128,512]{2,1,0:T(8,128)(2,1)S(1)}, bf16[2,128,512]{2,1,0:T(8,128)(2,1)}, u32[]{:S(2)}, u32[]{:S(2)}) collective-permute-start(bf16[2,128,512]{2,1,0:T(8,128)(2,1)S(1)} %bitcast.13), channel_id=1, source_target_pairs={{0,4},{1,5},{2,6},{3,7},{4,0},{5,1},{6,2},{7,3},{8,12},{9,13},{10,... | collective-permute-start | bytes 786440 | tf_op jit(solution)/shard_map/ppermute | solution.py:237
  13.3 0.0 collective-permute-done.refs_1_
  13.3 0.2 collective-permute-start.6
  13.6 0.3 collective-permute-done.2.refs_3_
  13.9 32.8 %shard_map.61 = f32[8,136,512]{2,1,0:T(8,128)S(1)} custom-call(bf16[128,512]{1,0:T(8,128)(2,1)S(1)} %bitcast.19, bf16[128,512]{1,0:T(8,128)(2,1)S(1)} %collective-permute-done.refs_1_, bf16[128,512]{1,0:T(8,128)(2,1)S(1)} %collective-permute-done.1.refs_2_, bf16[128,512]{1,0:T(8,128)(2,1)S(1)} %collective-permute-done.2.refs_3_, ...), custom_call_target="tpu_custom_call" | custom-call | flops 25769803776 | bytes 25165824 | tf_op jit(solution)/shard_map/pallas_call | solution.py:146
  46.7 1.3 %convert_element_type.16 = f16[8,136,512]{2,1,0:T(8,128)(2,1)} convert(f32[8,136,512]{2,1,0:T(8,128)S(1)} %shard_map.61) | non-fusion elementwise | flops 557056 | bytes 3342336 | tf_op jit(solution)/shard_map/convert_element_type | solution.py:258
  48.0 4.9 %all-to-all-start = ((f16[8,136,512]{2,1,0:T(8,128)(2,1)}), f16[8,136,512]{2,1,0:T(8,128)(2,1)}, u32[]{:S(2)}, u32[]{:S(2)}) async-start(f16[8,136,512]{2,1,0:T(8,128)(2,1)} %convert_element_type.16), calls=%async_computation | async-start | bytes 2228224 | tf_op jit(solution)/shard_map/all_to_all | solution.py:259
  52.9 0.0 copy-start.2
  52.9 0.9 copy-done.2
  53.8 0.9 %copy-done.4 = bf16[128,512]{1,0:T(8,128)(2,1)S(1)} copy-done((bf16[128,512]{1,0:T(8,128)(2,1)S(1)}, bf16[128,512]{1,0:T(8,128)(2,1)}, u32[]{:S(2)}) %copy-start.4) | copy-done | bytes 131096
  54.7 0.9 %copy-done.6 = bf16[128,512]{1,0:T(8,128)(2,1)S(1)} copy-done((bf16[128,512]{1,0:T(8,128)(2,1)S(1)}, bf16[128,512]{1,0:T(8,128)(2,1)}, u32[]{:S(2)}) %copy-start.6) | copy-done | bytes 131096
  55.6 31.4 %shard_map.60 = bf16[24,512,1024]{2,1,0:T(8,128)(2,1)} custom-call(bf16[128,512]{1,0:T(8,128)(2,1)S(1)} %bitcast.20, bf16[128,512]{1,0:T(8,128)(2,1)S(1)} %copy-done.2, bf16[128,512]{1,0:T(8,128)(2,1)S(1)} %copy-done.4, bf16[128,512]{1,0:T(8,128)(2,1)S(1)} %copy-done.6, bf16[2,128,512]{2,1,0:T(8,128)(2,1)S(1)} %bitcast.15, ...), custom_call_target="tpu_custom_call" | custom-call | flops 19327352832 | bytes 25165824 | tf_op jit(solution)/shard_map/pallas_call | solution.py:217
  87.0 0.9 fusion.2
  87.8 1.4 %multiply_reduce_fusion = bf16[128,512]{1,0:T(8,128)(2,1)S(1)} fusion(f16[8,136,512]{2,1,0:T(8,128)(2,1)} %all-to-all-done, f32[8,512]{1,0:T(8,128)S(1)} %bitcast.25), kind=kLoop, calls=%fused_computation | loop fusion | flops 1507328 | bytes 1196032 | tf_op jit(solution)/shard_map/reduce_sum | solution.py:262
  89.3 0.7 convert_element_type.20
  (17 shorter events, 0.1 us)
Async XLA Ops:
  1.6 7.5 %collective-permute-start.3 = (bf16[128,512]{1,0:T(8,128)(2,1)S(1)}, bf16[128,512]{1,0:T(8,128)(2,1)S(1)}, u32[]{:S(2)}, u32[]{:S(2)}) collective-permute-start(bf16[128,512]{1,0:T(8,128)(2,1)S(1)} %bitcast.21), channel_id=1, source_target_pairs={{0,1},{1,0},{2,3},{3,2},{4,5},{5,4},{6,7},{7,6},{8,9},{9,8},{10,11... | collective-permute-start | bytes 393224 | tf_op jit(solution)/shard_map/ppermute | solution.py:237
  5.5 7.8 %collective-permute-start = (bf16[128,512]{1,0:T(8,128)(2,1)S(1)}, bf16[128,512]{1,0:T(8,128)(2,1)S(1)}, u32[]{:S(2)}, u32[]{:S(2)}) collective-permute-start(bf16[128,512]{1,0:T(8,128)(2,1)S(1)} %bitcast.16), channel_id=1, source_target_pairs={{0,8},{8,0},{16,24},{24,16},{1,9},{9,1},{17,25},{25,17},{2,10},{10... | collective-permute-start | bytes 393224 | tf_op jit(solution)/shard_map/ppermute | solution.py:237
  5.6 8.0 %collective-permute-start.1 = (bf16[128,512]{1,0:T(8,128)(2,1)S(1)}, bf16[128,512]{1,0:T(8,128)(2,1)S(1)}, u32[]{:S(2)}, u32[]{:S(2)}) collective-permute-start(bf16[128,512]{1,0:T(8,128)(2,1)S(1)} %bitcast.17), channel_id=1, source_target_pairs={{0,16},{8,24},{16,0},{24,8},{1,17},{9,25},{17,1},{25,9},{2,18},{10... | collective-permute-start | bytes 393224 | tf_op jit(solution)/shard_map/ppermute | solution.py:237
  7.2 6.7 %collective-permute-start.2 = (bf16[128,512]{1,0:T(8,128)(2,1)S(1)}, bf16[128,512]{1,0:T(8,128)(2,1)S(1)}, u32[]{:S(2)}, u32[]{:S(2)}) collective-permute-start(bf16[128,512]{1,0:T(8,128)(2,1)S(1)} %bitcast.18), channel_id=1, source_target_pairs={{0,24},{8,16},{16,8},{24,0},{1,25},{9,17},{17,9},{25,1},{2,26},{10... | collective-permute-start | bytes 393224 | tf_op jit(solution)/shard_map/ppermute | solution.py:237
  7.5 0.7 copy-start
  9.1 43.8 %collective-permute-start.4 = (bf16[2,128,512]{2,1,0:T(8,128)(2,1)S(1)}, bf16[2,128,512]{2,1,0:T(8,128)(2,1)}, u32[]{:S(2)}, u32[]{:S(2)}) collective-permute-start(bf16[2,128,512]{2,1,0:T(8,128)(2,1)S(1)} %bitcast.12), channel_id=1, source_target_pairs={{0,2},{1,3},{2,0},{3,1},{4,6},{5,7},{6,4},{7,5},{8,10},{9,11},{10,... | collective-permute-start | bytes 786440 | tf_op jit(solution)/shard_map/ppermute | solution.py:237
  10.7 42.1 %collective-permute-start.5 = (bf16[2,128,512]{2,1,0:T(8,128)(2,1)S(1)}, bf16[2,128,512]{2,1,0:T(8,128)(2,1)}, u32[]{:S(2)}, u32[]{:S(2)}) collective-permute-start(bf16[2,128,512]{2,1,0:T(8,128)(2,1)S(1)} %bitcast.13), channel_id=1, source_target_pairs={{0,4},{1,5},{2,6},{3,7},{4,0},{5,1},{6,2},{7,3},{8,12},{9,13},{10,... | collective-permute-start | bytes 786440 | tf_op jit(solution)/shard_map/ppermute | solution.py:237
  13.3 33.3 %copy-start.1 = (bf16[128,512]{1,0:T(8,128)(2,1)}, bf16[128,512]{1,0:T(8,128)(2,1)S(1)}, u32[]{:S(2)}) copy-start(bf16[128,512]{1,0:T(8,128)(2,1)S(1)} %collective-permute-done.refs_1_) | copy-start | bytes 393220
  13.3 39.5 %collective-permute-start.6 = (bf16[2,128,512]{2,1,0:T(8,128)(2,1)S(1)}, bf16[2,128,512]{2,1,0:T(8,128)(2,1)}, u32[]{:S(2)}, u32[]{:S(2)}) collective-permute-start(bf16[2,128,512]{2,1,0:T(8,128)(2,1)S(1)} %bitcast.14), channel_id=1, source_target_pairs={{0,6},{1,7},{2,4},{3,5},{4,2},{5,3},{6,0},{7,1},{8,14},{9,15},{10,... | collective-permute-start | bytes 786440 | tf_op jit(solution)/shard_map/ppermute | solution.py:237
  13.6 33.1 %copy-start.3 = (bf16[128,512]{1,0:T(8,128)(2,1)}, bf16[128,512]{1,0:T(8,128)(2,1)S(1)}, u32[]{:S(2)}) copy-start(bf16[128,512]{1,0:T(8,128)(2,1)S(1)} %collective-permute-done.1.refs_2_) | copy-start | bytes 393220
  13.9 32.8 %copy-start.5 = (bf16[128,512]{1,0:T(8,128)(2,1)}, bf16[128,512]{1,0:T(8,128)(2,1)S(1)}, u32[]{:S(2)}) copy-start(bf16[128,512]{1,0:T(8,128)(2,1)S(1)} %collective-permute-done.2.refs_3_) | copy-start | bytes 393220
  48.0 39.0 %all-to-all-start = ((f16[8,136,512]{2,1,0:T(8,128)(2,1)}), f16[8,136,512]{2,1,0:T(8,128)(2,1)}, u32[]{:S(2)}, u32[]{:S(2)}) async-start(f16[8,136,512]{2,1,0:T(8,128)(2,1)} %convert_element_type.16), calls=%async_computation | async-start | bytes 2228224 | tf_op jit(solution)/shard_map/all_to_all | solution.py:259
  52.9 0.9 %copy-start.2 = (bf16[128,512]{1,0:T(8,128)(2,1)S(1)}, bf16[128,512]{1,0:T(8,128)(2,1)}, u32[]{:S(2)}) copy-start(bf16[128,512]{1,0:T(8,128)(2,1)} %copy-done.1) | copy-start | bytes 393220
  53.8 0.9 %copy-start.4 = (bf16[128,512]{1,0:T(8,128)(2,1)S(1)}, bf16[128,512]{1,0:T(8,128)(2,1)}, u32[]{:S(2)}) copy-start(bf16[128,512]{1,0:T(8,128)(2,1)} %copy-done.3) | copy-start | bytes 393220
  54.7 0.9 %copy-start.6 = (bf16[128,512]{1,0:T(8,128)(2,1)S(1)}, bf16[128,512]{1,0:T(8,128)(2,1)}, u32[]{:S(2)}) copy-start(bf16[128,512]{1,0:T(8,128)(2,1)} %copy-done.5) | copy-start | bytes 393220

commit v6 on v4

--- a/solution.py
+++ b/solution.py
@@ -12,6 +12,7 @@
 F32 = jnp.float32
 F8 = jnp.float8_e4m3fn
 MIB = 1024 * 1024
+GROUP = 4
 TINY = 1e-30
 
 
@@ -50,7 +51,7 @@
 
 def reach_of(table, gmax):
     length = table.shape[1]
-    sums = [jnp.sum(jnp.abs(table[k, 0:1, :length].astype(F32)), keepdims=True) for k in range(2)]
+    sums = [jnp.sum(jnp.abs(table[k, 0:1, :length].astype(F32)), keepdims=True) for k in range(table.shape[0])]
     return [jnp.maximum(total * gmax, TINY) for total in sums]
 
 
@@ -98,18 +99,17 @@
         gmax = functools.reduce(jnp.maximum, [largest(piece[...]) for piece in pieces])
         bounds[...] = jnp.broadcast_to(gmax, bounds.shape)
 
-    matrix = matrix_ref[...].reshape(2 * out_width, -1)
+    matrix = matrix_ref[...].reshape(GROUP * out_width, -1)
     peak = jnp.max(jnp.abs(matrix).reshape(-1, 16, matrix.shape[1]), axis=0)
     matrix_scale = (256.0 / jnp.maximum(largest(peak), TINY)).astype(BF16)
     matrix8 = (matrix * matrix_scale).astype(F8)
-    table = rows_ref[pl.ds(2 * step, 2)]
-    reach = reach_of(table, bounds[0:1, 0:1])
-    reach = jnp.maximum(reach[0], reach[1])
-    table = table.reshape(2 * length, 2 * length)
+    table = rows_ref[pl.ds(GROUP * step, GROUP)]
+    reach = functools.reduce(jnp.maximum, reach_of(table, bounds[0:1, 0:1]))
+    table = table.reshape(GROUP * length, 2 * length)
     for b in range(seqs):
         high, low = split(dot(table, grads[:, b * out_width : (b + 1) * out_width]))
         low = (low * (65536.0 / reach)).astype(F8)
-        for k in range(2):
+        for k in range(GROUP):
             source, columns = slice(k * length, (k + 1) * length), slice(k * out_width, (k + 1) * out_width)
             parts[b * length : (b + 1) * length, columns] = high[source]
             parts8[b * length : (b + 1) * length, columns] = low[source]
@@ -138,16 +138,16 @@
     return call(
         functools.partial(back_kernel, len(pieces)),
         (4 * count * out_width * in_width * tokens, 2 * matrices.size),
-        32,
+        40,
         out_shape=out,
-        grid=(count // 2,),
+        grid=(count // GROUP,),
         in_specs=[whole(piece) for piece in pieces]
-        + [whole(rows), pl.BlockSpec((2, out_width, in_width), lambda i: (i, 0, 0))],
+        + [whole(rows), pl.BlockSpec((GROUP, out_width, in_width), lambda i: (i, 0, 0))],
         out_specs=whole(out),
         scratch_shapes=[
             pltpu.VMEM((2 * length, seqs * out_width), BF16),
-            pltpu.VMEM((tokens, 2 * out_width), BF16),
-            pltpu.VMEM((tokens, 2 * out_width), F8),
+            pltpu.VMEM((tokens, GROUP * out_width), BF16),
+            pltpu.VMEM((tokens, GROUP * out_width), F8),
             pltpu.VMEM((tokens, in_width), F32),
             pltpu.VMEM((8, length), F32),
         ],
@@ -186,36 +186,25 @@
                 inputs[:, columns] = turned.astype(BF16)
                 inputs8[:, columns] = (turned * (256.0 / xmax)).astype(F8)
 
-    def pair(p, _):
-        table = rows_ref[pl.ds(4 * step + 2 * p, 2)]
-        reach = reach_of(table, bounds[0:1, 0:1])
-        table = table.reshape(2 * length, 2 * length)
-        for k in range(2):
-            back = (reach[k] / 65536.0) * (bounds[1:2, 0:1] / 256.0)
-            bounds[2 + k : 3 + k, :] = jnp.broadcast_to(back, (1, length))
-
-        def sequence(b, _):
-            place = pl.ds(pl.multiple_of(b * length, length), length)
-            source = grads[pl.ds(pl.multiple_of(b * out_width, out_width), out_width)]
-            filtered = lax.dot_general(source, table, (((1,), (1,)), ((), ())), preferred_element_type=F32)
+    table = rows_ref[pl.ds(GROUP * step, GROUP)]
+    reach = reach_of(table, bounds[0:1, 0:1])
+    table = table.reshape(GROUP * length, 2 * length)
+    for first in range(0, GROUP, 2):
+        some = table[first * length : (first + 2) * length]
+        for b in range(seqs):
+            place = slice(b * length, (b + 1) * length)
+            filtered = lax.dot_general(
+                grads[b * out_width : (b + 1) * out_width], some, (((1,), (1,)), ((), ())), preferred_element_type=F32
+            )
             high, low = split(filtered)
             for k in range(2):
                 columns = slice(k * length, (k + 1) * length)
-                parts[k, :, place] = high[:, columns]
-                parts8[k, :, place] = (low[:, columns] * (65536.0 / reach[k])).astype(F8)
-            return _
-
-        lax.fori_loop(0, seqs, sequence, 0)
-
-        def product(k, _):
-            back = bounds[pl.ds(2 + k, 1), 0:1]
-            total = dot(parts[k], inputs[...]) + dot(parts8[k], inputs8[...]) * back
-            out_ref[2 * p + k] = total.astype(BF16)
-            return _
-
-        return lax.fori_loop(0, 2, product, 0)
-
-    lax.fori_loop(0, 2, pair, 0)
+                parts[first + k, :, place] = high[:, columns]
+                parts8[first + k, :, place] = (low[:, columns] * (65536.0 / reach[first + k])).astype(F8)
+    for k in range(GROUP):
+        back = (reach[k] / 65536.0) * (bounds[1:2, 0:1] / 256.0)
+        product = dot(parts[k], inputs[...]) + dot(parts8[k], inputs8[...]) * back
+        out_ref[k] = product.astype(BF16)
 
 
 def matrix_sums(pieces, input_pieces, rows, cout_count, shape):
@@ -228,15 +217,15 @@
         (3 * count * out_width * in_width * tokens, 2 * count * out_width * in_width),
         32,
         out_shape=jax.ShapeDtypeStruct(shape, BF16),
-        grid=(count // 4,),
+        grid=(count // GROUP,),
         in_specs=[whole(piece) for piece in (*pieces, *input_pieces)] + [whole(rows)],
-        out_specs=pl.BlockSpec((4, out_width, in_width), lambda i: (i, 0, 0)),
+        out_specs=pl.BlockSpec((GROUP, out_width, in_width), lambda i: (i, 0, 0)),
         scratch_shapes=[
             pltpu.VMEM((seqs * out_width, 2 * length), BF16),
             pltpu.VMEM((tokens, in_width), BF16),
             pltpu.VMEM((tokens, in_width), F8),
-            pltpu.VMEM((2, out_width, tokens), BF16),
-            pltpu.VMEM((2, out_width, tokens), F8),
+            pltpu.VMEM((GROUP, out_width, tokens), BF16),
+            pltpu.VMEM((GROUP, out_width, tokens), F8),
             pltpu.VMEM((8, length), F32),
         ],
     )(*pieces, *input_pieces, rows)

time: 98.4 us -> 82.5 us (0.84)
  Pallas kernels: 75.1 us -> 59.3 us
    pallas_call x1, Pallas kernels: 43.1 us -> 28.9 us  [matrix_sums(): call(functools.partial(matrix_kernel, len(pieces), len(input_pieces), cou...]
    pallas_call x1, Pallas kernels: 31.5 us -> 29.9 us  [back_sums(): call(functools.partial(back_kernel, len(pieces)), (4 * count * out_width...]
  transfers between devices with their start and end apart: 8 -> 8, of which waited for: 1 -> 1; matrix products, arithmetic and copies ran while one was open for 2% -> 3% of each run, Pallas kernels for 77% -> 72%
where the time goes in v6:
time: 82.5 us; the launch traced here: 82.2 us
  Pallas kernels  59.3 us (72%)
  starting transfers between devices  14.3 us (17%)
  other arithmetic  3.61 us (4%)
  local copies, waits for them, and re-layouts  3.25 us (4%)
  waiting for transfers between devices  1.08 us (1%)
    pallas_call x1, Pallas kernels, back_sums(): call(functools.partial(back_kernel, len(pieces)), (4 * count * out_width...  29.9 us
    pallas_call x1, Pallas kernels, matrix_sums(): call(functools.partial(matrix_kernel, len(pieces), len(input_pieces), cou...  28.9 us
    ppermute x7, starting transfers between devices, exchange(): return lax.ppermute(array, axis, [(i, i ^ flip) for i in range(count)])  9.41 us
    all_to_all x1, starting transfers between devices, shards(): came = lax.all_to_all(blocks, 'cout', 0, 0, tiled=True)  4.87 us
    unnamed x5, local copies, waits for them, and re-layouts  2.56 us
  transfers between devices with their start and end apart: 8, of which 1 were waited for; matrix products, arithmetic and copies ran while one was open for 3% of the time, Pallas kernels for 72%

profile of v6, /device:TPU:0, one launch (start us, length us, event | category | flops | bytes accessed | tf_op | source)
XLA Modules:
  0.0 82.2 jit_solution(382165185824943890)
XLA Ops:
  0.6 0.9 %copy.12 = bf16[16,8,4,128]{3,1,2,0:T(8,128)(2,1)S(1)} copy(bf16[16,8,4,128]{3,2,1,0:T(4,128)(2,1)} %bitcast.23) | data formatting | bytes 262144
  1.6 3.0 %collective-permute-start.3 = (bf16[128,512]{1,0:T(8,128)(2,1)S(1)}, bf16[128,512]{1,0:T(8,128)(2,1)S(1)}, u32[]{:S(2)}, u32[]{:S(2)}) collective-permute-start(bf16[128,512]{1,0:T(8,128)(2,1)S(1)} %bitcast.21), channel_id=1, source_target_pairs={{0,1},{1,0},{2,3},{3,2},{4,5},{5,4},{6,7},{7,6},{8,9},{9,8},{10,11... | collective-permute-start | bytes 393224 | tf_op jit(solution)/shard_map/ppermute | solution.py:235
  4.6 0.9 %copy.13 = bf16[16,8,4,128]{3,1,2,0:T(8,128)(2,1)S(1)} copy(bf16[16,8,4,128]{3,2,1,0:T(4,128)(2,1)} %bitcast.24) | data formatting | bytes 262144
  5.5 0.7 collective-permute-start.2
  6.2 0.9 %collective-permute-start.1 = (bf16[128,512]{1,0:T(8,128)(2,1)S(1)}, bf16[128,512]{1,0:T(8,128)(2,1)S(1)}, u32[]{:S(2)}, u32[]{:S(2)}) collective-permute-start(bf16[128,512]{1,0:T(8,128)(2,1)S(1)} %bitcast.17), channel_id=1, source_target_pairs={{0,16},{8,24},{16,0},{24,8},{1,17},{9,25},{17,1},{25,9},{2,18},{10... | collective-permute-start | bytes 393224 | tf_op jit(solution)/shard_map/ppermute | solution.py:235
  7.2 0.3 collective-permute-start
  7.4 0.7 copy-done
  8.2 0.5 shard_map.59.refs_8_.refs_4_
  8.6 0.0 collective-permute-done.3
  8.7 3.7 %collective-permute-start.6 = (bf16[2,128,512]{2,1,0:T(8,128)(2,1)S(1)}, bf16[2,128,512]{2,1,0:T(8,128)(2,1)S(1)}, u32[]{:S(2)}, u32[]{:S(2)}) collective-permute-start(bf16[2,128,512]{2,1,0:T(8,128)(2,1)S(1)} %bitcast.12), channel_id=1, source_target_pairs={{0,6},{1,7},{2,4},{3,5},{4,2},{5,3},{6,0},{7,1},{8,14},{9,15},{10,... | collective-permute-start | bytes 786440 | tf_op jit(solution)/shard_map/ppermute | solution.py:235
  12.3 0.0 collective-permute-start.5
  12.3 0.0 collective-permute-done.2.refs_3_
  12.3 0.8 collective-permute-start.4
  13.1 1.1 %collective-permute-done.1.refs_2_ = bf16[128,512]{1,0:T(8,128)(2,1)S(1)} collective-permute-done((bf16[128,512]{1,0:T(8,128)(2,1)S(1)}, bf16[128,512]{1,0:T(8,128)(2,1)S(1)}, u32[]{:S(2)}, u32[]{:S(2)}) %collective-permute-start.1) | collective-permute-done | bytes 131104 | tf_op jit(solution)/shard_map/ppermute | solution.py:235
  14.2 0.0 collective-permute-done.refs_1_
  14.2 29.9 %shard_map.61 = f32[8,136,512]{2,1,0:T(8,128)S(1)} custom-call(bf16[128,512]{1,0:T(8,128)(2,1)S(1)} %bitcast.19, bf16[128,512]{1,0:T(8,128)(2,1)S(1)} %collective-permute-done.refs_1_, bf16[128,512]{1,0:T(8,128)(2,1)S(1)} %collective-permute-done.1.refs_2_, bf16[128,512]{1,0:T(8,128)(2,1)S(1)} %collective-permute-done.2.refs_3_, ...), custom_call_target="tpu_custom_call" | custom-call | flops 25769803776 | bytes 25165824 | tf_op jit(solution)/shard_map/pallas_call | solution.py:138
  44.1 1.3 %convert_element_type.16 = f16[8,136,512]{2,1,0:T(8,128)(2,1)} convert(f32[8,136,512]{2,1,0:T(8,128)S(1)} %shard_map.61) | non-fusion elementwise | flops 557056 | bytes 3342336 | tf_op jit(solution)/shard_map/convert_element_type | solution.py:256
  45.4 4.9 %all-to-all-start = ((f16[8,136,512]{2,1,0:T(8,128)(2,1)}), f16[8,136,512]{2,1,0:T(8,128)(2,1)}, u32[]{:S(2)}, u32[]{:S(2)}) async-start(f16[8,136,512]{2,1,0:T(8,128)(2,1)} %convert_element_type.16), calls=%async_computation | async-start | bytes 2228224 | tf_op jit(solution)/shard_map/all_to_all | solution.py:257
  50.2 0.0 collective-permute-done.5.refs_6_
  50.3 28.9 %shard_map.60 = bf16[24,512,1024]{2,1,0:T(8,128)(2,1)} custom-call(bf16[128,512]{1,0:T(8,128)(2,1)S(1)} %bitcast.20, bf16[128,512]{1,0:T(8,128)(2,1)S(1)} %collective-permute-done.refs_1_, bf16[128,512]{1,0:T(8,128)(2,1)S(1)} %collective-permute-done.1.refs_2_, bf16[128,512]{1,0:T(8,128)(2,1)S(1)} %collective-permute-done.2.refs_3_, ...), custom_call_target="tpu_custom_call" | custom-call | flops 19327352832 | bytes 25165824 | tf_op jit(solution)/shard_map/pallas_call | solution.py:215
  79.2 0.0 all-to-all-done
  79.2 0.9 %fusion.2 = f32[8,1,512]{2,1,0:T(1,128)S(1)} fusion(f16[8,136,512]{2,1,0:T(8,128)(2,1)} %all-to-all-done), kind=kLoop, calls=%fused_computation.7 | loop fusion | flops 12288 | bytes 24576 | tf_op jit(solution)/shard_map/exp2 | solution.py:259
  80.1 1.4 %multiply_reduce_fusion = bf16[128,512]{1,0:T(8,128)(2,1)S(1)} fusion(f16[8,136,512]{2,1,0:T(8,128)(2,1)} %all-to-all-done, f32[8,512]{1,0:T(8,128)S(1)} %bitcast.25), kind=kLoop, calls=%fused_computation | loop fusion | flops 1507328 | bytes 1196032 | tf_op jit(solution)/shard_map/reduce_sum | solution.py:260
  81.5 0.7 convert_element_type.20
  (5 shorter events, 0.0 us)
Async XLA Ops:
  1.6 7.1 %collective-permute-start.3 = (bf16[128,512]{1,0:T(8,128)(2,1)S(1)}, bf16[128,512]{1,0:T(8,128)(2,1)S(1)}, u32[]{:S(2)}, u32[]{:S(2)}) collective-permute-start(bf16[128,512]{1,0:T(8,128)(2,1)S(1)} %bitcast.21), channel_id=1, source_target_pairs={{0,1},{1,0},{2,3},{3,2},{4,5},{5,4},{6,7},{7,6},{8,9},{9,8},{10,11... | collective-permute-start | bytes 393224 | tf_op jit(solution)/shard_map/ppermute | solution.py:235
  5.5 6.8 %collective-permute-start.2 = (bf16[128,512]{1,0:T(8,128)(2,1)S(1)}, bf16[128,512]{1,0:T(8,128)(2,1)S(1)}, u32[]{:S(2)}, u32[]{:S(2)}) collective-permute-start(bf16[128,512]{1,0:T(8,128)(2,1)S(1)} %bitcast.16), channel_id=1, source_target_pairs={{0,24},{8,16},{16,8},{24,0},{1,25},{9,17},{17,9},{25,1},{2,26},{10... | collective-permute-start | bytes 393224 | tf_op jit(solution)/shard_map/ppermute | solution.py:235
  6.2 8.0 %collective-permute-start.1 = (bf16[128,512]{1,0:T(8,128)(2,1)S(1)}, bf16[128,512]{1,0:T(8,128)(2,1)S(1)}, u32[]{:S(2)}, u32[]{:S(2)}) collective-permute-start(bf16[128,512]{1,0:T(8,128)(2,1)S(1)} %bitcast.17), channel_id=1, source_target_pairs={{0,16},{8,24},{16,0},{24,8},{1,17},{9,25},{17,1},{25,9},{2,18},{10... | collective-permute-start | bytes 393224 | tf_op jit(solution)/shard_map/ppermute | solution.py:235
  7.2 7.0 %collective-permute-start = (bf16[128,512]{1,0:T(8,128)(2,1)S(1)}, bf16[128,512]{1,0:T(8,128)(2,1)S(1)}, u32[]{:S(2)}, u32[]{:S(2)}) collective-permute-start(bf16[128,512]{1,0:T(8,128)(2,1)S(1)} %bitcast.18), channel_id=1, source_target_pairs={{0,8},{8,0},{16,24},{24,16},{1,9},{9,1},{17,25},{25,17},{2,10},{10... | collective-permute-start | bytes 393224 | tf_op jit(solution)/shard_map/ppermute | solution.py:235
  7.4 0.7 copy-start
  8.7 41.6 %collective-permute-start.6 = (bf16[2,128,512]{2,1,0:T(8,128)(2,1)S(1)}, bf16[2,128,512]{2,1,0:T(8,128)(2,1)S(1)}, u32[]{:S(2)}, u32[]{:S(2)}) collective-permute-start(bf16[2,128,512]{2,1,0:T(8,128)(2,1)S(1)} %bitcast.12), channel_id=1, source_target_pairs={{0,6},{1,7},{2,4},{3,5},{4,2},{5,3},{6,0},{7,1},{8,14},{9,15},{10,... | collective-permute-start | bytes 786440 | tf_op jit(solution)/shard_map/ppermute | solution.py:235
  12.3 37.9 %collective-permute-start.5 = (bf16[2,128,512]{2,1,0:T(8,128)(2,1)S(1)}, bf16[2,128,512]{2,1,0:T(8,128)(2,1)S(1)}, u32[]{:S(2)}, u32[]{:S(2)}) collective-permute-start(bf16[2,128,512]{2,1,0:T(8,128)(2,1)S(1)} %bitcast.13), channel_id=1, source_target_pairs={{0,4},{1,5},{2,6},{3,7},{4,0},{5,1},{6,2},{7,3},{8,12},{9,13},{10,... | collective-permute-start | bytes 786440 | tf_op jit(solution)/shard_map/ppermute | solution.py:235
  12.3 37.9 %collective-permute-start.4 = (bf16[2,128,512]{2,1,0:T(8,128)(2,1)S(1)}, bf16[2,128,512]{2,1,0:T(8,128)(2,1)S(1)}, u32[]{:S(2)}, u32[]{:S(2)}) collective-permute-start(bf16[2,128,512]{2,1,0:T(8,128)(2,1)S(1)} %bitcast.14), channel_id=1, source_target_pairs={{0,2},{1,3},{2,0},{3,1},{4,6},{5,7},{6,4},{7,5},{8,10},{9,11},{10,... | collective-permute-start | bytes 786440 | tf_op jit(solution)/shard_map/ppermute | solution.py:235
  45.4 33.8 %all-to-all-start = ((f16[8,136,512]{2,1,0:T(8,128)(2,1)}), f16[8,136,512]{2,1,0:T(8,128)(2,1)}, u32[]{:S(2)}, u32[]{:S(2)}) async-start(f16[8,136,512]{2,1,0:T(8,128)(2,1)} %convert_element_type.16), calls=%async_computation | async-start | bytes 2228224 | tf_op jit(solution)/shard_map/all_to_all | solution.py:257

commit v7 on v6

--- a/solution.py
+++ b/solution.py
@@ -1,4 +1,5 @@
 import functools
+import itertools
 
 import jax
 import jax.numpy as jnp
@@ -13,6 +14,7 @@
 F8 = jnp.float8_e4m3fn
 MIB = 1024 * 1024
 GROUP = 4
+CHUNK = 256
 TINY = 1e-30
 
 
@@ -53,6 +55,18 @@
     length = table.shape[1]
     sums = [jnp.sum(jnp.abs(table[k, 0:1, :length].astype(F32)), keepdims=True) for k in range(table.shape[0])]
     return [jnp.maximum(total * gmax, TINY) for total in sums]
+
+
+def interleave(first, second):
+    for one, other in itertools.zip_longest(first, second):
+        for work in (one, other):
+            if work is not None:
+                work()
+
+
+def chunks(width):
+    size = min(width, CHUNK)
+    return [slice(start, start + size) for start in range(0, width, size)]
 
 
 def table_kernel(filters_ref, rows_ref):
@@ -85,6 +99,23 @@
     out_width = matrix_ref.shape[1]
     seqs = grads.shape[1] // out_width
     tokens = seqs * length
+
+    def table_of(first):
+        table = rows_ref[pl.ds(first, 2)]
+        reach = functools.reduce(jnp.maximum, reach_of(table, bounds[0:1, 0:1]))
+        return table.reshape(2 * length, 2 * length), reach
+
+    def filter_sequence(slot, table, reach, b):
+        high, low = split(dot(table, grads[:, b * out_width : (b + 1) * out_width]))
+        low = (low * (65536.0 / reach)).astype(F8)
+        rows = slice(b * length, (b + 1) * length)
+        for k in range(2):
+            source, columns = slice(k * length, (k + 1) * length), slice(k * out_width, (k + 1) * out_width)
+            parts[slot, rows, columns] = high[source]
+            parts8[slot, rows, columns] = low[source]
+
+    def filters_of(slot, table, reach):
+        return [functools.partial(filter_sequence, slot, table, reach, b) for b in range(seqs)]
 
     @pl.when(step == 0)
     def _():
@@ -98,23 +129,25 @@
                 grads[length:, columns] = turned
         gmax = functools.reduce(jnp.maximum, [largest(piece[...]) for piece in pieces])
         bounds[...] = jnp.broadcast_to(gmax, bounds.shape)
-
-    matrix = matrix_ref[...].reshape(GROUP * out_width, -1)
-    peak = jnp.max(jnp.abs(matrix).reshape(-1, 16, matrix.shape[1]), axis=0)
+        interleave(filters_of(0, *table_of(0)), [])
+
+    peak = jnp.max(jnp.abs(matrix_ref[...]).reshape(-1, 16, matrix_ref.shape[2]), axis=0)
     matrix_scale = (256.0 / jnp.maximum(largest(peak), TINY)).astype(BF16)
-    matrix8 = (matrix * matrix_scale).astype(F8)
-    table = rows_ref[pl.ds(GROUP * step, GROUP)]
-    reach = functools.reduce(jnp.maximum, reach_of(table, bounds[0:1, 0:1]))
-    table = table.reshape(GROUP * length, 2 * length)
-    for b in range(seqs):
-        high, low = split(dot(table, grads[:, b * out_width : (b + 1) * out_width]))
-        low = (low * (65536.0 / reach)).astype(F8)
-        for k in range(GROUP):
-            source, columns = slice(k * length, (k + 1) * length), slice(k * out_width, (k + 1) * out_width)
-            parts[b * length : (b + 1) * length, columns] = high[source]
-            parts8[b * length : (b + 1) * length, columns] = low[source]
-    back = (reach / 65536.0) / matrix_scale.astype(F32)
-    total[...] += dot(parts[...], matrix) + dot(parts8[...], matrix8) * back
+
+    def product(slot, back, columns):
+        matrix = matrix_ref[2 * slot : 2 * slot + 2, :, columns].reshape(2 * out_width, -1)
+        matrix8 = (matrix * matrix_scale).astype(F8)
+        total[:, columns] += dot(parts[slot], matrix) + dot(parts8[slot], matrix8) * back
+
+    def products_of(slot, reach):
+        back = (reach / 65536.0) / matrix_scale.astype(F32)
+        return [functools.partial(product, slot, back, columns) for columns in chunks(matrix_ref.shape[2])]
+
+    now = table_of(GROUP * step)
+    late = table_of(GROUP * step + 2)
+    coming = table_of(lax.rem(GROUP * step + GROUP, rows_ref.shape[0]))
+    interleave(products_of(0, now[1]), filters_of(1, *late))
+    interleave(products_of(1, late[1]), filters_of(0, *coming))
 
     @pl.when(step == pl.num_programs(0) - 1)
     def _():
@@ -146,8 +179,8 @@
         out_specs=whole(out),
         scratch_shapes=[
             pltpu.VMEM((2 * length, seqs * out_width), BF16),
-            pltpu.VMEM((tokens, GROUP * out_width), BF16),
-            pltpu.VMEM((tokens, GROUP * out_width), F8),
+            pltpu.VMEM((2, tokens, 2 * out_width), BF16),
+            pltpu.VMEM((2, tokens, 2 * out_width), F8),
             pltpu.VMEM((tokens, in_width), F32),
             pltpu.VMEM((8, length), F32),
         ],
@@ -163,6 +196,36 @@
     tokens = inputs.shape[0]
     seqs = tokens // length
     out_width = out_ref.shape[1]
+
+    def table_of(first):
+        table = rows_ref[pl.ds(first, 2)]
+        return table.reshape(2 * length, 2 * length), reach_of(table, bounds[0:1, 0:1])
+
+    def filter_sequence(slot, table, reach, b):
+        filtered = lax.dot_general(
+            grads[b * out_width : (b + 1) * out_width], table, (((1,), (1,)), ((), ())), preferred_element_type=F32
+        )
+        high, low = split(filtered)
+        place = slice(b * length, (b + 1) * length)
+        for k in range(2):
+            columns = slice(k * length, (k + 1) * length)
+            parts[2 * slot + k, :, place] = high[:, columns]
+            parts8[2 * slot + k, :, place] = (low[:, columns] * (65536.0 / reach[k])).astype(F8)
+
+    def filters_of(slot, table, reach):
+        return [functools.partial(filter_sequence, slot, table, reach, b) for b in range(seqs)]
+
+    def product(k, back, columns):
+        total = dot(parts[k], inputs[:, columns]) + dot(parts8[k], inputs8[:, columns]) * back
+        out_ref[k, :, columns] = total.astype(BF16)
+
+    def products_of(slot, reach):
+        backs = [(reach[k] / 65536.0) * (bounds[1:2, 0:1] / 256.0) for k in range(2)]
+        return [
+            functools.partial(product, 2 * slot + k, backs[k], columns)
+            for k in range(2)
+            for columns in chunks(inputs.shape[1])
+        ]
 
     @pl.when(step == 0)
     def _():
@@ -185,26 +248,13 @@
                 turned = piece[half].astype(F32).T
                 inputs[:, columns] = turned.astype(BF16)
                 inputs8[:, columns] = (turned * (256.0 / xmax)).astype(F8)
-
-    table = rows_ref[pl.ds(GROUP * step, GROUP)]
-    reach = reach_of(table, bounds[0:1, 0:1])
-    table = table.reshape(GROUP * length, 2 * length)
-    for first in range(0, GROUP, 2):
-        some = table[first * length : (first + 2) * length]
-        for b in range(seqs):
-            place = slice(b * length, (b + 1) * length)
-            filtered = lax.dot_general(
-                grads[b * out_width : (b + 1) * out_width], some, (((1,), (1,)), ((), ())), preferred_element_type=F32
-            )
-            high, low = split(filtered)
-            for k in range(2):
-                columns = slice(k * length, (k + 1) * length)
-                parts[first + k, :, place] = high[:, columns]
-                parts8[first + k, :, place] = (low[:, columns] * (65536.0 / reach[first + k])).astype(F8)
-    for k in range(GROUP):
-        back = (reach[k] / 65536.0) * (bounds[1:2, 0:1] / 256.0)
-        product = dot(parts[k], inputs[...]) + dot(parts8[k], inputs8[...]) * back
-        out_ref[k] = product.astype(BF16)
+        interleave(filters_of(0, *table_of(0)), [])
+
+    now = table_of(GROUP * step)
+    late = table_of(GROUP * step + 2)
+    coming = table_of(lax.rem(GROUP * step + GROUP, rows_ref.shape[0]))
+    interleave(products_of(0, now[1]), filters_of(1, *late))
+    interleave(products_of(1, late[1]), filters_of(0, *coming))
 
 
 def matrix_sums(pieces, input_pieces, rows, cout_count, shape):

time: 82.5 us -> 83.2 us (level)
    pallas_call x1, Pallas kernels: 29.9 us -> 31.4 us  [back_sums(): call(functools.partial(back_kernel, len(pieces)), (4 * count * out_width...]
    pallas_call x1, Pallas kernels: 28.9 us -> 28.1 us  [matrix_sums(): call(functools.partial(matrix_kernel, len(pieces), len(input_pieces), cou...]
where the time goes in v7:
time: 83.2 us; the launch traced here: 82.9 us
  Pallas kernels  59.9 us (72%)
  starting transfers between devices  14.3 us (17%)
  other arithmetic  3.61 us (4%)
  local copies, waits for them, and re-layouts  3.25 us (4%)
  waiting for transfers between devices  1.08 us (1%)
    pallas_call x1, Pallas kernels, back_sums(): call(functools.partial(back_kernel, len(pieces)), (4 * count * out_width...  31.4 us
    pallas_call x1, Pallas kernels, matrix_sums(): call(functools.partial(matrix_kernel, len(pieces), len(input_pieces), cou...  28.1 us
    ppermute x7, starting transfers between devices, exchange(): return lax.ppermute(array, axis, [(i, i ^ flip) for i in range(count)])  9.41 us
    all_to_all x1, starting transfers between devices, shards(): came = lax.all_to_all(blocks, 'cout', 0, 0, tiled=True)  4.87 us
    unnamed x5, local copies, waits for them, and re-layouts  2.56 us
  transfers between devices with their start and end apart: 8, of which 1 were waited for; matrix products, arithmetic and copies ran while one was open for 3% of the time, Pallas kernels for 72%

profile of v7, /device:TPU:0, one launch (start us, length us, event | category | flops | bytes accessed | tf_op | source)
XLA Modules:
  0.0 82.9 jit_solution(16295778863467109866)
XLA Ops:
  0.6 0.9 %copy.12 = bf16[16,8,4,128]{3,1,2,0:T(8,128)(2,1)S(1)} copy(bf16[16,8,4,128]{3,2,1,0:T(4,128)(2,1)} %bitcast.23) | data formatting | bytes 262144
  1.6 3.0 %collective-permute-start.3 = (bf16[128,512]{1,0:T(8,128)(2,1)S(1)}, bf16[128,512]{1,0:T(8,128)(2,1)S(1)}, u32[]{:S(2)}, u32[]{:S(2)}) collective-permute-start(bf16[128,512]{1,0:T(8,128)(2,1)S(1)} %bitcast.21), channel_id=1, source_target_pairs={{0,1},{1,0},{2,3},{3,2},{4,5},{5,4},{6,7},{7,6},{8,9},{9,8},{10,11... | collective-permute-start | bytes 393224 | tf_op jit(solution)/shard_map/ppermute | solution.py:285
  4.6 0.9 %copy.13 = bf16[16,8,4,128]{3,1,2,0:T(8,128)(2,1)S(1)} copy(bf16[16,8,4,128]{3,2,1,0:T(4,128)(2,1)} %bitcast.24) | data formatting | bytes 262144
  5.5 0.7 collective-permute-start.2
  6.2 0.9 %collective-permute-start.1 = (bf16[128,512]{1,0:T(8,128)(2,1)S(1)}, bf16[128,512]{1,0:T(8,128)(2,1)S(1)}, u32[]{:S(2)}, u32[]{:S(2)}) collective-permute-start(bf16[128,512]{1,0:T(8,128)(2,1)S(1)} %bitcast.17), channel_id=1, source_target_pairs={{0,16},{8,24},{16,0},{24,8},{1,17},{9,25},{17,1},{25,9},{2,18},{10... | collective-permute-start | bytes 393224 | tf_op jit(solution)/shard_map/ppermute | solution.py:285
  7.2 0.3 collective-permute-start
  7.4 0.7 copy-done
  8.2 0.5 shard_map.59.refs_8_.refs_4_
  8.6 0.0 collective-permute-done.3
  8.7 3.7 %collective-permute-start.6 = (bf16[2,128,512]{2,1,0:T(8,128)(2,1)S(1)}, bf16[2,128,512]{2,1,0:T(8,128)(2,1)S(1)}, u32[]{:S(2)}, u32[]{:S(2)}) collective-permute-start(bf16[2,128,512]{2,1,0:T(8,128)(2,1)S(1)} %bitcast.12), channel_id=1, source_target_pairs={{0,6},{1,7},{2,4},{3,5},{4,2},{5,3},{6,0},{7,1},{8,14},{9,15},{10,... | collective-permute-start | bytes 786440 | tf_op jit(solution)/shard_map/ppermute | solution.py:285
  12.3 0.0 collective-permute-start.5
  12.3 0.0 collective-permute-done.2.refs_3_
  12.3 0.8 collective-permute-start.4
  13.1 1.1 %collective-permute-done.1.refs_2_ = bf16[128,512]{1,0:T(8,128)(2,1)S(1)} collective-permute-done((bf16[128,512]{1,0:T(8,128)(2,1)S(1)}, bf16[128,512]{1,0:T(8,128)(2,1)S(1)}, u32[]{:S(2)}, u32[]{:S(2)}) %collective-permute-start.1) | collective-permute-done | bytes 131104 | tf_op jit(solution)/shard_map/ppermute | solution.py:285
  14.2 0.0 collective-permute-done.refs_1_
  14.2 31.4 %shard_map.61 = f32[8,136,512]{2,1,0:T(8,128)S(1)} custom-call(bf16[128,512]{1,0:T(8,128)(2,1)S(1)} %bitcast.19, bf16[128,512]{1,0:T(8,128)(2,1)S(1)} %collective-permute-done.refs_1_, bf16[128,512]{1,0:T(8,128)(2,1)S(1)} %collective-permute-done.1.refs_2_, bf16[128,512]{1,0:T(8,128)(2,1)S(1)} %collective-permute-done.2.refs_3_, ...), custom_call_target="tpu_custom_call" | custom-call | flops 25769803776 | bytes 25165824 | tf_op jit(solution)/shard_map/pallas_call | solution.py:171
  45.6 1.3 %convert_element_type.16 = f16[8,136,512]{2,1,0:T(8,128)(2,1)} convert(f32[8,136,512]{2,1,0:T(8,128)S(1)} %shard_map.61) | non-fusion elementwise | flops 557056 | bytes 3342336 | tf_op jit(solution)/shard_map/convert_element_type | solution.py:306
  46.9 4.9 %all-to-all-start = ((f16[8,136,512]{2,1,0:T(8,128)(2,1)}), f16[8,136,512]{2,1,0:T(8,128)(2,1)}, u32[]{:S(2)}, u32[]{:S(2)}) async-start(f16[8,136,512]{2,1,0:T(8,128)(2,1)} %convert_element_type.16), calls=%async_computation | async-start | bytes 2228224 | tf_op jit(solution)/shard_map/all_to_all | solution.py:307
  51.7 0.0 collective-permute-done.6.refs_7_
  51.7 0.0 collective-permute-done.4.refs_5_
  51.8 28.1 %shard_map.60 = bf16[24,512,1024]{2,1,0:T(8,128)(2,1)} custom-call(bf16[128,512]{1,0:T(8,128)(2,1)S(1)} %bitcast.20, bf16[128,512]{1,0:T(8,128)(2,1)S(1)} %collective-permute-done.refs_1_, bf16[128,512]{1,0:T(8,128)(2,1)S(1)} %collective-permute-done.1.refs_2_, bf16[128,512]{1,0:T(8,128)(2,1)S(1)} %collective-permute-done.2.refs_3_, ...), custom_call_target="tpu_custom_call" | custom-call | flops 19327352832 | bytes 25165824 | tf_op jit(solution)/shard_map/pallas_call | solution.py:265
  79.8 0.9 %fusion.2 = f32[8,1,512]{2,1,0:T(1,128)S(1)} fusion(f16[8,136,512]{2,1,0:T(8,128)(2,1)} %all-to-all-done), kind=kLoop, calls=%fused_computation.7 | loop fusion | flops 12288 | bytes 24576 | tf_op jit(solution)/shard_map/exp2 | solution.py:309
  80.7 1.4 %multiply_reduce_fusion = bf16[128,512]{1,0:T(8,128)(2,1)S(1)} fusion(f16[8,136,512]{2,1,0:T(8,128)(2,1)} %all-to-all-done, f32[8,512]{1,0:T(8,128)S(1)} %bitcast.25), kind=kLoop, calls=%fused_computation | loop fusion | flops 1507328 | bytes 1196032 | tf_op jit(solution)/shard_map/reduce_sum | solution.py:310
  82.2 0.7 convert_element_type.20
  (5 shorter events, 0.0 us)
Async XLA Ops:
  1.6 7.1 %collective-permute-start.3 = (bf16[128,512]{1,0:T(8,128)(2,1)S(1)}, bf16[128,512]{1,0:T(8,128)(2,1)S(1)}, u32[]{:S(2)}, u32[]{:S(2)}) collective-permute-start(bf16[128,512]{1,0:T(8,128)(2,1)S(1)} %bitcast.21), channel_id=1, source_target_pairs={{0,1},{1,0},{2,3},{3,2},{4,5},{5,4},{6,7},{7,6},{8,9},{9,8},{10,11... | collective-permute-start | bytes 393224 | tf_op jit(solution)/shard_map/ppermute | solution.py:285
  5.5 6.8 %collective-permute-start.2 = (bf16[128,512]{1,0:T(8,128)(2,1)S(1)}, bf16[128,512]{1,0:T(8,128)(2,1)S(1)}, u32[]{:S(2)}, u32[]{:S(2)}) collective-permute-start(bf16[128,512]{1,0:T(8,128)(2,1)S(1)} %bitcast.16), channel_id=1, source_target_pairs={{0,24},{8,16},{16,8},{24,0},{1,25},{9,17},{17,9},{25,1},{2,26},{10... | collective-permute-start | bytes 393224 | tf_op jit(solution)/shard_map/ppermute | solution.py:285
  6.2 8.0 %collective-permute-start.1 = (bf16[128,512]{1,0:T(8,128)(2,1)S(1)}, bf16[128,512]{1,0:T(8,128)(2,1)S(1)}, u32[]{:S(2)}, u32[]{:S(2)}) collective-permute-start(bf16[128,512]{1,0:T(8,128)(2,1)S(1)} %bitcast.17), channel_id=1, source_target_pairs={{0,16},{8,24},{16,0},{24,8},{1,17},{9,25},{17,1},{25,9},{2,18},{10... | collective-permute-start | bytes 393224 | tf_op jit(solution)/shard_map/ppermute | solution.py:285
  7.2 7.0 %collective-permute-start = (bf16[128,512]{1,0:T(8,128)(2,1)S(1)}, bf16[128,512]{1,0:T(8,128)(2,1)S(1)}, u32[]{:S(2)}, u32[]{:S(2)}) collective-permute-start(bf16[128,512]{1,0:T(8,128)(2,1)S(1)} %bitcast.18), channel_id=1, source_target_pairs={{0,8},{8,0},{16,24},{24,16},{1,9},{9,1},{17,25},{25,17},{2,10},{10... | collective-permute-start | bytes 393224 | tf_op jit(solution)/shard_map/ppermute | solution.py:285
  7.4 0.7 copy-start
  8.7 43.1 %collective-permute-start.6 = (bf16[2,128,512]{2,1,0:T(8,128)(2,1)S(1)}, bf16[2,128,512]{2,1,0:T(8,128)(2,1)S(1)}, u32[]{:S(2)}, u32[]{:S(2)}) collective-permute-start(bf16[2,128,512]{2,1,0:T(8,128)(2,1)S(1)} %bitcast.12), channel_id=1, source_target_pairs={{0,6},{1,7},{2,4},{3,5},{4,2},{5,3},{6,0},{7,1},{8,14},{9,15},{10,... | collective-permute-start | bytes 786440 | tf_op jit(solution)/shard_map/ppermute | solution.py:285
  12.3 39.4 %collective-permute-start.5 = (bf16[2,128,512]{2,1,0:T(8,128)(2,1)S(1)}, bf16[2,128,512]{2,1,0:T(8,128)(2,1)S(1)}, u32[]{:S(2)}, u32[]{:S(2)}) collective-permute-start(bf16[2,128,512]{2,1,0:T(8,128)(2,1)S(1)} %bitcast.13), channel_id=1, source_target_pairs={{0,4},{1,5},{2,6},{3,7},{4,0},{5,1},{6,2},{7,3},{8,12},{9,13},{10,... | collective-permute-start | bytes 786440 | tf_op jit(solution)/shard_map/ppermute | solution.py:285
  12.3 39.4 %collective-permute-start.4 = (bf16[2,128,512]{2,1,0:T(8,128)(2,1)S(1)}, bf16[2,128,512]{2,1,0:T(8,128)(2,1)S(1)}, u32[]{:S(2)}, u32[]{:S(2)}) collective-permute-start(bf16[2,128,512]{2,1,0:T(8,128)(2,1)S(1)} %bitcast.14), channel_id=1, source_target_pairs={{0,2},{1,3},{2,0},{3,1},{4,6},{5,7},{6,4},{7,5},{8,10},{9,11},{10,... | collective-permute-start | bytes 786440 | tf_op jit(solution)/shard_map/ppermute | solution.py:285
  46.9 33.0 %all-to-all-start = ((f16[8,136,512]{2,1,0:T(8,128)(2,1)}), f16[8,136,512]{2,1,0:T(8,128)(2,1)}, u32[]{:S(2)}, u32[]{:S(2)}) async-start(f16[8,136,512]{2,1,0:T(8,128)(2,1)} %convert_element_type.16), calls=%async_computation | async-start | bytes 2228224 | tf_op jit(solution)/shard_map/all_to_all | solution.py:307

commit v8 on v7

--- a/solution.py
+++ b/solution.py
@@ -93,32 +93,21 @@
 
 def back_kernel(cin_count, *refs):
     pieces = refs[:cin_count]
-    rows_ref, matrix_ref, out, grads, parts, parts8, total, bounds = refs[cin_count:]
+    rows_ref, matrices_ref, out, grads, parts, parts8, total, bounds, blocks, arrived = refs[cin_count:]
     step = pl.program_id(0)
+    slot = lax.rem(step, 2)
     _, length, _ = rows_ref.shape
-    out_width = matrix_ref.shape[1]
+    out_width = matrices_ref.shape[1]
     seqs = grads.shape[1] // out_width
     tokens = seqs * length
 
-    def table_of(first):
-        table = rows_ref[pl.ds(first, 2)]
-        reach = functools.reduce(jnp.maximum, reach_of(table, bounds[0:1, 0:1]))
-        return table.reshape(2 * length, 2 * length), reach
-
-    def filter_sequence(slot, table, reach, b):
-        high, low = split(dot(table, grads[:, b * out_width : (b + 1) * out_width]))
-        low = (low * (65536.0 / reach)).astype(F8)
-        rows = slice(b * length, (b + 1) * length)
-        for k in range(2):
-            source, columns = slice(k * length, (k + 1) * length), slice(k * out_width, (k + 1) * out_width)
-            parts[slot, rows, columns] = high[source]
-            parts8[slot, rows, columns] = low[source]
-
-    def filters_of(slot, table, reach):
-        return [functools.partial(filter_sequence, slot, table, reach, b) for b in range(seqs)]
+    def fetch(index):
+        target = lax.rem(index, 2)
+        return pltpu.make_async_copy(matrices_ref.at[pl.ds(GROUP * index, GROUP)], blocks.at[target], arrived.at[target])
 
     @pl.when(step == 0)
     def _():
+        fetch(step).start()
         total[...] = jnp.zeros_like(total)
         block = pieces[0].shape[0]
         for b in range(seqs):
@@ -129,25 +118,30 @@
                 grads[length:, columns] = turned
         gmax = functools.reduce(jnp.maximum, [largest(piece[...]) for piece in pieces])
         bounds[...] = jnp.broadcast_to(gmax, bounds.shape)
-        interleave(filters_of(0, *table_of(0)), [])
-
-    peak = jnp.max(jnp.abs(matrix_ref[...]).reshape(-1, 16, matrix_ref.shape[2]), axis=0)
+
+    @pl.when(step + 1 < pl.num_programs(0))
+    def _():
+        fetch(step + 1).start()
+
+    fetch(step).wait()
+    matrix = blocks[slot].reshape(GROUP * out_width, -1)
+    peak = jnp.max(jnp.abs(matrix).reshape(-1, 16, matrix.shape[1]), axis=0)
     matrix_scale = (256.0 / jnp.maximum(largest(peak), TINY)).astype(BF16)
-
-    def product(slot, back, columns):
-        matrix = matrix_ref[2 * slot : 2 * slot + 2, :, columns].reshape(2 * out_width, -1)
+    table = rows_ref[pl.ds(GROUP * step, GROUP)]
+    reach = functools.reduce(jnp.maximum, reach_of(table, bounds[0:1, 0:1]))
+    table = table.reshape(GROUP * length, 2 * length)
+    for b in range(seqs):
+        high, low = split(dot(table, grads[:, b * out_width : (b + 1) * out_width]))
+        low = (low * (65536.0 / reach)).astype(F8)
+        for k in range(GROUP):
+            source, columns = slice(k * length, (k + 1) * length), slice(k * out_width, (k + 1) * out_width)
+            parts[b * length : (b + 1) * length, columns] = high[source]
+            parts8[b * length : (b + 1) * length, columns] = low[source]
+    back = (reach / 65536.0) / matrix_scale.astype(F32)
+    for columns in chunks(total.shape[1]):
+        matrix = blocks[slot, :, :, columns].reshape(GROUP * out_width, -1)
         matrix8 = (matrix * matrix_scale).astype(F8)
-        total[:, columns] += dot(parts[slot], matrix) + dot(parts8[slot], matrix8) * back
-
-    def products_of(slot, reach):
-        back = (reach / 65536.0) / matrix_scale.astype(F32)
-        return [functools.partial(product, slot, back, columns) for columns in chunks(matrix_ref.shape[2])]
-
-    now = table_of(GROUP * step)
-    late = table_of(GROUP * step + 2)
-    coming = table_of(lax.rem(GROUP * step + GROUP, rows_ref.shape[0]))
-    interleave(products_of(0, now[1]), filters_of(1, *late))
-    interleave(products_of(1, late[1]), filters_of(0, *coming))
+        total[:, columns] += dot(parts[...], matrix) + dot(parts8[...], matrix8) * back
 
     @pl.when(step == pl.num_programs(0) - 1)
     def _():
@@ -175,14 +169,16 @@
         out_shape=out,
         grid=(count // GROUP,),
         in_specs=[whole(piece) for piece in pieces]
-        + [whole(rows), pl.BlockSpec((GROUP, out_width, in_width), lambda i: (i, 0, 0))],
+        + [whole(rows), pl.BlockSpec(memory_space=pl.ANY)],
         out_specs=whole(out),
         scratch_shapes=[
             pltpu.VMEM((2 * length, seqs * out_width), BF16),
-            pltpu.VMEM((2, tokens, 2 * out_width), BF16),
-            pltpu.VMEM((2, tokens, 2 * out_width), F8),
+            pltpu.VMEM((tokens, GROUP * out_width), BF16),
+            pltpu.VMEM((tokens, GROUP * out_width), F8),
             pltpu.VMEM((tokens, in_width), F32),
             pltpu.VMEM((8, length), F32),
+            pltpu.VMEM((2, GROUP, out_width, in_width), BF16),
+            pltpu.SemaphoreType.DMA((2,)),
         ],
     )(*pieces, rows, matrices)
 

time: 83.2 us -> 86.6 us (1.041)
  Pallas kernels: 59.9 us -> 63.3 us
    pallas_call x1, Pallas kernels: 31.4 us -> 34.7 us  [back_sums(): call(functools.partial(back_kernel, len(pieces)), (4 * count * out_width...]
  transfers between devices with their start and end apart: 8 -> 8, of which waited for: 1 -> 1; matrix products, arithmetic and copies ran while one was open for 3% -> 3% of each run, Pallas kernels for 72% -> 73%
where the time goes in v8:
time: 86.6 us; the launch traced here: 86.2 us
  Pallas kernels  63.3 us (73%)
  starting transfers between devices  14.3 us (17%)
  other arithmetic  3.61 us (4%)
  local copies, waits for them, and re-layouts  3.25 us (4%)
  waiting for transfers between devices  1.08 us (1%)
    pallas_call x1, Pallas kernels, back_sums(): call(functools.partial(back_kernel, len(pieces)), (4 * count * out_width...  34.7 us
    pallas_call x1, Pallas kernels, matrix_sums(): call(functools.partial(matrix_kernel, len(pieces), len(input_pieces), cou...  28.1 us
    ppermute x7, starting transfers between devices, exchange(): return lax.ppermute(array, axis, [(i, i ^ flip) for i in range(count)])  9.41 us
    all_to_all x1, starting transfers between devices, shards(): came = lax.all_to_all(blocks, 'cout', 0, 0, tiled=True)  4.88 us
    unnamed x5, local copies, waits for them, and re-layouts  2.56 us
  transfers between devices with their start and end apart: 8, of which 1 were waited for; matrix products, arithmetic and copies ran while one was open for 3% of the time, Pallas kernels for 73%

profile of v8, /device:TPU:0, one launch (start us, length us, event | category | flops | bytes accessed | tf_op | source)
XLA Modules:
  0.0 86.2 jit_solution(13451584488396833338)
XLA Ops:
  0.6 0.9 %copy.12 = bf16[16,8,4,128]{3,1,2,0:T(8,128)(2,1)S(1)} copy(bf16[16,8,4,128]{3,2,1,0:T(4,128)(2,1)} %bitcast.23) | data formatting | bytes 262144
  1.6 3.0 %collective-permute-start.3 = (bf16[128,512]{1,0:T(8,128)(2,1)S(1)}, bf16[128,512]{1,0:T(8,128)(2,1)S(1)}, u32[]{:S(2)}, u32[]{:S(2)}) collective-permute-start(bf16[128,512]{1,0:T(8,128)(2,1)S(1)} %bitcast.21), channel_id=1, source_target_pairs={{0,1},{1,0},{2,3},{3,2},{4,5},{5,4},{6,7},{7,6},{8,9},{9,8},{10,11... | collective-permute-start | bytes 393224 | tf_op jit(solution)/shard_map/ppermute | solution.py:281
  4.6 0.9 %copy.13 = bf16[16,8,4,128]{3,1,2,0:T(8,128)(2,1)S(1)} copy(bf16[16,8,4,128]{3,2,1,0:T(4,128)(2,1)} %bitcast.24) | data formatting | bytes 262144
  5.5 0.7 collective-permute-start.2
  6.2 0.9 %collective-permute-start.1 = (bf16[128,512]{1,0:T(8,128)(2,1)S(1)}, bf16[128,512]{1,0:T(8,128)(2,1)S(1)}, u32[]{:S(2)}, u32[]{:S(2)}) collective-permute-start(bf16[128,512]{1,0:T(8,128)(2,1)S(1)} %bitcast.17), channel_id=1, source_target_pairs={{0,16},{8,24},{16,0},{24,8},{1,17},{9,25},{17,1},{25,9},{2,18},{10... | collective-permute-start | bytes 393224 | tf_op jit(solution)/shard_map/ppermute | solution.py:281
  7.2 0.3 collective-permute-start
  7.4 0.7 copy-done
  8.2 0.5 shard_map.59.refs_8_.refs_4_
  8.6 0.0 collective-permute-done.3
  8.7 3.7 %collective-permute-start.6 = (bf16[2,128,512]{2,1,0:T(8,128)(2,1)S(1)}, bf16[2,128,512]{2,1,0:T(8,128)(2,1)S(1)}, u32[]{:S(2)}, u32[]{:S(2)}) collective-permute-start(bf16[2,128,512]{2,1,0:T(8,128)(2,1)S(1)} %bitcast.12), channel_id=1, source_target_pairs={{0,6},{1,7},{2,4},{3,5},{4,2},{5,3},{6,0},{7,1},{8,14},{9,15},{10,... | collective-permute-start | bytes 786440 | tf_op jit(solution)/shard_map/ppermute | solution.py:281
  12.3 0.0 collective-permute-done.2.refs_3_
  12.3 0.8 collective-permute-start.4
  13.1 1.1 %collective-permute-done.1.refs_2_ = bf16[128,512]{1,0:T(8,128)(2,1)S(1)} collective-permute-done((bf16[128,512]{1,0:T(8,128)(2,1)S(1)}, bf16[128,512]{1,0:T(8,128)(2,1)S(1)}, u32[]{:S(2)}, u32[]{:S(2)}) %collective-permute-start.1) | collective-permute-done | bytes 131104 | tf_op jit(solution)/shard_map/ppermute | solution.py:281
  14.2 0.0 collective-permute-done.refs_1_
  14.2 34.7 %shard_map.61 = f32[8,136,512]{2,1,0:T(8,128)S(1)} custom-call(bf16[128,512]{1,0:T(8,128)(2,1)S(1)} %bitcast.19, bf16[128,512]{1,0:T(8,128)(2,1)S(1)} %collective-permute-done.refs_1_, bf16[128,512]{1,0:T(8,128)(2,1)S(1)} %collective-permute-done.1.refs_2_, bf16[128,512]{1,0:T(8,128)(2,1)S(1)} %collective-permute-done.2.refs_3_, ...), custom_call_target="tpu_custom_call" | custom-call | flops 25769803776 | bytes 25165824 | tf_op jit(solution)/shard_map/pallas_call | solution.py:165
  48.9 1.3 %convert_element_type.16 = f16[8,136,512]{2,1,0:T(8,128)(2,1)} convert(f32[8,136,512]{2,1,0:T(8,128)S(1)} %shard_map.61) | non-fusion elementwise | flops 557056 | bytes 3342336 | tf_op jit(solution)/shard_map/convert_element_type | solution.py:302
  50.2 4.9 %all-to-all-start = ((f16[8,136,512]{2,1,0:T(8,128)(2,1)}), f16[8,136,512]{2,1,0:T(8,128)(2,1)}, u32[]{:S(2)}, u32[]{:S(2)}) async-start(f16[8,136,512]{2,1,0:T(8,128)(2,1)} %convert_element_type.16), calls=%async_computation | async-start | bytes 2228224 | tf_op jit(solution)/shard_map/all_to_all | solution.py:303
  55.1 0.0 collective-permute-done.6.refs_7_
  55.1 0.0 collective-permute-done.4.refs_5_
  55.1 28.1 %shard_map.60 = bf16[24,512,1024]{2,1,0:T(8,128)(2,1)} custom-call(bf16[128,512]{1,0:T(8,128)(2,1)S(1)} %bitcast.20, bf16[128,512]{1,0:T(8,128)(2,1)S(1)} %collective-permute-done.refs_1_, bf16[128,512]{1,0:T(8,128)(2,1)S(1)} %collective-permute-done.1.refs_2_, bf16[128,512]{1,0:T(8,128)(2,1)S(1)} %collective-permute-done.2.refs_3_, ...), custom_call_target="tpu_custom_call" | custom-call | flops 19327352832 | bytes 25165824 | tf_op jit(solution)/shard_map/pallas_call | solution.py:261
  83.2 0.0 all-to-all-done
  83.2 0.9 %fusion.2 = f32[8,1,512]{2,1,0:T(1,128)S(1)} fusion(f16[8,136,512]{2,1,0:T(8,128)(2,1)} %all-to-all-done), kind=kLoop, calls=%fused_computation.7 | loop fusion | flops 12288 | bytes 24576 | tf_op jit(solution)/shard_map/exp2 | solution.py:305
  84.1 1.4 %multiply_reduce_fusion = bf16[128,512]{1,0:T(8,128)(2,1)S(1)} fusion(f16[8,136,512]{2,1,0:T(8,128)(2,1)} %all-to-all-done, f32[8,512]{1,0:T(8,128)S(1)} %bitcast.25), kind=kLoop, calls=%fused_computation | loop fusion | flops 1507328 | bytes 1196032 | tf_op jit(solution)/shard_map/reduce_sum | solution.py:306
  85.5 0.7 convert_element_type.20
  (5 shorter events, 0.0 us)
Async XLA Ops:
  1.6 7.1 %collective-permute-start.3 = (bf16[128,512]{1,0:T(8,128)(2,1)S(1)}, bf16[128,512]{1,0:T(8,128)(2,1)S(1)}, u32[]{:S(2)}, u32[]{:S(2)}) collective-permute-start(bf16[128,512]{1,0:T(8,128)(2,1)S(1)} %bitcast.21), channel_id=1, source_target_pairs={{0,1},{1,0},{2,3},{3,2},{4,5},{5,4},{6,7},{7,6},{8,9},{9,8},{10,11... | collective-permute-start | bytes 393224 | tf_op jit(solution)/shard_map/ppermute | solution.py:281
  5.5 6.8 %collective-permute-start.2 = (bf16[128,512]{1,0:T(8,128)(2,1)S(1)}, bf16[128,512]{1,0:T(8,128)(2,1)S(1)}, u32[]{:S(2)}, u32[]{:S(2)}) collective-permute-start(bf16[128,512]{1,0:T(8,128)(2,1)S(1)} %bitcast.16), channel_id=1, source_target_pairs={{0,24},{8,16},{16,8},{24,0},{1,25},{9,17},{17,9},{25,1},{2,26},{10... | collective-permute-start | bytes 393224 | tf_op jit(solution)/shard_map/ppermute | solution.py:281
  6.2 8.0 %collective-permute-start.1 = (bf16[128,512]{1,0:T(8,128)(2,1)S(1)}, bf16[128,512]{1,0:T(8,128)(2,1)S(1)}, u32[]{:S(2)}, u32[]{:S(2)}) collective-permute-start(bf16[128,512]{1,0:T(8,128)(2,1)S(1)} %bitcast.17), channel_id=1, source_target_pairs={{0,16},{8,24},{16,0},{24,8},{1,17},{9,25},{17,1},{25,9},{2,18},{10... | collective-permute-start | bytes 393224 | tf_op jit(solution)/shard_map/ppermute | solution.py:281
  7.2 7.0 %collective-permute-start = (bf16[128,512]{1,0:T(8,128)(2,1)S(1)}, bf16[128,512]{1,0:T(8,128)(2,1)S(1)}, u32[]{:S(2)}, u32[]{:S(2)}) collective-permute-start(bf16[128,512]{1,0:T(8,128)(2,1)S(1)} %bitcast.18), channel_id=1, source_target_pairs={{0,8},{8,0},{16,24},{24,16},{1,9},{9,1},{17,25},{25,17},{2,10},{10... | collective-permute-start | bytes 393224 | tf_op jit(solution)/shard_map/ppermute | solution.py:281
  7.4 0.7 copy-start
  8.7 46.4 %collective-permute-start.6 = (bf16[2,128,512]{2,1,0:T(8,128)(2,1)S(1)}, bf16[2,128,512]{2,1,0:T(8,128)(2,1)S(1)}, u32[]{:S(2)}, u32[]{:S(2)}) collective-permute-start(bf16[2,128,512]{2,1,0:T(8,128)(2,1)S(1)} %bitcast.12), channel_id=1, source_target_pairs={{0,6},{1,7},{2,4},{3,5},{4,2},{5,3},{6,0},{7,1},{8,14},{9,15},{10,... | collective-permute-start | bytes 786440 | tf_op jit(solution)/shard_map/ppermute | solution.py:281
  12.3 42.8 %collective-permute-start.5 = (bf16[2,128,512]{2,1,0:T(8,128)(2,1)S(1)}, bf16[2,128,512]{2,1,0:T(8,128)(2,1)S(1)}, u32[]{:S(2)}, u32[]{:S(2)}) collective-permute-start(bf16[2,128,512]{2,1,0:T(8,128)(2,1)S(1)} %bitcast.13), channel_id=1, source_target_pairs={{0,4},{1,5},{2,6},{3,7},{4,0},{5,1},{6,2},{7,3},{8,12},{9,13},{10,... | collective-permute-start | bytes 786440 | tf_op jit(solution)/shard_map/ppermute | solution.py:281
  12.3 42.8 %collective-permute-start.4 = (bf16[2,128,512]{2,1,0:T(8,128)(2,1)S(1)}, bf16[2,128,512]{2,1,0:T(8,128)(2,1)S(1)}, u32[]{:S(2)}, u32[]{:S(2)}) collective-permute-start(bf16[2,128,512]{2,1,0:T(8,128)(2,1)S(1)} %bitcast.14), channel_id=1, source_target_pairs={{0,2},{1,3},{2,0},{3,1},{4,6},{5,7},{6,4},{7,5},{8,10},{9,11},{10,... | collective-permute-start | bytes 786440 | tf_op jit(solution)/shard_map/ppermute | solution.py:281
  50.2 33.0 %all-to-all-start = ((f16[8,136,512]{2,1,0:T(8,128)(2,1)}), f16[8,136,512]{2,1,0:T(8,128)(2,1)}, u32[]{:S(2)}, u32[]{:S(2)}) async-start(f16[8,136,512]{2,1,0:T(8,128)(2,1)} %convert_element_type.16), calls=%async_computation | async-start | bytes 2228224 | tf_op jit(solution)/shard_map/all_to_all | solution.py:303

commit v9 on v6

--- a/solution.py
+++ b/solution.py
@@ -12,6 +12,7 @@
 F32 = jnp.float32
 F8 = jnp.float8_e4m3fn
 MIB = 1024 * 1024
+BACK_GROUP = 6
 GROUP = 4
 TINY = 1e-30
 
@@ -53,6 +54,14 @@
     length = table.shape[1]
     sums = [jnp.sum(jnp.abs(table[k, 0:1, :length].astype(F32)), keepdims=True) for k in range(table.shape[0])]
     return [jnp.maximum(total * gmax, TINY) for total in sums]
+
+
+def interleave(first, second):
+    ratio = -(-len(first) // len(second))
+    for i, work in enumerate(second):
+        for earlier in first[i * ratio : (i + 1) * ratio]:
+            earlier()
+        work()
 
 
 def table_kernel(filters_ref, rows_ref):
@@ -99,17 +108,17 @@
         gmax = functools.reduce(jnp.maximum, [largest(piece[...]) for piece in pieces])
         bounds[...] = jnp.broadcast_to(gmax, bounds.shape)
 
-    matrix = matrix_ref[...].reshape(GROUP * out_width, -1)
+    matrix = matrix_ref[...].reshape(BACK_GROUP * out_width, -1)
     peak = jnp.max(jnp.abs(matrix).reshape(-1, 16, matrix.shape[1]), axis=0)
     matrix_scale = (256.0 / jnp.maximum(largest(peak), TINY)).astype(BF16)
     matrix8 = (matrix * matrix_scale).astype(F8)
-    table = rows_ref[pl.ds(GROUP * step, GROUP)]
+    table = rows_ref[pl.ds(BACK_GROUP * step, BACK_GROUP)]
     reach = functools.reduce(jnp.maximum, reach_of(table, bounds[0:1, 0:1]))
-    table = table.reshape(GROUP * length, 2 * length)
+    table = table.reshape(BACK_GROUP * length, 2 * length)
     for b in range(seqs):
         high, low = split(dot(table, grads[:, b * out_width : (b + 1) * out_width]))
         low = (low * (65536.0 / reach)).astype(F8)
-        for k in range(GROUP):
+        for k in range(BACK_GROUP):
             source, columns = slice(k * length, (k + 1) * length), slice(k * out_width, (k + 1) * out_width)
             parts[b * length : (b + 1) * length, columns] = high[source]
             parts8[b * length : (b + 1) * length, columns] = low[source]
@@ -138,16 +147,16 @@
     return call(
         functools.partial(back_kernel, len(pieces)),
         (4 * count * out_width * in_width * tokens, 2 * matrices.size),
-        40,
+        48,
         out_shape=out,
-        grid=(count // GROUP,),
+        grid=(count // BACK_GROUP,),
         in_specs=[whole(piece) for piece in pieces]
-        + [whole(rows), pl.BlockSpec((GROUP, out_width, in_width), lambda i: (i, 0, 0))],
+        + [whole(rows), pl.BlockSpec((BACK_GROUP, out_width, in_width), lambda i: (i, 0, 0))],
         out_specs=whole(out),
         scratch_shapes=[
             pltpu.VMEM((2 * length, seqs * out_width), BF16),
-            pltpu.VMEM((tokens, GROUP * out_width), BF16),
-            pltpu.VMEM((tokens, GROUP * out_width), F8),
+            pltpu.VMEM((tokens, BACK_GROUP * out_width), BF16),
+            pltpu.VMEM((tokens, BACK_GROUP * out_width), F8),
             pltpu.VMEM((tokens, in_width), F32),
             pltpu.VMEM((8, length), F32),
         ],
@@ -163,6 +172,32 @@
     tokens = inputs.shape[0]
     seqs = tokens // length
     out_width = out_ref.shape[1]
+
+    def table_of(first):
+        table = rows_ref[pl.ds(first, 2)]
+        return table.reshape(2 * length, 2 * length), reach_of(table, bounds[0:1, 0:1])
+
+    def filter_sequence(slot, table, reach, b):
+        filtered = lax.dot_general(
+            grads[b * out_width : (b + 1) * out_width], table, (((1,), (1,)), ((), ())), preferred_element_type=F32
+        )
+        high, low = split(filtered)
+        place = slice(b * length, (b + 1) * length)
+        for k in range(2):
+            columns = slice(k * length, (k + 1) * length)
+            parts[2 * slot + k, :, place] = high[:, columns]
+            parts8[2 * slot + k, :, place] = (low[:, columns] * (65536.0 / reach[k])).astype(F8)
+
+    def filters_of(slot, table, reach):
+        return [functools.partial(filter_sequence, slot, table, reach, b) for b in range(seqs)]
+
+    def product(k, back):
+        total = dot(parts[k], inputs[...]) + dot(parts8[k], inputs8[...]) * back
+        out_ref[k] = total.astype(BF16)
+
+    def products_of(slot, reach):
+        backs = [(reach[k] / 65536.0) * (bounds[1:2, 0:1] / 256.0) for k in range(2)]
+        return [functools.partial(product, 2 * slot + k, backs[k]) for k in range(2)]
 
     @pl.when(step == 0)
     def _():
@@ -185,26 +220,14 @@
                 turned = piece[half].astype(F32).T
                 inputs[:, columns] = turned.astype(BF16)
                 inputs8[:, columns] = (turned * (256.0 / xmax)).astype(F8)
-
-    table = rows_ref[pl.ds(GROUP * step, GROUP)]
-    reach = reach_of(table, bounds[0:1, 0:1])
-    table = table.reshape(GROUP * length, 2 * length)
-    for first in range(0, GROUP, 2):
-        some = table[first * length : (first + 2) * length]
-        for b in range(seqs):
-            place = slice(b * length, (b + 1) * length)
-            filtered = lax.dot_general(
-                grads[b * out_width : (b + 1) * out_width], some, (((1,), (1,)), ((), ())), preferred_element_type=F32
-            )
-            high, low = split(filtered)
-            for k in range(2):
-                columns = slice(k * length, (k + 1) * length)
-                parts[first + k, :, place] = high[:, columns]
-                parts8[first + k, :, place] = (low[:, columns] * (65536.0 / reach[first + k])).astype(F8)
-    for k in range(GROUP):
-        back = (reach[k] / 65536.0) * (bounds[1:2, 0:1] / 256.0)
-        product = dot(parts[k], inputs[...]) + dot(parts8[k], inputs8[...]) * back
-        out_ref[k] = product.astype(BF16)
+        for work in filters_of(0, *table_of(0)):
+            work()
+
+    now = table_of(GROUP * step)
+    late = table_of(GROUP * step + 2)
+    coming = table_of(lax.rem(GROUP * step + GROUP, rows_ref.shape[0]))
+    interleave(filters_of(1, *late), products_of(0, now[1]))
+    interleave(filters_of(0, *coming), products_of(1, late[1]))
 
 
 def matrix_sums(pieces, input_pieces, rows, cout_count, shape):

time: 82.5 us -> 82 us (level)
  no operation moved by 1% of the time
where the time goes in v9:
time: 82 us; the launch traced here: 81.7 us
  Pallas kernels  58.8 us (72%)
  starting transfers between devices  14.3 us (17%)
  other arithmetic  3.61 us (4%)
  local copies, waits for them, and re-layouts  3.25 us (4%)
  waiting for transfers between devices  1.08 us (1%)
    pallas_call x1, Pallas kernels, back_sums(): call(functools.partial(back_kernel, len(pieces)), (4 * count * out_width...  29.6 us
    pallas_call x1, Pallas kernels, matrix_sums(): call(functools.partial(matrix_kernel, len(pieces), len(input_pieces), cou...  28.7 us
    ppermute x7, starting transfers between devices, exchange(): return lax.ppermute(array, axis, [(i, i ^ flip) for i in range(count)])  9.41 us
    all_to_all x1, starting transfers between devices, shards(): came = lax.all_to_all(blocks, 'cout', 0, 0, tiled=True)  4.86 us
    unnamed x5, local copies, waits for them, and re-layouts  2.56 us
  transfers between devices with their start and end apart: 8, of which 1 were waited for; matrix products, arithmetic and copies ran while one was open for 3% of the time, Pallas kernels for 72%

profile of v9, /device:TPU:0, one launch (start us, length us, event | category | flops | bytes accessed | tf_op | source)
XLA Modules:
  0.0 81.7 jit_solution(18111010262594119721)
XLA Ops:
  0.6 0.9 %copy.12 = bf16[16,8,4,128]{3,1,2,0:T(8,128)(2,1)S(1)} copy(bf16[16,8,4,128]{3,2,1,0:T(4,128)(2,1)} %bitcast.23) | data formatting | bytes 262144
  1.6 3.0 %collective-permute-start.3 = (bf16[128,512]{1,0:T(8,128)(2,1)S(1)}, bf16[128,512]{1,0:T(8,128)(2,1)S(1)}, u32[]{:S(2)}, u32[]{:S(2)}) collective-permute-start(bf16[128,512]{1,0:T(8,128)(2,1)S(1)} %bitcast.21), channel_id=1, source_target_pairs={{0,1},{1,0},{2,3},{3,2},{4,5},{5,4},{6,7},{7,6},{8,9},{9,8},{10,11... | collective-permute-start | bytes 393224 | tf_op jit(solution)/shard_map/ppermute | solution.py:258
  4.6 0.9 %copy.13 = bf16[16,8,4,128]{3,1,2,0:T(8,128)(2,1)S(1)} copy(bf16[16,8,4,128]{3,2,1,0:T(4,128)(2,1)} %bitcast.24) | data formatting | bytes 262144
  5.5 0.7 collective-permute-start.2
  6.2 0.9 %collective-permute-start.1 = (bf16[128,512]{1,0:T(8,128)(2,1)S(1)}, bf16[128,512]{1,0:T(8,128)(2,1)S(1)}, u32[]{:S(2)}, u32[]{:S(2)}) collective-permute-start(bf16[128,512]{1,0:T(8,128)(2,1)S(1)} %bitcast.17), channel_id=1, source_target_pairs={{0,16},{8,24},{16,0},{24,8},{1,17},{9,25},{17,1},{25,9},{2,18},{10... | collective-permute-start | bytes 393224 | tf_op jit(solution)/shard_map/ppermute | solution.py:258
  7.2 0.3 collective-permute-start
  7.4 0.7 copy-done
  8.2 0.5 shard_map.59.refs_8_.refs_4_
  8.6 0.0 collective-permute-done.3
  8.7 3.7 %collective-permute-start.6 = (bf16[2,128,512]{2,1,0:T(8,128)(2,1)S(1)}, bf16[2,128,512]{2,1,0:T(8,128)(2,1)S(1)}, u32[]{:S(2)}, u32[]{:S(2)}) collective-permute-start(bf16[2,128,512]{2,1,0:T(8,128)(2,1)S(1)} %bitcast.12), channel_id=1, source_target_pairs={{0,6},{1,7},{2,4},{3,5},{4,2},{5,3},{6,0},{7,1},{8,14},{9,15},{10,... | collective-permute-start | bytes 786440 | tf_op jit(solution)/shard_map/ppermute | solution.py:258
  12.3 0.0 collective-permute-start.5
  12.3 0.0 collective-permute-done.2.refs_3_
  12.3 0.8 collective-permute-start.4
  13.1 1.1 %collective-permute-done.1.refs_2_ = bf16[128,512]{1,0:T(8,128)(2,1)S(1)} collective-permute-done((bf16[128,512]{1,0:T(8,128)(2,1)S(1)}, bf16[128,512]{1,0:T(8,128)(2,1)S(1)}, u32[]{:S(2)}, u32[]{:S(2)}) %collective-permute-start.1) | collective-permute-done | bytes 131104 | tf_op jit(solution)/shard_map/ppermute | solution.py:258
  14.2 0.0 collective-permute-done.refs_1_
  14.2 29.6 %shard_map.61 = f32[8,136,512]{2,1,0:T(8,128)S(1)} custom-call(bf16[128,512]{1,0:T(8,128)(2,1)S(1)} %bitcast.19, bf16[128,512]{1,0:T(8,128)(2,1)S(1)} %collective-permute-done.refs_1_, bf16[128,512]{1,0:T(8,128)(2,1)S(1)} %collective-permute-done.1.refs_2_, bf16[128,512]{1,0:T(8,128)(2,1)S(1)} %collective-permute-done.2.refs_3_, ...), custom_call_target="tpu_custom_call" | custom-call | flops 25769803776 | bytes 25165824 | tf_op jit(solution)/shard_map/pallas_call | solution.py:147
  43.8 1.3 %convert_element_type.16 = f16[8,136,512]{2,1,0:T(8,128)(2,1)} convert(f32[8,136,512]{2,1,0:T(8,128)S(1)} %shard_map.61) | non-fusion elementwise | flops 557056 | bytes 3342336 | tf_op jit(solution)/shard_map/convert_element_type | solution.py:279
  45.1 4.9 %all-to-all-start = ((f16[8,136,512]{2,1,0:T(8,128)(2,1)}), f16[8,136,512]{2,1,0:T(8,128)(2,1)}, u32[]{:S(2)}, u32[]{:S(2)}) async-start(f16[8,136,512]{2,1,0:T(8,128)(2,1)} %convert_element_type.16), calls=%async_computation | async-start | bytes 2228224 | tf_op jit(solution)/shard_map/all_to_all | solution.py:280
  49.9 0.0 collective-permute-done.6.refs_7_
  49.9 0.0 collective-permute-done.5.refs_6_
  50.0 28.7 %shard_map.60 = bf16[24,512,1024]{2,1,0:T(8,128)(2,1)} custom-call(bf16[128,512]{1,0:T(8,128)(2,1)S(1)} %bitcast.20, bf16[128,512]{1,0:T(8,128)(2,1)S(1)} %collective-permute-done.refs_1_, bf16[128,512]{1,0:T(8,128)(2,1)S(1)} %collective-permute-done.1.refs_2_, bf16[128,512]{1,0:T(8,128)(2,1)S(1)} %collective-permute-done.2.refs_3_, ...), custom_call_target="tpu_custom_call" | custom-call | flops 19327352832 | bytes 25165824 | tf_op jit(solution)/shard_map/pallas_call | solution.py:238
  78.7 0.9 %fusion.2 = f32[8,1,512]{2,1,0:T(1,128)S(1)} fusion(f16[8,136,512]{2,1,0:T(8,128)(2,1)} %all-to-all-done), kind=kLoop, calls=%fused_computation.7 | loop fusion | flops 12288 | bytes 24576 | tf_op jit(solution)/shard_map/exp2 | solution.py:282
  79.6 1.4 %multiply_reduce_fusion = bf16[128,512]{1,0:T(8,128)(2,1)S(1)} fusion(f16[8,136,512]{2,1,0:T(8,128)(2,1)} %all-to-all-done, f32[8,512]{1,0:T(8,128)S(1)} %bitcast.25), kind=kLoop, calls=%fused_computation | loop fusion | flops 1507328 | bytes 1196032 | tf_op jit(solution)/shard_map/reduce_sum | solution.py:283
  81.0 0.7 convert_element_type.20
  (5 shorter events, 0.0 us)
Async XLA Ops:
  1.6 7.1 %collective-permute-start.3 = (bf16[128,512]{1,0:T(8,128)(2,1)S(1)}, bf16[128,512]{1,0:T(8,128)(2,1)S(1)}, u32[]{:S(2)}, u32[]{:S(2)}) collective-permute-start(bf16[128,512]{1,0:T(8,128)(2,1)S(1)} %bitcast.21), channel_id=1, source_target_pairs={{0,1},{1,0},{2,3},{3,2},{4,5},{5,4},{6,7},{7,6},{8,9},{9,8},{10,11... | collective-permute-start | bytes 393224 | tf_op jit(solution)/shard_map/ppermute | solution.py:258
  5.5 6.8 %collective-permute-start.2 = (bf16[128,512]{1,0:T(8,128)(2,1)S(1)}, bf16[128,512]{1,0:T(8,128)(2,1)S(1)}, u32[]{:S(2)}, u32[]{:S(2)}) collective-permute-start(bf16[128,512]{1,0:T(8,128)(2,1)S(1)} %bitcast.16), channel_id=1, source_target_pairs={{0,24},{8,16},{16,8},{24,0},{1,25},{9,17},{17,9},{25,1},{2,26},{10... | collective-permute-start | bytes 393224 | tf_op jit(solution)/shard_map/ppermute | solution.py:258
  6.2 8.0 %collective-permute-start.1 = (bf16[128,512]{1,0:T(8,128)(2,1)S(1)}, bf16[128,512]{1,0:T(8,128)(2,1)S(1)}, u32[]{:S(2)}, u32[]{:S(2)}) collective-permute-start(bf16[128,512]{1,0:T(8,128)(2,1)S(1)} %bitcast.17), channel_id=1, source_target_pairs={{0,16},{8,24},{16,0},{24,8},{1,17},{9,25},{17,1},{25,9},{2,18},{10... | collective-permute-start | bytes 393224 | tf_op jit(solution)/shard_map/ppermute | solution.py:258
  7.2 7.0 %collective-permute-start = (bf16[128,512]{1,0:T(8,128)(2,1)S(1)}, bf16[128,512]{1,0:T(8,128)(2,1)S(1)}, u32[]{:S(2)}, u32[]{:S(2)}) collective-permute-start(bf16[128,512]{1,0:T(8,128)(2,1)S(1)} %bitcast.18), channel_id=1, source_target_pairs={{0,8},{8,0},{16,24},{24,16},{1,9},{9,1},{17,25},{25,17},{2,10},{10... | collective-permute-start | bytes 393224 | tf_op jit(solution)/shard_map/ppermute | solution.py:258
  7.4 0.7 copy-start
  8.7 41.3 %collective-permute-start.6 = (bf16[2,128,512]{2,1,0:T(8,128)(2,1)S(1)}, bf16[2,128,512]{2,1,0:T(8,128)(2,1)S(1)}, u32[]{:S(2)}, u32[]{:S(2)}) collective-permute-start(bf16[2,128,512]{2,1,0:T(8,128)(2,1)S(1)} %bitcast.12), channel_id=1, source_target_pairs={{0,6},{1,7},{2,4},{3,5},{4,2},{5,3},{6,0},{7,1},{8,14},{9,15},{10,... | collective-permute-start | bytes 786440 | tf_op jit(solution)/shard_map/ppermute | solution.py:258
  12.3 37.6 %collective-permute-start.5 = (bf16[2,128,512]{2,1,0:T(8,128)(2,1)S(1)}, bf16[2,128,512]{2,1,0:T(8,128)(2,1)S(1)}, u32[]{:S(2)}, u32[]{:S(2)}) collective-permute-start(bf16[2,128,512]{2,1,0:T(8,128)(2,1)S(1)} %bitcast.13), channel_id=1, source_target_pairs={{0,4},{1,5},{2,6},{3,7},{4,0},{5,1},{6,2},{7,3},{8,12},{9,13},{10,... | collective-permute-start | bytes 786440 | tf_op jit(solution)/shard_map/ppermute | solution.py:258
  12.3 37.6 %collective-permute-start.4 = (bf16[2,128,512]{2,1,0:T(8,128)(2,1)S(1)}, bf16[2,128,512]{2,1,0:T(8,128)(2,1)S(1)}, u32[]{:S(2)}, u32[]{:S(2)}) collective-permute-start(bf16[2,128,512]{2,1,0:T(8,128)(2,1)S(1)} %bitcast.14), channel_id=1, source_target_pairs={{0,2},{1,3},{2,0},{3,1},{4,6},{5,7},{6,4},{7,5},{8,10},{9,11},{10,... | collective-permute-start | bytes 786440 | tf_op jit(solution)/shard_map/ppermute | solution.py:258
  45.1 33.6 %all-to-all-start = ((f16[8,136,512]{2,1,0:T(8,128)(2,1)}), f16[8,136,512]{2,1,0:T(8,128)(2,1)}, u32[]{:S(2)}, u32[]{:S(2)}) async-start(f16[8,136,512]{2,1,0:T(8,128)(2,1)} %convert_element_type.16), calls=%async_computation | async-start | bytes 2228224 | tf_op jit(solution)/shard_map/all_to_all | solution.py:280

commit v10 on v8

--- a/solution.py
+++ b/solution.py
@@ -93,21 +93,15 @@
 
 def back_kernel(cin_count, *refs):
     pieces = refs[:cin_count]
-    rows_ref, matrices_ref, out, grads, parts, parts8, total, bounds, blocks, arrived = refs[cin_count:]
+    rows_ref, matrix_ref, out, grads, parts, parts8, total, bounds = refs[cin_count:]
     step = pl.program_id(0)
-    slot = lax.rem(step, 2)
     _, length, _ = rows_ref.shape
-    out_width = matrices_ref.shape[1]
+    out_width = matrix_ref.shape[1]
     seqs = grads.shape[1] // out_width
     tokens = seqs * length
 
-    def fetch(index):
-        target = lax.rem(index, 2)
-        return pltpu.make_async_copy(matrices_ref.at[pl.ds(GROUP * index, GROUP)], blocks.at[target], arrived.at[target])
-
     @pl.when(step == 0)
     def _():
-        fetch(step).start()
         total[...] = jnp.zeros_like(total)
         block = pieces[0].shape[0]
         for b in range(seqs):
@@ -119,14 +113,10 @@
         gmax = functools.reduce(jnp.maximum, [largest(piece[...]) for piece in pieces])
         bounds[...] = jnp.broadcast_to(gmax, bounds.shape)
 
-    @pl.when(step + 1 < pl.num_programs(0))
-    def _():
-        fetch(step + 1).start()
-
-    fetch(step).wait()
-    matrix = blocks[slot].reshape(GROUP * out_width, -1)
+    matrix = matrix_ref[...].reshape(GROUP * out_width, -1)
     peak = jnp.max(jnp.abs(matrix).reshape(-1, 16, matrix.shape[1]), axis=0)
     matrix_scale = (256.0 / jnp.maximum(largest(peak), TINY)).astype(BF16)
+    matrix8 = (matrix * matrix_scale).astype(F8)
     table = rows_ref[pl.ds(GROUP * step, GROUP)]
     reach = functools.reduce(jnp.maximum, reach_of(table, bounds[0:1, 0:1]))
     table = table.reshape(GROUP * length, 2 * length)
@@ -138,22 +128,24 @@
             parts[b * length : (b + 1) * length, columns] = high[source]
             parts8[b * length : (b + 1) * length, columns] = low[source]
     back = (reach / 65536.0) / matrix_scale.astype(F32)
-    for columns in chunks(total.shape[1]):
-        matrix = blocks[slot, :, :, columns].reshape(GROUP * out_width, -1)
-        matrix8 = (matrix * matrix_scale).astype(F8)
-        total[:, columns] += dot(parts[...], matrix) + dot(parts8[...], matrix8) * back
+    total[...] += dot(parts[...], matrix) + dot(parts8[...], matrix8) * back
 
     @pl.when(step == pl.num_programs(0) - 1)
     def _():
         summed = total[...]
         exponent = jnp.floor(jnp.log2(jnp.maximum(largest(summed), TINY))) + 1.0
         summed = summed * jnp.exp2(14.0 - exponent)
-        block = out.shape[1] - 8
-        turned = [] if block % 128 == 0 else [summed.T]
-        for j in range(out.shape[0]):
-            place = slice(j * block, (j + 1) * block)
-            out[j, :block] = turned[0][place] if turned else summed[:, place].T
-            out[j, block:] = jnp.broadcast_to(exponent, (8, tokens))
+        if out.shape[1] == tokens + 8:
+            block = out.shape[2]
+            for j in range(out.shape[0]):
+                out[j, :tokens] = summed[:, j * block : (j + 1) * block]
+                out[j, tokens:] = jnp.broadcast_to(exponent, (8, block))
+        else:
+            block = out.shape[1] - 8
+            turned = summed.T
+            for j in range(out.shape[0]):
+                out[j, :block] = turned[j * block : (j + 1) * block]
+                out[j, block:] = jnp.broadcast_to(exponent, (8, tokens))
 
 
 def back_sums(pieces, rows, matrices, cout):
@@ -161,7 +153,9 @@
     length = rows.shape[1]
     tokens = pieces[0].shape[1]
     seqs = tokens // length
-    out = jax.ShapeDtypeStruct((cout, in_width // cout + 8, tokens), F32)
+    own = in_width // cout
+    shape = (tokens + 8, own) if own % 128 == 0 else (own + 8, tokens)
+    out = jax.ShapeDtypeStruct((cout, *shape), F32)
     return call(
         functools.partial(back_kernel, len(pieces)),
         (4 * count * out_width * in_width * tokens, 2 * matrices.size),
@@ -169,7 +163,7 @@
         out_shape=out,
         grid=(count // GROUP,),
         in_specs=[whole(piece) for piece in pieces]
-        + [whole(rows), pl.BlockSpec(memory_space=pl.ANY)],
+        + [whole(rows), pl.BlockSpec((GROUP, out_width, in_width), lambda i: (i, 0, 0))],
         out_specs=whole(out),
         scratch_shapes=[
             pltpu.VMEM((2 * length, seqs * out_width), BF16),
@@ -177,8 +171,6 @@
             pltpu.VMEM((tokens, GROUP * out_width), F8),
             pltpu.VMEM((tokens, in_width), F32),
             pltpu.VMEM((8, length), F32),
-            pltpu.VMEM((2, GROUP, out_width, in_width), BF16),
-            pltpu.SemaphoreType.DMA((2,)),
         ],
     )(*pieces, rows, matrices)
 
@@ -302,8 +294,11 @@
     blocks = back_sums(pieces, rows, matrices, cout).astype(F16)
     came = lax.all_to_all(blocks, "cout", 0, 0, tiled=True)
     matrix_grads = matrix_sums(pieces, input_pieces, rows, cout_count, matrices.shape)
-    scales = jnp.exp2(came[:, own : own + 1].astype(F32) - 14.0)
-    input_grads = jnp.sum(came[:, :own].astype(F32) * scales, axis=0).astype(BF16)
+    rows = came.shape[1] - 8
+    scales = jnp.exp2(came[:, rows : rows + 1].astype(F32) - 14.0)
+    input_grads = jnp.sum(came[:, :rows].astype(F32) * scales, axis=0).astype(BF16)
+    if rows == tokens:
+        input_grads = input_grads.reshape(seq_count, length, own).transpose(2, 0, 1)
     return (matrix_grads, input_grads.reshape(own, seq_count, length))
 
 

time: 86.6 us -> 81.1 us (0.936)
  Pallas kernels: 63.3 us -> 58 us
    pallas_call x1, Pallas kernels: 34.7 us -> 29.4 us  [back_sums(): call(functools.partial(back_kernel, len(pieces)), (4 * count * out_width...]
    unnamed x5 -> x4, local copies, waits for them, and re-layouts: 2.56 us -> 2.55 us
  transfers between devices with their start and end apart: 8 -> 8, of which waited for: 1 -> 1; matrix products, arithmetic and copies ran while one was open for 3% -> 3% of each run, Pallas kernels for 73% -> 72%
where the time goes in v10:
time: 81.1 us; the launch traced here: 80.7 us
  Pallas kernels  58 us (72%)
  starting transfers between devices  14.3 us (18%)
  other arithmetic  3.36 us (4%)
  local copies, waits for them, and re-layouts  3.34 us (4%)
  waiting for transfers between devices  1.08 us (1%)
    pallas_call x1, Pallas kernels, back_sums(): call(functools.partial(back_kernel, len(pieces)), (4 * count * out_width...  29.4 us
    pallas_call x1, Pallas kernels, matrix_sums(): call(functools.partial(matrix_kernel, len(pieces), len(input_pieces), cou...  28.1 us
    ppermute x7, starting transfers between devices, exchange(): return lax.ppermute(array, axis, [(i, i ^ flip) for i in range(count)])  9.41 us
    all_to_all x1, starting transfers between devices, shards(): came = lax.all_to_all(blocks, 'cout', 0, 0, tiled=True)  4.87 us
    unnamed x4, local copies, waits for them, and re-layouts  2.55 us
  transfers between devices with their start and end apart: 8, of which 1 were waited for; matrix products, arithmetic and copies ran while one was open for 3% of the time, Pallas kernels for 72%

profile of v10, /device:TPU:0, one launch (start us, length us, event | category | flops | bytes accessed | tf_op | source)
XLA Modules:
  0.0 80.7 jit_solution(16789303083797865993)
XLA Ops:
  0.6 0.9 %copy.12 = bf16[16,8,4,128]{3,1,2,0:T(8,128)(2,1)S(1)} copy(bf16[16,8,4,128]{3,2,1,0:T(4,128)(2,1)} %bitcast.24) | data formatting | bytes 262144
  1.6 3.0 %collective-permute-start.3 = (bf16[128,512]{1,0:T(8,128)(2,1)S(1)}, bf16[128,512]{1,0:T(8,128)(2,1)S(1)}, u32[]{:S(2)}, u32[]{:S(2)}) collective-permute-start(bf16[128,512]{1,0:T(8,128)(2,1)S(1)} %bitcast.22), channel_id=1, source_target_pairs={{0,1},{1,0},{2,3},{3,2},{4,5},{5,4},{6,7},{7,6},{8,9},{9,8},{10,11... | collective-permute-start | bytes 393224 | tf_op jit(solution)/shard_map/ppermute | solution.py:273
  4.6 0.9 %copy.13 = bf16[16,8,4,128]{3,1,2,0:T(8,128)(2,1)S(1)} copy(bf16[16,8,4,128]{3,2,1,0:T(4,128)(2,1)} %bitcast.25) | data formatting | bytes 262144
  5.5 0.7 collective-permute-start.2
  6.2 0.9 %collective-permute-start.1 = (bf16[128,512]{1,0:T(8,128)(2,1)S(1)}, bf16[128,512]{1,0:T(8,128)(2,1)S(1)}, u32[]{:S(2)}, u32[]{:S(2)}) collective-permute-start(bf16[128,512]{1,0:T(8,128)(2,1)S(1)} %bitcast.17), channel_id=1, source_target_pairs={{0,16},{8,24},{16,0},{24,8},{1,17},{9,25},{17,1},{25,9},{2,18},{10... | collective-permute-start | bytes 393224 | tf_op jit(solution)/shard_map/ppermute | solution.py:273
  7.2 0.3 collective-permute-start
  7.4 0.7 copy-done
  8.2 0.5 shard_map.59.refs_8_.refs_4_
  8.6 0.0 collective-permute-done.3
  8.7 3.7 %collective-permute-start.6 = (bf16[2,128,512]{2,1,0:T(8,128)(2,1)S(1)}, bf16[2,128,512]{2,1,0:T(8,128)(2,1)S(1)}, u32[]{:S(2)}, u32[]{:S(2)}) collective-permute-start(bf16[2,128,512]{2,1,0:T(8,128)(2,1)S(1)} %bitcast.12), channel_id=1, source_target_pairs={{0,6},{1,7},{2,4},{3,5},{4,2},{5,3},{6,0},{7,1},{8,14},{9,15},{10,... | collective-permute-start | bytes 786440 | tf_op jit(solution)/shard_map/ppermute | solution.py:273
  12.3 0.0 collective-permute-start.5
  12.3 0.0 collective-permute-done.2.refs_3_
  12.3 0.8 collective-permute-start.4
  13.1 1.1 %collective-permute-done.1.refs_2_ = bf16[128,512]{1,0:T(8,128)(2,1)S(1)} collective-permute-done((bf16[128,512]{1,0:T(8,128)(2,1)S(1)}, bf16[128,512]{1,0:T(8,128)(2,1)S(1)}, u32[]{:S(2)}, u32[]{:S(2)}) %collective-permute-start.1) | collective-permute-done | bytes 131104 | tf_op jit(solution)/shard_map/ppermute | solution.py:273
  14.2 29.4 %shard_map.61 = f32[8,520,128]{2,1,0:T(8,128)S(1)} custom-call(bf16[128,512]{1,0:T(8,128)(2,1)S(1)} %bitcast.19, bf16[128,512]{1,0:T(8,128)(2,1)S(1)} %collective-permute-done.refs_1_, bf16[128,512]{1,0:T(8,128)(2,1)S(1)} %collective-permute-done.1.refs_2_, bf16[128,512]{1,0:T(8,128)(2,1)S(1)} %collective-permute-done.2.refs_3_, ...), custom_call_target="tpu_custom_call" | custom-call | flops 25769803776 | bytes 25165824 | tf_op jit(solution)/shard_map/pallas_call | solution.py:159
  43.6 1.2 %convert_element_type.16 = f16[8,520,128]{2,1,0:T(8,128)(2,1)} convert(f32[8,520,128]{2,1,0:T(8,128)S(1)} %shard_map.61) | non-fusion elementwise | flops 532480 | bytes 3194880 | tf_op jit(solution)/shard_map/convert_element_type | solution.py:294
  44.8 4.9 %all-to-all-start = ((f16[8,520,128]{2,1,0:T(8,128)(2,1)}), f16[8,520,128]{2,1,0:T(8,128)(2,1)}, u32[]{:S(2)}, u32[]{:S(2)}) async-start(f16[8,520,128]{2,1,0:T(8,128)(2,1)} %convert_element_type.16), calls=%async_computation | async-start | bytes 2129920 | tf_op jit(solution)/shard_map/all_to_all | solution.py:295
  49.7 0.0 collective-permute-done.6.refs_7_
  49.7 0.0 collective-permute-done.4.refs_5_
  49.7 28.1 %shard_map.60 = bf16[24,512,1024]{2,1,0:T(8,128)(2,1)} custom-call(bf16[128,512]{1,0:T(8,128)(2,1)S(1)} %bitcast.20, bf16[128,512]{1,0:T(8,128)(2,1)S(1)} %collective-permute-done.refs_1_, bf16[128,512]{1,0:T(8,128)(2,1)S(1)} %collective-permute-done.1.refs_2_, bf16[128,512]{1,0:T(8,128)(2,1)S(1)} %collective-permute-done.2.refs_3_, ...), custom_call_target="tpu_custom_call" | custom-call | flops 19327352832 | bytes 25165824 | tf_op jit(solution)/shard_map/pallas_call | solution.py:253
  77.8 0.0 all-to-all-done
  77.8 0.7 fusion.2
  78.5 1.4 %multiply_reduce_fusion = bf16[512,128]{1,0:T(8,128)(2,1)S(1)} fusion(f16[8,520,128]{2,1,0:T(8,128)(2,1)} %all-to-all-done, f32[8,128]{1,0:T(8,128)S(1)} %bitcast.27), kind=kLoop, calls=%fused_computation | loop fusion | flops 1507328 | bytes 1183744 | tf_op jit(solution)/shard_map/reduce_sum | solution.py:299
  79.9 0.8 copy.7
  (4 shorter events, 0.0 us)
Async XLA Ops:
  1.6 7.1 %collective-permute-start.3 = (bf16[128,512]{1,0:T(8,128)(2,1)S(1)}, bf16[128,512]{1,0:T(8,128)(2,1)S(1)}, u32[]{:S(2)}, u32[]{:S(2)}) collective-permute-start(bf16[128,512]{1,0:T(8,128)(2,1)S(1)} %bitcast.22), channel_id=1, source_target_pairs={{0,1},{1,0},{2,3},{3,2},{4,5},{5,4},{6,7},{7,6},{8,9},{9,8},{10,11... | collective-permute-start | bytes 393224 | tf_op jit(solution)/shard_map/ppermute | solution.py:273
  5.5 6.8 %collective-permute-start.2 = (bf16[128,512]{1,0:T(8,128)(2,1)S(1)}, bf16[128,512]{1,0:T(8,128)(2,1)S(1)}, u32[]{:S(2)}, u32[]{:S(2)}) collective-permute-start(bf16[128,512]{1,0:T(8,128)(2,1)S(1)} %bitcast.16), channel_id=1, source_target_pairs={{0,24},{8,16},{16,8},{24,0},{1,25},{9,17},{17,9},{25,1},{2,26},{10... | collective-permute-start | bytes 393224 | tf_op jit(solution)/shard_map/ppermute | solution.py:273
  6.2 8.0 %collective-permute-start.1 = (bf16[128,512]{1,0:T(8,128)(2,1)S(1)}, bf16[128,512]{1,0:T(8,128)(2,1)S(1)}, u32[]{:S(2)}, u32[]{:S(2)}) collective-permute-start(bf16[128,512]{1,0:T(8,128)(2,1)S(1)} %bitcast.17), channel_id=1, source_target_pairs={{0,16},{8,24},{16,0},{24,8},{1,17},{9,25},{17,1},{25,9},{2,18},{10... | collective-permute-start | bytes 393224 | tf_op jit(solution)/shard_map/ppermute | solution.py:273
  7.2 7.0 %collective-permute-start = (bf16[128,512]{1,0:T(8,128)(2,1)S(1)}, bf16[128,512]{1,0:T(8,128)(2,1)S(1)}, u32[]{:S(2)}, u32[]{:S(2)}) collective-permute-start(bf16[128,512]{1,0:T(8,128)(2,1)S(1)} %bitcast.18), channel_id=1, source_target_pairs={{0,8},{8,0},{16,24},{24,16},{1,9},{9,1},{17,25},{25,17},{2,10},{10... | collective-permute-start | bytes 393224 | tf_op jit(solution)/shard_map/ppermute | solution.py:273
  7.4 0.7 copy-start
  8.7 41.0 %collective-permute-start.6 = (bf16[2,128,512]{2,1,0:T(8,128)(2,1)S(1)}, bf16[2,128,512]{2,1,0:T(8,128)(2,1)S(1)}, u32[]{:S(2)}, u32[]{:S(2)}) collective-permute-start(bf16[2,128,512]{2,1,0:T(8,128)(2,1)S(1)} %bitcast.12), channel_id=1, source_target_pairs={{0,6},{1,7},{2,4},{3,5},{4,2},{5,3},{6,0},{7,1},{8,14},{9,15},{10,... | collective-permute-start | bytes 786440 | tf_op jit(solution)/shard_map/ppermute | solution.py:273
  12.3 37.3 %collective-permute-start.5 = (bf16[2,128,512]{2,1,0:T(8,128)(2,1)S(1)}, bf16[2,128,512]{2,1,0:T(8,128)(2,1)S(1)}, u32[]{:S(2)}, u32[]{:S(2)}) collective-permute-start(bf16[2,128,512]{2,1,0:T(8,128)(2,1)S(1)} %bitcast.13), channel_id=1, source_target_pairs={{0,4},{1,5},{2,6},{3,7},{4,0},{5,1},{6,2},{7,3},{8,12},{9,13},{10,... | collective-permute-start | bytes 786440 | tf_op jit(solution)/shard_map/ppermute | solution.py:273
  12.3 37.3 %collective-permute-start.4 = (bf16[2,128,512]{2,1,0:T(8,128)(2,1)S(1)}, bf16[2,128,512]{2,1,0:T(8,128)(2,1)S(1)}, u32[]{:S(2)}, u32[]{:S(2)}) collective-permute-start(bf16[2,128,512]{2,1,0:T(8,128)(2,1)S(1)} %bitcast.14), channel_id=1, source_target_pairs={{0,2},{1,3},{2,0},{3,1},{4,6},{5,7},{6,4},{7,5},{8,10},{9,11},{10,... | collective-permute-start | bytes 786440 | tf_op jit(solution)/shard_map/ppermute | solution.py:273
  44.8 33.0 %all-to-all-start = ((f16[8,520,128]{2,1,0:T(8,128)(2,1)}), f16[8,520,128]{2,1,0:T(8,128)(2,1)}, u32[]{:S(2)}, u32[]{:S(2)}) async-start(f16[8,520,128]{2,1,0:T(8,128)(2,1)} %convert_element_type.16), calls=%async_computation | async-start | bytes 2129920 | tf_op jit(solution)/shard_map/all_to_all | solution.py:295

commit v11 on v10

--- a/solution.py
+++ b/solution.py
@@ -229,13 +229,12 @@
         xmax = jnp.maximum(xmax, TINY)
         bounds[0:1, :] = jnp.broadcast_to(gmax, (1, length))
         bounds[1:2, :] = jnp.broadcast_to(xmax, (1, length))
-        block = input_pieces[0].shape[1]
+        block = input_pieces[0].shape[2]
         for r, piece in enumerate(input_pieces):
             for half in range(piece.shape[0]):
                 columns = spot("cout", 2 * r + half, block, cout_count)
-                turned = piece[half].astype(F32).T
-                inputs[:, columns] = turned.astype(BF16)
-                inputs8[:, columns] = (turned * (256.0 / xmax)).astype(F8)
+                inputs[:, columns] = piece[half]
+                inputs8[:, columns] = (piece[half].astype(F32) * (256.0 / xmax)).astype(F8)
         interleave(filters_of(0, *table_of(0)), [])
 
     now = table_of(GROUP * step)
@@ -282,12 +281,12 @@
     else:
         pieces = [flat_grads] + [exchange(flat_grads, "cin", cin, flip) for flip in range(1, cin)]
     rows = make_tables(lax.optimization_barrier((filters, flat_grads))[0])
-    flat_inputs = inputs.reshape(-1, tokens)
+    turned = inputs.transpose(1, 2, 0).reshape(tokens, own)
     if cout < 2 or cout & (cout - 1) or own % 128:
-        input_pieces = [lax.all_gather(flat_inputs, "cout", axis=0, tiled=True)[None]]
+        input_pieces = [lax.all_gather(turned, "cout", axis=1, tiled=True)[None]]
         cout_count = 1
     else:
-        both = jnp.concatenate([flat_inputs, exchange(flat_inputs, "cout", cout, 1)]).reshape(2, own, tokens)
+        both = jnp.concatenate([turned, exchange(turned, "cout", cout, 1)]).reshape(2, tokens, own)
         input_pieces = [both] + [exchange(both, "cout", cout, flip) for flip in range(2, cout, 2)]
         cout_count = cout
 

time: 81.1 us -> 81.3 us (level)
    reshape x0 -> x1, local copies, waits for them, and re-layouts: none -> 1.03 us  [shards(): turned = inputs.transpose(1, 2, 0).reshape(tokens, own)]
    unnamed x4 -> x3, local copies, waits for them, and re-layouts: 2.55 us -> 1.63 us
where the time goes in v11:
time: 81.3 us; the launch traced here: 81 us
  Pallas kernels  58.1 us (71%)
  starting transfers between devices  14.3 us (18%)
  local copies, waits for them, and re-layouts  3.45 us (4%)
  other arithmetic  3.36 us (4%)
  waiting for transfers between devices  1.08 us (1%)
    pallas_call x1, Pallas kernels, back_sums(): call(functools.partial(back_kernel, len(pieces)), (4 * count * out_width...  29.4 us
    pallas_call x1, Pallas kernels, matrix_sums(): call(functools.partial(matrix_kernel, len(pieces), len(input_pieces), cou...  28.2 us
    ppermute x7, starting transfers between devices, exchange(): return lax.ppermute(array, axis, [(i, i ^ flip) for i in range(count)])  9.41 us
    all_to_all x1, starting transfers between devices, shards(): came = lax.all_to_all(blocks, 'cout', 0, 0, tiled=True)  4.86 us
    unnamed x3, local copies, waits for them, and re-layouts  1.63 us
  transfers between devices with their start and end apart: 8, of which 1 were waited for; matrix products, arithmetic and copies ran while one was open for 3% of the time, Pallas kernels for 72%

profile of v11, /device:TPU:0, one launch (start us, length us, event | category | flops | bytes accessed | tf_op | source)
XLA Modules:
  0.0 81.0 jit_solution(17108852429198972325)
XLA Ops:
  0.6 1.0 %copy.14 = bf16[4,128,128]{2,1,0:T(8,128)(2,1)S(1)} copy(bf16[4,128,128]{1,0,2:T(4,128)(2,1)} %bitcast.22) | data formatting | bytes 262144 | tf_op jit(solution)/shard_map/reshape | solution.py:284
  1.7 3.0 %collective-permute-start.3 = (bf16[512,128]{1,0:T(8,128)(2,1)S(1)}, bf16[512,128]{1,0:T(8,128)(2,1)S(1)}, u32[]{:S(2)}, u32[]{:S(2)}) collective-permute-start(bf16[512,128]{1,0:T(8,128)(2,1)S(1)} %bitcast.20), channel_id=1, source_target_pairs={{0,1},{1,0},{2,3},{3,2},{4,5},{5,4},{6,7},{7,6},{8,9},{9,8},{10,11... | collective-permute-start | bytes 393224 | tf_op jit(solution)/shard_map/ppermute | solution.py:272
  4.7 0.9 %copy.17 = bf16[16,8,4,128]{3,1,2,0:T(8,128)(2,1)S(1)} copy(bf16[16,8,4,128]{3,2,1,0:T(4,128)(2,1)} %bitcast.23) | data formatting | bytes 262144
  5.6 0.7 collective-permute-start.2
  6.3 0.9 %collective-permute-start.1 = (bf16[128,512]{1,0:T(8,128)(2,1)S(1)}, bf16[128,512]{1,0:T(8,128)(2,1)S(1)}, u32[]{:S(2)}, u32[]{:S(2)}) collective-permute-start(bf16[128,512]{1,0:T(8,128)(2,1)S(1)} %bitcast.15), channel_id=1, source_target_pairs={{0,16},{8,24},{16,0},{24,8},{1,17},{9,25},{17,1},{25,9},{2,18},{10... | collective-permute-start | bytes 393224 | tf_op jit(solution)/shard_map/ppermute | solution.py:272
  7.3 0.3 collective-permute-start
  7.6 0.7 copy-done
  8.3 0.5 shard_map.59.refs_8_.refs_4_
  8.7 0.0 collective-permute-done.3
  8.8 3.7 %collective-permute-start.6 = (bf16[2,512,128]{2,1,0:T(8,128)(2,1)S(1)}, bf16[2,512,128]{2,1,0:T(8,128)(2,1)S(1)}, u32[]{:S(2)}, u32[]{:S(2)}) collective-permute-start(bf16[2,512,128]{2,1,0:T(8,128)(2,1)S(1)} %bitcast.10), channel_id=1, source_target_pairs={{0,6},{1,7},{2,4},{3,5},{4,2},{5,3},{6,0},{7,1},{8,14},{9,15},{10,... | collective-permute-start | bytes 786440 | tf_op jit(solution)/shard_map/ppermute | solution.py:272
  12.4 0.0 collective-permute-start.5
  12.4 0.0 collective-permute-done.2.refs_3_
  12.5 0.8 collective-permute-start.4
  13.2 1.1 %collective-permute-done.1.refs_2_ = bf16[128,512]{1,0:T(8,128)(2,1)S(1)} collective-permute-done((bf16[128,512]{1,0:T(8,128)(2,1)S(1)}, bf16[128,512]{1,0:T(8,128)(2,1)S(1)}, u32[]{:S(2)}, u32[]{:S(2)}) %collective-permute-start.1) | collective-permute-done | bytes 131104 | tf_op jit(solution)/shard_map/ppermute | solution.py:272
  14.3 29.4 %shard_map.61 = f32[8,520,128]{2,1,0:T(8,128)S(1)} custom-call(bf16[128,512]{1,0:T(8,128)(2,1)S(1)} %bitcast.17, bf16[128,512]{1,0:T(8,128)(2,1)S(1)} %collective-permute-done.refs_1_, bf16[128,512]{1,0:T(8,128)(2,1)S(1)} %collective-permute-done.1.refs_2_, bf16[128,512]{1,0:T(8,128)(2,1)S(1)} %collective-permute-done.2.refs_3_, ...), custom_call_target="tpu_custom_call" | custom-call | flops 25769803776 | bytes 25165824 | tf_op jit(solution)/shard_map/pallas_call | solution.py:159
  43.7 1.2 %convert_element_type.16 = f16[8,520,128]{2,1,0:T(8,128)(2,1)} convert(f32[8,520,128]{2,1,0:T(8,128)S(1)} %shard_map.61) | non-fusion elementwise | flops 532480 | bytes 3194880 | tf_op jit(solution)/shard_map/convert_element_type | solution.py:293
  44.9 4.9 %all-to-all-start = ((f16[8,520,128]{2,1,0:T(8,128)(2,1)}), f16[8,520,128]{2,1,0:T(8,128)(2,1)}, u32[]{:S(2)}, u32[]{:S(2)}) async-start(f16[8,520,128]{2,1,0:T(8,128)(2,1)} %convert_element_type.16), calls=%async_computation | async-start | bytes 2129920 | tf_op jit(solution)/shard_map/all_to_all | solution.py:294
  49.8 0.0 collective-permute-done.6.refs_7_
  49.8 0.0 collective-permute-done.4.refs_5_
  49.8 28.2 %shard_map.60 = bf16[24,512,1024]{2,1,0:T(8,128)(2,1)} custom-call(bf16[128,512]{1,0:T(8,128)(2,1)S(1)} %bitcast.18, bf16[128,512]{1,0:T(8,128)(2,1)S(1)} %collective-permute-done.refs_1_, bf16[128,512]{1,0:T(8,128)(2,1)S(1)} %collective-permute-done.1.refs_2_, bf16[128,512]{1,0:T(8,128)(2,1)S(1)} %collective-permute-done.2.refs_3_, ...), custom_call_target="tpu_custom_call" | custom-call | flops 19327352832 | bytes 25165824 | tf_op jit(solution)/shard_map/pallas_call | solution.py:252
  78.0 0.0 all-to-all-done
  78.0 0.7 fusion.2
  78.7 1.4 %multiply_reduce_fusion = bf16[512,128]{1,0:T(8,128)(2,1)S(1)} fusion(f16[8,520,128]{2,1,0:T(8,128)(2,1)} %all-to-all-done, f32[8,128]{1,0:T(8,128)S(1)} %bitcast.25), kind=kLoop, calls=%fused_computation | loop fusion | flops 1507328 | bytes 1183744 | tf_op jit(solution)/shard_map/reduce_sum | solution.py:298
  80.2 0.8 copy.13
  (4 shorter events, 0.0 us)
Async XLA Ops:
  1.7 7.1 %collective-permute-start.3 = (bf16[512,128]{1,0:T(8,128)(2,1)S(1)}, bf16[512,128]{1,0:T(8,128)(2,1)S(1)}, u32[]{:S(2)}, u32[]{:S(2)}) collective-permute-start(bf16[512,128]{1,0:T(8,128)(2,1)S(1)} %bitcast.20), channel_id=1, source_target_pairs={{0,1},{1,0},{2,3},{3,2},{4,5},{5,4},{6,7},{7,6},{8,9},{9,8},{10,11... | collective-permute-start | bytes 393224 | tf_op jit(solution)/shard_map/ppermute | solution.py:272
  5.6 6.8 %collective-permute-start.2 = (bf16[128,512]{1,0:T(8,128)(2,1)S(1)}, bf16[128,512]{1,0:T(8,128)(2,1)S(1)}, u32[]{:S(2)}, u32[]{:S(2)}) collective-permute-start(bf16[128,512]{1,0:T(8,128)(2,1)S(1)} %bitcast.14), channel_id=1, source_target_pairs={{0,24},{8,16},{16,8},{24,0},{1,25},{9,17},{17,9},{25,1},{2,26},{10... | collective-permute-start | bytes 393224 | tf_op jit(solution)/shard_map/ppermute | solution.py:272
  6.3 8.0 %collective-permute-start.1 = (bf16[128,512]{1,0:T(8,128)(2,1)S(1)}, bf16[128,512]{1,0:T(8,128)(2,1)S(1)}, u32[]{:S(2)}, u32[]{:S(2)}) collective-permute-start(bf16[128,512]{1,0:T(8,128)(2,1)S(1)} %bitcast.15), channel_id=1, source_target_pairs={{0,16},{8,24},{16,0},{24,8},{1,17},{9,25},{17,1},{25,9},{2,18},{10... | collective-permute-start | bytes 393224 | tf_op jit(solution)/shard_map/ppermute | solution.py:272
  7.3 7.0 %collective-permute-start = (bf16[128,512]{1,0:T(8,128)(2,1)S(1)}, bf16[128,512]{1,0:T(8,128)(2,1)S(1)}, u32[]{:S(2)}, u32[]{:S(2)}) collective-permute-start(bf16[128,512]{1,0:T(8,128)(2,1)S(1)} %bitcast.16), channel_id=1, source_target_pairs={{0,8},{8,0},{16,24},{24,16},{1,9},{9,1},{17,25},{25,17},{2,10},{10... | collective-permute-start | bytes 393224 | tf_op jit(solution)/shard_map/ppermute | solution.py:272
  7.6 0.7 copy-start
  8.8 41.0 %collective-permute-start.6 = (bf16[2,512,128]{2,1,0:T(8,128)(2,1)S(1)}, bf16[2,512,128]{2,1,0:T(8,128)(2,1)S(1)}, u32[]{:S(2)}, u32[]{:S(2)}) collective-permute-start(bf16[2,512,128]{2,1,0:T(8,128)(2,1)S(1)} %bitcast.10), channel_id=1, source_target_pairs={{0,6},{1,7},{2,4},{3,5},{4,2},{5,3},{6,0},{7,1},{8,14},{9,15},{10,... | collective-permute-start | bytes 786440 | tf_op jit(solution)/shard_map/ppermute | solution.py:272
  12.4 37.3 %collective-permute-start.5 = (bf16[2,512,128]{2,1,0:T(8,128)(2,1)S(1)}, bf16[2,512,128]{2,1,0:T(8,128)(2,1)S(1)}, u32[]{:S(2)}, u32[]{:S(2)}) collective-permute-start(bf16[2,512,128]{2,1,0:T(8,128)(2,1)S(1)} %bitcast.11), channel_id=1, source_target_pairs={{0,4},{1,5},{2,6},{3,7},{4,0},{5,1},{6,2},{7,3},{8,12},{9,13},{10,... | collective-permute-start | bytes 786440 | tf_op jit(solution)/shard_map/ppermute | solution.py:272
  12.5 37.3 %collective-permute-start.4 = (bf16[2,512,128]{2,1,0:T(8,128)(2,1)S(1)}, bf16[2,512,128]{2,1,0:T(8,128)(2,1)S(1)}, u32[]{:S(2)}, u32[]{:S(2)}) collective-permute-start(bf16[2,512,128]{2,1,0:T(8,128)(2,1)S(1)} %bitcast.12), channel_id=1, source_target_pairs={{0,2},{1,3},{2,0},{3,1},{4,6},{5,7},{6,4},{7,5},{8,10},{9,11},{10,... | collective-permute-start | bytes 786440 | tf_op jit(solution)/shard_map/ppermute | solution.py:272
  44.9 33.1 %all-to-all-start = ((f16[8,520,128]{2,1,0:T(8,128)(2,1)}), f16[8,520,128]{2,1,0:T(8,128)(2,1)}, u32[]{:S(2)}, u32[]{:S(2)}) async-start(f16[8,520,128]{2,1,0:T(8,128)(2,1)} %convert_element_type.16), calls=%async_computation | async-start | bytes 2129920 | tf_op jit(solution)/shard_map/all_to_all | solution.py:294

commit v12 on v10

--- a/solution.py
+++ b/solution.py
@@ -93,7 +93,7 @@
 
 def back_kernel(cin_count, *refs):
     pieces = refs[:cin_count]
-    rows_ref, matrix_ref, out, grads, parts, parts8, total, bounds = refs[cin_count:]
+    rows_ref, matrix_ref, out, grads, parts, parts8, total, bounds, matrix8 = refs[cin_count:]
     step = pl.program_id(0)
     _, length, _ = rows_ref.shape
     out_width = matrix_ref.shape[1]
@@ -113,10 +113,6 @@
         gmax = functools.reduce(jnp.maximum, [largest(piece[...]) for piece in pieces])
         bounds[...] = jnp.broadcast_to(gmax, bounds.shape)
 
-    matrix = matrix_ref[...].reshape(GROUP * out_width, -1)
-    peak = jnp.max(jnp.abs(matrix).reshape(-1, 16, matrix.shape[1]), axis=0)
-    matrix_scale = (256.0 / jnp.maximum(largest(peak), TINY)).astype(BF16)
-    matrix8 = (matrix * matrix_scale).astype(F8)
     table = rows_ref[pl.ds(GROUP * step, GROUP)]
     reach = functools.reduce(jnp.maximum, reach_of(table, bounds[0:1, 0:1]))
     table = table.reshape(GROUP * length, 2 * length)
@@ -127,8 +123,14 @@
             source, columns = slice(k * length, (k + 1) * length), slice(k * out_width, (k + 1) * out_width)
             parts[b * length : (b + 1) * length, columns] = high[source]
             parts8[b * length : (b + 1) * length, columns] = low[source]
+        if b == 0:
+            peak = jnp.max(jnp.abs(matrix_ref[...]).reshape(-1, 16, matrix_ref.shape[2]), axis=0)
+            matrix_scale = (256.0 / jnp.maximum(largest(peak), TINY)).astype(BF16)
+        for k in range(b, GROUP, seqs):
+            matrix8[k * out_width : (k + 1) * out_width] = (matrix_ref[k] * matrix_scale).astype(F8)
+    matrix = matrix_ref[...].reshape(GROUP * out_width, -1)
     back = (reach / 65536.0) / matrix_scale.astype(F32)
-    total[...] += dot(parts[...], matrix) + dot(parts8[...], matrix8) * back
+    total[...] += dot(parts[...], matrix) + dot(parts8[...], matrix8[...]) * back
 
     @pl.when(step == pl.num_programs(0) - 1)
     def _():
@@ -171,6 +173,7 @@
             pltpu.VMEM((tokens, GROUP * out_width), F8),
             pltpu.VMEM((tokens, in_width), F32),
             pltpu.VMEM((8, length), F32),
+            pltpu.VMEM((GROUP * out_width, in_width), F8),
         ],
     )(*pieces, rows, matrices)
 

time: 81.1 us -> 79.9 us (0.985)
  Pallas kernels: 58 us -> 56.7 us
    pallas_call x1, Pallas kernels: 29.4 us -> 28.2 us  [back_sums(): call(functools.partial(back_kernel, len(pieces)), (4 * count * out_width...]
  transfers between devices with their start and end apart: 8 -> 8, of which waited for: 1 -> 1; matrix products, arithmetic and copies ran while one was open for 3% -> 3% of each run, Pallas kernels for 72% -> 71%
where the time goes in v12:
time: 79.9 us; the launch traced here: 79.5 us
  Pallas kernels  56.7 us (71%)
  starting transfers between devices  14.3 us (18%)
  other arithmetic  3.36 us (4%)
  local copies, waits for them, and re-layouts  3.34 us (4%)
  waiting for transfers between devices  1.08 us (1%)
    pallas_call x1, Pallas kernels, back_sums(): call(functools.partial(back_kernel, len(pieces)), (4 * count * out_width...  28.2 us
    pallas_call x1, Pallas kernels, matrix_sums(): call(functools.partial(matrix_kernel, len(pieces), len(input_pieces), cou...  28.1 us
    ppermute x7, starting transfers between devices, exchange(): return lax.ppermute(array, axis, [(i, i ^ flip) for i in range(count)])  9.41 us
    all_to_all x1, starting transfers between devices, shards(): came = lax.all_to_all(blocks, 'cout', 0, 0, tiled=True)  4.89 us
    unnamed x4, local copies, waits for them, and re-layouts  2.55 us
  transfers between devices with their start and end apart: 8, of which 1 were waited for; matrix products, arithmetic and copies ran while one was open for 3% of the time, Pallas kernels for 71%

profile of v12, /device:TPU:0, one launch (start us, length us, event | category | flops | bytes accessed | tf_op | source)
XLA Modules:
  0.0 79.5 jit_solution(13794797207209965223)
XLA Ops:
  0.6 0.9 %copy.12 = bf16[16,8,4,128]{3,1,2,0:T(8,128)(2,1)S(1)} copy(bf16[16,8,4,128]{3,2,1,0:T(4,128)(2,1)} %bitcast.24) | data formatting | bytes 262144
  1.6 3.0 %collective-permute-start.3 = (bf16[128,512]{1,0:T(8,128)(2,1)S(1)}, bf16[128,512]{1,0:T(8,128)(2,1)S(1)}, u32[]{:S(2)}, u32[]{:S(2)}) collective-permute-start(bf16[128,512]{1,0:T(8,128)(2,1)S(1)} %bitcast.22), channel_id=1, source_target_pairs={{0,1},{1,0},{2,3},{3,2},{4,5},{5,4},{6,7},{7,6},{8,9},{9,8},{10,11... | collective-permute-start | bytes 393224 | tf_op jit(solution)/shard_map/ppermute | solution.py:276
  4.6 0.9 %copy.13 = bf16[16,8,4,128]{3,1,2,0:T(8,128)(2,1)S(1)} copy(bf16[16,8,4,128]{3,2,1,0:T(4,128)(2,1)} %bitcast.25) | data formatting | bytes 262144
  5.5 0.7 collective-permute-start.2
  6.2 0.9 %collective-permute-start.1 = (bf16[128,512]{1,0:T(8,128)(2,1)S(1)}, bf16[128,512]{1,0:T(8,128)(2,1)S(1)}, u32[]{:S(2)}, u32[]{:S(2)}) collective-permute-start(bf16[128,512]{1,0:T(8,128)(2,1)S(1)} %bitcast.17), channel_id=1, source_target_pairs={{0,16},{8,24},{16,0},{24,8},{1,17},{9,25},{17,1},{25,9},{2,18},{10... | collective-permute-start | bytes 393224 | tf_op jit(solution)/shard_map/ppermute | solution.py:276
  7.2 0.3 collective-permute-start
  7.4 0.7 copy-done
  8.2 0.5 shard_map.59.refs_8_.refs_4_
  8.6 0.0 collective-permute-done.3
  8.7 3.7 %collective-permute-start.6 = (bf16[2,128,512]{2,1,0:T(8,128)(2,1)S(1)}, bf16[2,128,512]{2,1,0:T(8,128)(2,1)S(1)}, u32[]{:S(2)}, u32[]{:S(2)}) collective-permute-start(bf16[2,128,512]{2,1,0:T(8,128)(2,1)S(1)} %bitcast.12), channel_id=1, source_target_pairs={{0,6},{1,7},{2,4},{3,5},{4,2},{5,3},{6,0},{7,1},{8,14},{9,15},{10,... | collective-permute-start | bytes 786440 | tf_op jit(solution)/shard_map/ppermute | solution.py:276
  12.3 0.0 collective-permute-start.5
  12.3 0.0 collective-permute-done.2.refs_3_
  12.3 0.8 collective-permute-start.4
  13.1 1.1 %collective-permute-done.1.refs_2_ = bf16[128,512]{1,0:T(8,128)(2,1)S(1)} collective-permute-done((bf16[128,512]{1,0:T(8,128)(2,1)S(1)}, bf16[128,512]{1,0:T(8,128)(2,1)S(1)}, u32[]{:S(2)}, u32[]{:S(2)}) %collective-permute-start.1) | collective-permute-done | bytes 131104 | tf_op jit(solution)/shard_map/ppermute | solution.py:276
  14.2 0.0 collective-permute-done.refs_1_
  14.2 28.2 %shard_map.61 = f32[8,520,128]{2,1,0:T(8,128)S(1)} custom-call(bf16[128,512]{1,0:T(8,128)(2,1)S(1)} %bitcast.19, bf16[128,512]{1,0:T(8,128)(2,1)S(1)} %collective-permute-done.refs_1_, bf16[128,512]{1,0:T(8,128)(2,1)S(1)} %collective-permute-done.1.refs_2_, bf16[128,512]{1,0:T(8,128)(2,1)S(1)} %collective-permute-done.2.refs_3_, ...), custom_call_target="tpu_custom_call" | custom-call | flops 25769803776 | bytes 25165824 | tf_op jit(solution)/shard_map/pallas_call | solution.py:161
  42.4 1.2 %convert_element_type.16 = f16[8,520,128]{2,1,0:T(8,128)(2,1)} convert(f32[8,520,128]{2,1,0:T(8,128)S(1)} %shard_map.61) | non-fusion elementwise | flops 532480 | bytes 3194880 | tf_op jit(solution)/shard_map/convert_element_type | solution.py:297
  43.6 4.9 %all-to-all-start = ((f16[8,520,128]{2,1,0:T(8,128)(2,1)}), f16[8,520,128]{2,1,0:T(8,128)(2,1)}, u32[]{:S(2)}, u32[]{:S(2)}) async-start(f16[8,520,128]{2,1,0:T(8,128)(2,1)} %convert_element_type.16), calls=%async_computation | async-start | bytes 2129920 | tf_op jit(solution)/shard_map/all_to_all | solution.py:298
  48.5 0.0 collective-permute-done.6.refs_7_
  48.5 0.0 collective-permute-done.4.refs_5_
  48.5 28.1 %shard_map.60 = bf16[24,512,1024]{2,1,0:T(8,128)(2,1)} custom-call(bf16[128,512]{1,0:T(8,128)(2,1)S(1)} %bitcast.20, bf16[128,512]{1,0:T(8,128)(2,1)S(1)} %collective-permute-done.refs_1_, bf16[128,512]{1,0:T(8,128)(2,1)S(1)} %collective-permute-done.1.refs_2_, bf16[128,512]{1,0:T(8,128)(2,1)S(1)} %collective-permute-done.2.refs_3_, ...), custom_call_target="tpu_custom_call" | custom-call | flops 19327352832 | bytes 25165824 | tf_op jit(solution)/shard_map/pallas_call | solution.py:256
  76.6 0.7 fusion.2
  77.3 1.4 %multiply_reduce_fusion = bf16[512,128]{1,0:T(8,128)(2,1)S(1)} fusion(f16[8,520,128]{2,1,0:T(8,128)(2,1)} %all-to-all-done, f32[8,128]{1,0:T(8,128)S(1)} %bitcast.27), kind=kLoop, calls=%fused_computation | loop fusion | flops 1507328 | bytes 1183744 | tf_op jit(solution)/shard_map/reduce_sum | solution.py:302
  78.7 0.8 copy.7
  (4 shorter events, 0.0 us)
Async XLA Ops:
  1.6 7.1 %collective-permute-start.3 = (bf16[128,512]{1,0:T(8,128)(2,1)S(1)}, bf16[128,512]{1,0:T(8,128)(2,1)S(1)}, u32[]{:S(2)}, u32[]{:S(2)}) collective-permute-start(bf16[128,512]{1,0:T(8,128)(2,1)S(1)} %bitcast.22), channel_id=1, source_target_pairs={{0,1},{1,0},{2,3},{3,2},{4,5},{5,4},{6,7},{7,6},{8,9},{9,8},{10,11... | collective-permute-start | bytes 393224 | tf_op jit(solution)/shard_map/ppermute | solution.py:276
  5.5 6.8 %collective-permute-start.2 = (bf16[128,512]{1,0:T(8,128)(2,1)S(1)}, bf16[128,512]{1,0:T(8,128)(2,1)S(1)}, u32[]{:S(2)}, u32[]{:S(2)}) collective-permute-start(bf16[128,512]{1,0:T(8,128)(2,1)S(1)} %bitcast.16), channel_id=1, source_target_pairs={{0,24},{8,16},{16,8},{24,0},{1,25},{9,17},{17,9},{25,1},{2,26},{10... | collective-permute-start | bytes 393224 | tf_op jit(solution)/shard_map/ppermute | solution.py:276
  6.2 8.0 %collective-permute-start.1 = (bf16[128,512]{1,0:T(8,128)(2,1)S(1)}, bf16[128,512]{1,0:T(8,128)(2,1)S(1)}, u32[]{:S(2)}, u32[]{:S(2)}) collective-permute-start(bf16[128,512]{1,0:T(8,128)(2,1)S(1)} %bitcast.17), channel_id=1, source_target_pairs={{0,16},{8,24},{16,0},{24,8},{1,17},{9,25},{17,1},{25,9},{2,18},{10... | collective-permute-start | bytes 393224 | tf_op jit(solution)/shard_map/ppermute | solution.py:276
  7.2 7.0 %collective-permute-start = (bf16[128,512]{1,0:T(8,128)(2,1)S(1)}, bf16[128,512]{1,0:T(8,128)(2,1)S(1)}, u32[]{:S(2)}, u32[]{:S(2)}) collective-permute-start(bf16[128,512]{1,0:T(8,128)(2,1)S(1)} %bitcast.18), channel_id=1, source_target_pairs={{0,8},{8,0},{16,24},{24,16},{1,9},{9,1},{17,25},{25,17},{2,10},{10... | collective-permute-start | bytes 393224 | tf_op jit(solution)/shard_map/ppermute | solution.py:276
  7.4 0.7 copy-start
  8.7 39.8 %collective-permute-start.6 = (bf16[2,128,512]{2,1,0:T(8,128)(2,1)S(1)}, bf16[2,128,512]{2,1,0:T(8,128)(2,1)S(1)}, u32[]{:S(2)}, u32[]{:S(2)}) collective-permute-start(bf16[2,128,512]{2,1,0:T(8,128)(2,1)S(1)} %bitcast.12), channel_id=1, source_target_pairs={{0,6},{1,7},{2,4},{3,5},{4,2},{5,3},{6,0},{7,1},{8,14},{9,15},{10,... | collective-permute-start | bytes 786440 | tf_op jit(solution)/shard_map/ppermute | solution.py:276
  12.3 36.1 %collective-permute-start.5 = (bf16[2,128,512]{2,1,0:T(8,128)(2,1)S(1)}, bf16[2,128,512]{2,1,0:T(8,128)(2,1)S(1)}, u32[]{:S(2)}, u32[]{:S(2)}) collective-permute-start(bf16[2,128,512]{2,1,0:T(8,128)(2,1)S(1)} %bitcast.13), channel_id=1, source_target_pairs={{0,4},{1,5},{2,6},{3,7},{4,0},{5,1},{6,2},{7,3},{8,12},{9,13},{10,... | collective-permute-start | bytes 786440 | tf_op jit(solution)/shard_map/ppermute | solution.py:276
  12.3 36.1 %collective-permute-start.4 = (bf16[2,128,512]{2,1,0:T(8,128)(2,1)S(1)}, bf16[2,128,512]{2,1,0:T(8,128)(2,1)S(1)}, u32[]{:S(2)}, u32[]{:S(2)}) collective-permute-start(bf16[2,128,512]{2,1,0:T(8,128)(2,1)S(1)} %bitcast.14), channel_id=1, source_target_pairs={{0,2},{1,3},{2,0},{3,1},{4,6},{5,7},{6,4},{7,5},{8,10},{9,11},{10,... | collective-permute-start | bytes 786440 | tf_op jit(solution)/shard_map/ppermute | solution.py:276
  43.6 33.0 %all-to-all-start = ((f16[8,520,128]{2,1,0:T(8,128)(2,1)}), f16[8,520,128]{2,1,0:T(8,128)(2,1)}, u32[]{:S(2)}, u32[]{:S(2)}) async-start(f16[8,520,128]{2,1,0:T(8,128)(2,1)} %convert_element_type.16), calls=%async_computation | async-start | bytes 2129920 | tf_op jit(solution)/shard_map/all_to_all | solution.py:298

commit v13 on v12

--- a/solution.py
+++ b/solution.py
@@ -126,11 +126,14 @@
         if b == 0:
             peak = jnp.max(jnp.abs(matrix_ref[...]).reshape(-1, 16, matrix_ref.shape[2]), axis=0)
             matrix_scale = (256.0 / jnp.maximum(largest(peak), TINY)).astype(BF16)
-        for k in range(b, GROUP, seqs):
+    back = (reach / 65536.0) / matrix_scale.astype(F32)
+    products = []
+    for first in range(0, GROUP, 2):
+        columns = slice(first * out_width, (first + 2) * out_width)
+        products.append(dot(parts[:, columns], matrix_ref[first : first + 2].reshape(2 * out_width, -1)))
+        for k in range(first, first + 2):
             matrix8[k * out_width : (k + 1) * out_width] = (matrix_ref[k] * matrix_scale).astype(F8)
-    matrix = matrix_ref[...].reshape(GROUP * out_width, -1)
-    back = (reach / 65536.0) / matrix_scale.astype(F32)
-    total[...] += dot(parts[...], matrix) + dot(parts8[...], matrix8[...]) * back
+    total[...] += functools.reduce(jnp.add, products) + dot(parts8[...], matrix8[...]) * back
 
     @pl.when(step == pl.num_programs(0) - 1)
     def _():

time: 79.9 us -> 79.9 us (level)
  no operation moved by 1% of the time
where the time goes in v13:
time: 79.9 us; the launch traced here: 79.5 us
  Pallas kernels  56.7 us (71%)
  starting transfers between devices  14.3 us (18%)
  other arithmetic  3.36 us (4%)
  local copies, waits for them, and re-layouts  3.34 us (4%)
  waiting for transfers between devices  1.08 us (1%)
    pallas_call x1, Pallas kernels, back_sums(): call(functools.partial(back_kernel, len(pieces)), (4 * count * out_width...  28.2 us
    pallas_call x1, Pallas kernels, matrix_sums(): call(functools.partial(matrix_kernel, len(pieces), len(input_pieces), cou...  28.1 us
    ppermute x7, starting transfers between devices, exchange(): return lax.ppermute(array, axis, [(i, i ^ flip) for i in range(count)])  9.41 us
    all_to_all x1, starting transfers between devices, shards(): came = lax.all_to_all(blocks, 'cout', 0, 0, tiled=True)  4.88 us
    unnamed x4, local copies, waits for them, and re-layouts  2.55 us
  transfers between devices with their start and end apart: 8, of which 1 were waited for; matrix products, arithmetic and copies ran while one was open for 3% of the time, Pallas kernels for 71%

profile of v13, /device:TPU:0, one launch (start us, length us, event | category | flops | bytes accessed | tf_op | source)
XLA Modules:
  0.0 79.5 jit_solution(12471926737942693693)
XLA Ops:
  0.6 0.9 %copy.12 = bf16[16,8,4,128]{3,1,2,0:T(8,128)(2,1)S(1)} copy(bf16[16,8,4,128]{3,2,1,0:T(4,128)(2,1)} %bitcast.24) | data formatting | bytes 262144
  1.6 3.0 %collective-permute-start.3 = (bf16[128,512]{1,0:T(8,128)(2,1)S(1)}, bf16[128,512]{1,0:T(8,128)(2,1)S(1)}, u32[]{:S(2)}, u32[]{:S(2)}) collective-permute-start(bf16[128,512]{1,0:T(8,128)(2,1)S(1)} %bitcast.22), channel_id=1, source_target_pairs={{0,1},{1,0},{2,3},{3,2},{4,5},{5,4},{6,7},{7,6},{8,9},{9,8},{10,11... | collective-permute-start | bytes 393224 | tf_op jit(solution)/shard_map/ppermute | solution.py:279
  4.6 0.9 %copy.13 = bf16[16,8,4,128]{3,1,2,0:T(8,128)(2,1)S(1)} copy(bf16[16,8,4,128]{3,2,1,0:T(4,128)(2,1)} %bitcast.25) | data formatting | bytes 262144
  5.5 0.7 collective-permute-start.2
  6.2 0.9 %collective-permute-start.1 = (bf16[128,512]{1,0:T(8,128)(2,1)S(1)}, bf16[128,512]{1,0:T(8,128)(2,1)S(1)}, u32[]{:S(2)}, u32[]{:S(2)}) collective-permute-start(bf16[128,512]{1,0:T(8,128)(2,1)S(1)} %bitcast.17), channel_id=1, source_target_pairs={{0,16},{8,24},{16,0},{24,8},{1,17},{9,25},{17,1},{25,9},{2,18},{10... | collective-permute-start | bytes 393224 | tf_op jit(solution)/shard_map/ppermute | solution.py:279
  7.2 0.3 collective-permute-start
  7.4 0.7 copy-done
  8.2 0.5 shard_map.59.refs_8_.refs_4_
  8.6 0.0 collective-permute-done.3
  8.7 3.7 %collective-permute-start.6 = (bf16[2,128,512]{2,1,0:T(8,128)(2,1)S(1)}, bf16[2,128,512]{2,1,0:T(8,128)(2,1)S(1)}, u32[]{:S(2)}, u32[]{:S(2)}) collective-permute-start(bf16[2,128,512]{2,1,0:T(8,128)(2,1)S(1)} %bitcast.12), channel_id=1, source_target_pairs={{0,6},{1,7},{2,4},{3,5},{4,2},{5,3},{6,0},{7,1},{8,14},{9,15},{10,... | collective-permute-start | bytes 786440 | tf_op jit(solution)/shard_map/ppermute | solution.py:279
  12.3 0.0 collective-permute-start.5
  12.3 0.0 collective-permute-done.2.refs_3_
  12.3 0.8 collective-permute-start.4
  13.1 1.1 %collective-permute-done.1.refs_2_ = bf16[128,512]{1,0:T(8,128)(2,1)S(1)} collective-permute-done((bf16[128,512]{1,0:T(8,128)(2,1)S(1)}, bf16[128,512]{1,0:T(8,128)(2,1)S(1)}, u32[]{:S(2)}, u32[]{:S(2)}) %collective-permute-start.1) | collective-permute-done | bytes 131104 | tf_op jit(solution)/shard_map/ppermute | solution.py:279
  14.2 0.0 collective-permute-done.refs_1_
  14.2 28.2 %shard_map.61 = f32[8,520,128]{2,1,0:T(8,128)S(1)} custom-call(bf16[128,512]{1,0:T(8,128)(2,1)S(1)} %bitcast.19, bf16[128,512]{1,0:T(8,128)(2,1)S(1)} %collective-permute-done.refs_1_, bf16[128,512]{1,0:T(8,128)(2,1)S(1)} %collective-permute-done.1.refs_2_, bf16[128,512]{1,0:T(8,128)(2,1)S(1)} %collective-permute-done.2.refs_3_, ...), custom_call_target="tpu_custom_call" | custom-call | flops 25769803776 | bytes 25165824 | tf_op jit(solution)/shard_map/pallas_call | solution.py:164
  42.4 1.2 %convert_element_type.16 = f16[8,520,128]{2,1,0:T(8,128)(2,1)} convert(f32[8,520,128]{2,1,0:T(8,128)S(1)} %shard_map.61) | non-fusion elementwise | flops 532480 | bytes 3194880 | tf_op jit(solution)/shard_map/convert_element_type | solution.py:300
  43.6 4.9 %all-to-all-start = ((f16[8,520,128]{2,1,0:T(8,128)(2,1)}), f16[8,520,128]{2,1,0:T(8,128)(2,1)}, u32[]{:S(2)}, u32[]{:S(2)}) async-start(f16[8,520,128]{2,1,0:T(8,128)(2,1)} %convert_element_type.16), calls=%async_computation | async-start | bytes 2129920 | tf_op jit(solution)/shard_map/all_to_all | solution.py:301
  48.4 0.0 collective-permute-done.6.refs_7_
  48.4 0.0 collective-permute-done.5.refs_6_
  48.5 28.1 %shard_map.60 = bf16[24,512,1024]{2,1,0:T(8,128)(2,1)} custom-call(bf16[128,512]{1,0:T(8,128)(2,1)S(1)} %bitcast.20, bf16[128,512]{1,0:T(8,128)(2,1)S(1)} %collective-permute-done.refs_1_, bf16[128,512]{1,0:T(8,128)(2,1)S(1)} %collective-permute-done.1.refs_2_, bf16[128,512]{1,0:T(8,128)(2,1)S(1)} %collective-permute-done.2.refs_3_, ...), custom_call_target="tpu_custom_call" | custom-call | flops 19327352832 | bytes 25165824 | tf_op jit(solution)/shard_map/pallas_call | solution.py:259
  76.5 0.7 fusion.2
  77.3 1.4 %multiply_reduce_fusion = bf16[512,128]{1,0:T(8,128)(2,1)S(1)} fusion(f16[8,520,128]{2,1,0:T(8,128)(2,1)} %all-to-all-done, f32[8,128]{1,0:T(8,128)S(1)} %bitcast.27), kind=kLoop, calls=%fused_computation | loop fusion | flops 1507328 | bytes 1183744 | tf_op jit(solution)/shard_map/reduce_sum | solution.py:305
  78.7 0.8 copy.7
  (4 shorter events, 0.0 us)
Async XLA Ops:
  1.6 7.1 %collective-permute-start.3 = (bf16[128,512]{1,0:T(8,128)(2,1)S(1)}, bf16[128,512]{1,0:T(8,128)(2,1)S(1)}, u32[]{:S(2)}, u32[]{:S(2)}) collective-permute-start(bf16[128,512]{1,0:T(8,128)(2,1)S(1)} %bitcast.22), channel_id=1, source_target_pairs={{0,1},{1,0},{2,3},{3,2},{4,5},{5,4},{6,7},{7,6},{8,9},{9,8},{10,11... | collective-permute-start | bytes 393224 | tf_op jit(solution)/shard_map/ppermute | solution.py:279
  5.5 6.8 %collective-permute-start.2 = (bf16[128,512]{1,0:T(8,128)(2,1)S(1)}, bf16[128,512]{1,0:T(8,128)(2,1)S(1)}, u32[]{:S(2)}, u32[]{:S(2)}) collective-permute-start(bf16[128,512]{1,0:T(8,128)(2,1)S(1)} %bitcast.16), channel_id=1, source_target_pairs={{0,24},{8,16},{16,8},{24,0},{1,25},{9,17},{17,9},{25,1},{2,26},{10... | collective-permute-start | bytes 393224 | tf_op jit(solution)/shard_map/ppermute | solution.py:279
  6.2 8.0 %collective-permute-start.1 = (bf16[128,512]{1,0:T(8,128)(2,1)S(1)}, bf16[128,512]{1,0:T(8,128)(2,1)S(1)}, u32[]{:S(2)}, u32[]{:S(2)}) collective-permute-start(bf16[128,512]{1,0:T(8,128)(2,1)S(1)} %bitcast.17), channel_id=1, source_target_pairs={{0,16},{8,24},{16,0},{24,8},{1,17},{9,25},{17,1},{25,9},{2,18},{10... | collective-permute-start | bytes 393224 | tf_op jit(solution)/shard_map/ppermute | solution.py:279
  7.2 7.0 %collective-permute-start = (bf16[128,512]{1,0:T(8,128)(2,1)S(1)}, bf16[128,512]{1,0:T(8,128)(2,1)S(1)}, u32[]{:S(2)}, u32[]{:S(2)}) collective-permute-start(bf16[128,512]{1,0:T(8,128)(2,1)S(1)} %bitcast.18), channel_id=1, source_target_pairs={{0,8},{8,0},{16,24},{24,16},{1,9},{9,1},{17,25},{25,17},{2,10},{10... | collective-permute-start | bytes 393224 | tf_op jit(solution)/shard_map/ppermute | solution.py:279
  7.4 0.7 copy-start
  8.7 39.8 %collective-permute-start.6 = (bf16[2,128,512]{2,1,0:T(8,128)(2,1)S(1)}, bf16[2,128,512]{2,1,0:T(8,128)(2,1)S(1)}, u32[]{:S(2)}, u32[]{:S(2)}) collective-permute-start(bf16[2,128,512]{2,1,0:T(8,128)(2,1)S(1)} %bitcast.12), channel_id=1, source_target_pairs={{0,6},{1,7},{2,4},{3,5},{4,2},{5,3},{6,0},{7,1},{8,14},{9,15},{10,... | collective-permute-start | bytes 786440 | tf_op jit(solution)/shard_map/ppermute | solution.py:279
  12.3 36.1 %collective-permute-start.5 = (bf16[2,128,512]{2,1,0:T(8,128)(2,1)S(1)}, bf16[2,128,512]{2,1,0:T(8,128)(2,1)S(1)}, u32[]{:S(2)}, u32[]{:S(2)}) collective-permute-start(bf16[2,128,512]{2,1,0:T(8,128)(2,1)S(1)} %bitcast.13), channel_id=1, source_target_pairs={{0,4},{1,5},{2,6},{3,7},{4,0},{5,1},{6,2},{7,3},{8,12},{9,13},{10,... | collective-permute-start | bytes 786440 | tf_op jit(solution)/shard_map/ppermute | solution.py:279
  12.3 36.1 %collective-permute-start.4 = (bf16[2,128,512]{2,1,0:T(8,128)(2,1)S(1)}, bf16[2,128,512]{2,1,0:T(8,128)(2,1)S(1)}, u32[]{:S(2)}, u32[]{:S(2)}) collective-permute-start(bf16[2,128,512]{2,1,0:T(8,128)(2,1)S(1)} %bitcast.14), channel_id=1, source_target_pairs={{0,2},{1,3},{2,0},{3,1},{4,6},{5,7},{6,4},{7,5},{8,10},{9,11},{10,... | collective-permute-start | bytes 786440 | tf_op jit(solution)/shard_map/ppermute | solution.py:279
  43.6 33.0 %all-to-all-start = ((f16[8,520,128]{2,1,0:T(8,128)(2,1)}), f16[8,520,128]{2,1,0:T(8,128)(2,1)}, u32[]{:S(2)}, u32[]{:S(2)}) async-start(f16[8,520,128]{2,1,0:T(8,128)(2,1)} %convert_element_type.16), calls=%async_computation | async-start | bytes 2129920 | tf_op jit(solution)/shard_map/all_to_all | solution.py:301

commit v14 on v13

--- a/solution.py
+++ b/solution.py
@@ -14,7 +14,7 @@
 F8 = jnp.float8_e4m3fn
 MIB = 1024 * 1024
 GROUP = 4
-CHUNK = 256
+CHUNK = 512
 TINY = 1e-30
 
 

time: 79.9 us -> 80.1 us (level)
  no operation moved by 1% of the time
where the time goes in v14:
time: 80.1 us; the launch traced here: 79.7 us
  Pallas kernels  57 us (71%)
  starting transfers between devices  14.3 us (18%)
  other arithmetic  3.36 us (4%)
  local copies, waits for them, and re-layouts  3.34 us (4%)
  waiting for transfers between devices  1.08 us (1%)
    pallas_call x1, Pallas kernels, matrix_sums(): call(functools.partial(matrix_kernel, len(pieces), len(input_pieces), cou...  28.3 us
    pallas_call x1, Pallas kernels, back_sums(): call(functools.partial(back_kernel, len(pieces)), (4 * count * out_width...  28.2 us
    ppermute x7, starting transfers between devices, exchange(): return lax.ppermute(array, axis, [(i, i ^ flip) for i in range(count)])  9.41 us
    all_to_all x1, starting transfers between devices, shards(): came = lax.all_to_all(blocks, 'cout', 0, 0, tiled=True)  4.88 us
    unnamed x4, local copies, waits for them, and re-layouts  2.55 us
  transfers between devices with their start and end apart: 8, of which 1 were waited for; matrix products, arithmetic and copies ran while one was open for 3% of the time, Pallas kernels for 71%

profile of v14, /device:TPU:0, one launch (start us, length us, event | category | flops | bytes accessed | tf_op | source)
XLA Modules:
  0.0 79.7 jit_solution(10697294532748721802)
XLA Ops:
  0.6 0.9 %copy.12 = bf16[16,8,4,128]{3,1,2,0:T(8,128)(2,1)S(1)} copy(bf16[16,8,4,128]{3,2,1,0:T(4,128)(2,1)} %bitcast.24) | data formatting | bytes 262144
  1.6 3.0 %collective-permute-start.3 = (bf16[128,512]{1,0:T(8,128)(2,1)S(1)}, bf16[128,512]{1,0:T(8,128)(2,1)S(1)}, u32[]{:S(2)}, u32[]{:S(2)}) collective-permute-start(bf16[128,512]{1,0:T(8,128)(2,1)S(1)} %bitcast.22), channel_id=1, source_target_pairs={{0,1},{1,0},{2,3},{3,2},{4,5},{5,4},{6,7},{7,6},{8,9},{9,8},{10,11... | collective-permute-start | bytes 393224 | tf_op jit(solution)/shard_map/ppermute | solution.py:279
  4.6 0.9 %copy.13 = bf16[16,8,4,128]{3,1,2,0:T(8,128)(2,1)S(1)} copy(bf16[16,8,4,128]{3,2,1,0:T(4,128)(2,1)} %bitcast.25) | data formatting | bytes 262144
  5.5 0.7 collective-permute-start.2
  6.2 0.9 %collective-permute-start.1 = (bf16[128,512]{1,0:T(8,128)(2,1)S(1)}, bf16[128,512]{1,0:T(8,128)(2,1)S(1)}, u32[]{:S(2)}, u32[]{:S(2)}) collective-permute-start(bf16[128,512]{1,0:T(8,128)(2,1)S(1)} %bitcast.17), channel_id=1, source_target_pairs={{0,16},{8,24},{16,0},{24,8},{1,17},{9,25},{17,1},{25,9},{2,18},{10... | collective-permute-start | bytes 393224 | tf_op jit(solution)/shard_map/ppermute | solution.py:279
  7.2 0.3 collective-permute-start
  7.4 0.7 copy-done
  8.2 0.5 shard_map.59.refs_8_.refs_4_
  8.6 0.0 collective-permute-done.3
  8.7 3.7 %collective-permute-start.6 = (bf16[2,128,512]{2,1,0:T(8,128)(2,1)S(1)}, bf16[2,128,512]{2,1,0:T(8,128)(2,1)S(1)}, u32[]{:S(2)}, u32[]{:S(2)}) collective-permute-start(bf16[2,128,512]{2,1,0:T(8,128)(2,1)S(1)} %bitcast.12), channel_id=1, source_target_pairs={{0,6},{1,7},{2,4},{3,5},{4,2},{5,3},{6,0},{7,1},{8,14},{9,15},{10,... | collective-permute-start | bytes 786440 | tf_op jit(solution)/shard_map/ppermute | solution.py:279
  12.3 0.0 collective-permute-start.5
  12.3 0.0 collective-permute-done.2.refs_3_
  12.3 0.8 collective-permute-start.4
  13.1 1.1 %collective-permute-done.1.refs_2_ = bf16[128,512]{1,0:T(8,128)(2,1)S(1)} collective-permute-done((bf16[128,512]{1,0:T(8,128)(2,1)S(1)}, bf16[128,512]{1,0:T(8,128)(2,1)S(1)}, u32[]{:S(2)}, u32[]{:S(2)}) %collective-permute-start.1) | collective-permute-done | bytes 131104 | tf_op jit(solution)/shard_map/ppermute | solution.py:279
  14.2 0.0 collective-permute-done.refs_1_
  14.2 28.2 %shard_map.61 = f32[8,520,128]{2,1,0:T(8,128)S(1)} custom-call(bf16[128,512]{1,0:T(8,128)(2,1)S(1)} %bitcast.19, bf16[128,512]{1,0:T(8,128)(2,1)S(1)} %collective-permute-done.refs_1_, bf16[128,512]{1,0:T(8,128)(2,1)S(1)} %collective-permute-done.1.refs_2_, bf16[128,512]{1,0:T(8,128)(2,1)S(1)} %collective-permute-done.2.refs_3_, ...), custom_call_target="tpu_custom_call" | custom-call | flops 25769803776 | bytes 25165824 | tf_op jit(solution)/shard_map/pallas_call | solution.py:164
  42.4 1.2 %convert_element_type.16 = f16[8,520,128]{2,1,0:T(8,128)(2,1)} convert(f32[8,520,128]{2,1,0:T(8,128)S(1)} %shard_map.61) | non-fusion elementwise | flops 532480 | bytes 3194880 | tf_op jit(solution)/shard_map/convert_element_type | solution.py:300
  43.6 4.9 %all-to-all-start = ((f16[8,520,128]{2,1,0:T(8,128)(2,1)}), f16[8,520,128]{2,1,0:T(8,128)(2,1)}, u32[]{:S(2)}, u32[]{:S(2)}) async-start(f16[8,520,128]{2,1,0:T(8,128)(2,1)} %convert_element_type.16), calls=%async_computation | async-start | bytes 2129920 | tf_op jit(solution)/shard_map/all_to_all | solution.py:301
  48.4 0.0 collective-permute-done.6.refs_7_
  48.5 0.0 collective-permute-done.4.refs_5_
  48.5 28.3 %shard_map.60 = bf16[24,512,1024]{2,1,0:T(8,128)(2,1)} custom-call(bf16[128,512]{1,0:T(8,128)(2,1)S(1)} %bitcast.20, bf16[128,512]{1,0:T(8,128)(2,1)S(1)} %collective-permute-done.refs_1_, bf16[128,512]{1,0:T(8,128)(2,1)S(1)} %collective-permute-done.1.refs_2_, bf16[128,512]{1,0:T(8,128)(2,1)S(1)} %collective-permute-done.2.refs_3_, ...), custom_call_target="tpu_custom_call" | custom-call | flops 19327352832 | bytes 25165824 | tf_op jit(solution)/shard_map/pallas_call | solution.py:259
  76.8 0.7 fusion.2
  77.5 1.4 %multiply_reduce_fusion = bf16[512,128]{1,0:T(8,128)(2,1)S(1)} fusion(f16[8,520,128]{2,1,0:T(8,128)(2,1)} %all-to-all-done, f32[8,128]{1,0:T(8,128)S(1)} %bitcast.27), kind=kLoop, calls=%fused_computation | loop fusion | flops 1507328 | bytes 1183744 | tf_op jit(solution)/shard_map/reduce_sum | solution.py:305
  78.9 0.8 copy.7
  (4 shorter events, 0.0 us)
Async XLA Ops:
  1.6 7.1 %collective-permute-start.3 = (bf16[128,512]{1,0:T(8,128)(2,1)S(1)}, bf16[128,512]{1,0:T(8,128)(2,1)S(1)}, u32[]{:S(2)}, u32[]{:S(2)}) collective-permute-start(bf16[128,512]{1,0:T(8,128)(2,1)S(1)} %bitcast.22), channel_id=1, source_target_pairs={{0,1},{1,0},{2,3},{3,2},{4,5},{5,4},{6,7},{7,6},{8,9},{9,8},{10,11... | collective-permute-start | bytes 393224 | tf_op jit(solution)/shard_map/ppermute | solution.py:279
  5.5 6.8 %collective-permute-start.2 = (bf16[128,512]{1,0:T(8,128)(2,1)S(1)}, bf16[128,512]{1,0:T(8,128)(2,1)S(1)}, u32[]{:S(2)}, u32[]{:S(2)}) collective-permute-start(bf16[128,512]{1,0:T(8,128)(2,1)S(1)} %bitcast.16), channel_id=1, source_target_pairs={{0,24},{8,16},{16,8},{24,0},{1,25},{9,17},{17,9},{25,1},{2,26},{10... | collective-permute-start | bytes 393224 | tf_op jit(solution)/shard_map/ppermute | solution.py:279
  6.2 8.0 %collective-permute-start.1 = (bf16[128,512]{1,0:T(8,128)(2,1)S(1)}, bf16[128,512]{1,0:T(8,128)(2,1)S(1)}, u32[]{:S(2)}, u32[]{:S(2)}) collective-permute-start(bf16[128,512]{1,0:T(8,128)(2,1)S(1)} %bitcast.17), channel_id=1, source_target_pairs={{0,16},{8,24},{16,0},{24,8},{1,17},{9,25},{17,1},{25,9},{2,18},{10... | collective-permute-start | bytes 393224 | tf_op jit(solution)/shard_map/ppermute | solution.py:279
  7.2 7.0 %collective-permute-start = (bf16[128,512]{1,0:T(8,128)(2,1)S(1)}, bf16[128,512]{1,0:T(8,128)(2,1)S(1)}, u32[]{:S(2)}, u32[]{:S(2)}) collective-permute-start(bf16[128,512]{1,0:T(8,128)(2,1)S(1)} %bitcast.18), channel_id=1, source_target_pairs={{0,8},{8,0},{16,24},{24,16},{1,9},{9,1},{17,25},{25,17},{2,10},{10... | collective-permute-start | bytes 393224 | tf_op jit(solution)/shard_map/ppermute | solution.py:279
  7.4 0.7 copy-start
  8.7 39.8 %collective-permute-start.6 = (bf16[2,128,512]{2,1,0:T(8,128)(2,1)S(1)}, bf16[2,128,512]{2,1,0:T(8,128)(2,1)S(1)}, u32[]{:S(2)}, u32[]{:S(2)}) collective-permute-start(bf16[2,128,512]{2,1,0:T(8,128)(2,1)S(1)} %bitcast.12), channel_id=1, source_target_pairs={{0,6},{1,7},{2,4},{3,5},{4,2},{5,3},{6,0},{7,1},{8,14},{9,15},{10,... | collective-permute-start | bytes 786440 | tf_op jit(solution)/shard_map/ppermute | solution.py:279
  12.3 36.1 %collective-permute-start.5 = (bf16[2,128,512]{2,1,0:T(8,128)(2,1)S(1)}, bf16[2,128,512]{2,1,0:T(8,128)(2,1)S(1)}, u32[]{:S(2)}, u32[]{:S(2)}) collective-permute-start(bf16[2,128,512]{2,1,0:T(8,128)(2,1)S(1)} %bitcast.13), channel_id=1, source_target_pairs={{0,4},{1,5},{2,6},{3,7},{4,0},{5,1},{6,2},{7,3},{8,12},{9,13},{10,... | collective-permute-start | bytes 786440 | tf_op jit(solution)/shard_map/ppermute | solution.py:279
  12.3 36.1 %collective-permute-start.4 = (bf16[2,128,512]{2,1,0:T(8,128)(2,1)S(1)}, bf16[2,128,512]{2,1,0:T(8,128)(2,1)S(1)}, u32[]{:S(2)}, u32[]{:S(2)}) collective-permute-start(bf16[2,128,512]{2,1,0:T(8,128)(2,1)S(1)} %bitcast.14), channel_id=1, source_target_pairs={{0,2},{1,3},{2,0},{3,1},{4,6},{5,7},{6,4},{7,5},{8,10},{9,11},{10,... | collective-permute-start | bytes 786440 | tf_op jit(solution)/shard_map/ppermute | solution.py:279
  43.6 33.2 %all-to-all-start = ((f16[8,520,128]{2,1,0:T(8,128)(2,1)}), f16[8,520,128]{2,1,0:T(8,128)(2,1)}, u32[]{:S(2)}, u32[]{:S(2)}) async-start(f16[8,520,128]{2,1,0:T(8,128)(2,1)} %convert_element_type.16), calls=%async_computation | async-start | bytes 2129920 | tf_op jit(solution)/shard_map/all_to_all | solution.py:301
